TPU v7x, 128 devices: a whole 4x4x4 slice. The times are simulated.
128 devices in a mesh: ctx: 32 (over y, x, core), chan: 4 (over z).
Axes of the slice: x: 4, y: 4, z: 4, core: 2. Of those that a mesh axis runs over, the one named last changes fastest.
Arguments:
- hyena_q: bfloat16 [4096, 8192], P('ctx', 'chan'), may hold values from -20 to 20
- hyena_k: bfloat16 [4096, 8192], P('ctx', 'chan'), may hold values from -6 to 6
- hyena_v: bfloat16 [4096, 8192], P('ctx', 'chan'), may hold values from -6 to 6
- hyena_grad: bfloat16 [4096, 8192], P('ctx', 'chan'), may hold values from -6 to 6
- pole_rate: float32 [16, 8192], P(None, 'chan'), may hold values from 0.00024414062 to 0.033333335
- residue: float32 [16, 8192], P(None, 'chan'), may hold values from -1.5 to 1.5
- norm_gain: float32 [8192], P('chan'), may hold values from 0.25 to 1.75
- doc_ids: int32 [4096], P('ctx'), may hold values from 0 to 3, never falling along the last dimension, each value on 1 to 2048 neighbouring positions
- attn_q: bfloat16 [4096, 4096], P('ctx', 'chan'), may hold values from -5 to 5
- attn_k: bfloat16 [4096, 4096], P('ctx', 'chan'), may hold values from -5 to 5
- attn_v: bfloat16 [4096, 4096], P('ctx', 'chan'), may hold values from -6 to 6
- attn_grad: bfloat16 [4096, 4096], P('ctx', 'chan'), may hold values from -6 to 6
Outputs:
- grad_hq: bfloat16 [4096, 8192], P('ctx', 'chan')
- grad_hk: bfloat16 [4096, 8192], P('ctx', 'chan')
- grad_hv: bfloat16 [4096, 8192], P('ctx', 'chan')
- grad_residue: float32 [16, 8192], P(None, 'chan')
- grad_gain: float32 [8192], P('chan')
- grad_aq: bfloat16 [4096, 4096], P('ctx', 'chan')
- grad_ak: bfloat16 [4096, 4096], P('ctx', 'chan')
- grad_av: bfloat16 [4096, 4096], P('ctx', 'chan')
Inputs may be any that keep to these rules, and one draw needn't show every extreme that they name: doc_ids never falls along the tokens; each of the 4 documents is one contiguous run of tokens, and the longest run holds exactly half of the 4096 tokens.
All inputs are finite; a program needn't handle non-finite values.
Results may differ from a plain program's by a relative error of at most 0.015.
Values may be sent and summed in bfloat16 or wider, within the bound.
No kernel may reach another device: no remote copies, remote signals or barrier semaphores. Data moves between devices by JAX's collectives and lax.ppermute only.
A program may use at most 128 MiB of HBM per device.

v0:
```python
import math

import jax
import jax.numpy as jnp
from jax import lax
from jax.sharding import PartitionSpec as P

D = 8192
HEAD_DIM = 128


EPSILON = 1e-06
FLOOR_SCORE = -1e30
SPLIT_PASSES = lax.Precision.HIGHEST


def from_behind(value, axis, steps):
    count = lax.axis_size(axis)
    first, last = (max(0, -steps), min(count, count - steps))
    return lax.ppermute(value, axis, [(source, source + steps) for source in range(first, last)])


def pass_states(entry, exit_doc, gain, state, backward):
    step_by = -1 if backward else 1

    def pass_advance(turn, carry):
        outgoing, got_state, got_exit = carry
        got_state, got_exit = from_behind((outgoing, exit_doc), "ctx", step_by)
        outgoing = state + (got_exit == entry).astype(jnp.float32) * gain * got_state
        return (outgoing, got_state, got_exit)

    start = (state, jnp.zeros_like(state), exit_doc)
    _, got_state, got_exit = lax.fori_loop(0, lax.axis_size("ctx") - 1, pass_advance, start)
    result = jnp.where(got_exit == entry, got_state, 0.0)
    return result


def local_sweep(source, docs, rate, weight, feed):
    length, width = source.shape
    span = math.gcd(length, 32)
    count = length // span
    within = jnp.arange(span, dtype=jnp.float32)
    rise = jnp.exp(rate[None] * within[:, None, None])
    fall = jnp.exp(-rate[None] * within[:, None, None])
    step_in = jnp.exp(-rate[None] * (within[:, None, None] + 1.0))
    order = within[None, :] <= within[:, None]

    def local_advance(carry, block):
        entry, entry_doc, totals = carry
        part, doc_part, feed_part = block
        lower = (order & (doc_part[None, :] == doc_part[:, None])).astype(jnp.float32)
        inner = jnp.einsum("ts,spc->tpc", lower, rise * part[:, None, :], precision=SPLIT_PASSES)
        joins = (doc_part == entry_doc).astype(jnp.float32)[:, None, None]
        states = fall * inner + step_in * joins * entry[None]
        totals = totals + jnp.sum(states * feed_part[:, None, :], axis=0)
        return ((states[-1], doc_part[-1], totals), jnp.sum(states * weight[None], axis=1))

    blocks = (
        source.reshape(count, span, width),
        docs.reshape(count, span),
        feed.reshape(count, span, width),
    )
    start = (jnp.zeros_like(rate), docs[0], jnp.zeros_like(rate))
    (last, _, totals), rows = lax.scan(local_advance, start, blocks)
    return (rows.reshape(length, width), last, totals)


def carry_terms(carry, docs, rate, weight, feed):
    length, width = feed.shape
    span = math.gcd(length, 32)
    count = length // span
    within = jnp.arange(span, dtype=jnp.float32)

    def one(block):
        offset, doc_part, feed_part = block
        fading = jnp.exp(-rate[None] * (offset + within + 1.0)[:, None, None])
        joins = (doc_part == docs[0]).astype(jnp.float32)[:, None, None]
        spread = fading * joins * carry[None]
        return (
            jnp.sum(spread * weight[None], axis=1),
            jnp.sum(spread * feed_part[:, None, :], axis=0),
        )

    offsets = (jnp.arange(count) * span).astype(jnp.float32)
    rows, parts = lax.map(
        one, (offsets, docs.reshape(count, span), feed.reshape(count, span, width))
    )
    return (rows.reshape(length, width), jnp.sum(parts, axis=0))


def body(
    hyena_q,
    hyena_k,
    hyena_v,
    hyena_grad,
    pole_rate,
    residue,
    norm_gain,
    doc_ids,
    attn_q,
    attn_k,
    attn_v,
    attn_grad,
):
    length = hyena_q.shape[0]
    scaling = jnp.sqrt(-jnp.expm1(-2.0 * pole_rate))
    weight = residue * scaling
    through = jnp.exp(-pole_rate * length) * (doc_ids[0] == doc_ids[-1]).astype(jnp.float32)
    first_doc = doc_ids[:1]
    last_doc = doc_ids[-1:]
    query_vals = hyena_q.astype(jnp.float32)
    key_vals = hyena_k.astype(jnp.float32)
    value_vals = hyena_v.astype(jnp.float32)
    mixed = key_vals * value_vals
    local_rows, end_state, _ = local_sweep(mixed, doc_ids, pole_rate, weight, mixed)
    carry_fwd = pass_states(first_doc, last_doc, through, end_state, False)
    added_rows, _ = carry_terms(carry_fwd, doc_ids, pole_rate, weight, mixed)
    filtered = local_rows + added_rows
    out_y = query_vals * filtered
    scaled_grad = hyena_grad.astype(jnp.float32) * norm_gain
    total_sq, along = lax.psum(
        (jnp.sum(out_y * out_y, axis=1), jnp.sum(scaled_grad * out_y, axis=1)), "chan"
    )
    inv_rms = lax.rsqrt(total_sq / D + EPSILON)
    grad_y = inv_rms[:, None] * scaled_grad - out_y * (inv_rms**3 * along / D)[:, None]
    grad_hq = (grad_y * filtered).astype(jnp.bfloat16)
    grad_filtered = grad_y * query_vals
    gain_part = jnp.sum(hyena_grad.astype(jnp.float32) * out_y * inv_rms[:, None], axis=0)
    flip_docs = doc_ids[::-1]
    flip_mixed = mixed[::-1]
    back_rows, start_state, back_totals = local_sweep(
        grad_filtered[::-1], flip_docs, pole_rate, weight, flip_mixed
    )
    carry_back = pass_states(last_doc, first_doc, through, start_state, True)
    added_back, added_totals = carry_terms(carry_back, flip_docs, pole_rate, weight, flip_mixed)
    grad_mixed = (back_rows + added_back)[::-1]
    grad_hk = (grad_mixed * value_vals).astype(jnp.bfloat16)
    grad_hv = (grad_mixed * key_vals).astype(jnp.bfloat16)
    residue_part = scaling * (back_totals + added_totals)
    grad_residue, grad_gain = lax.psum((residue_part, gain_part), "ctx")
    heads = attn_q.shape[1] // HEAD_DIM
    scale = HEAD_DIM ** (-0.5)
    rows_q = attn_q.reshape(length, heads, HEAD_DIM)
    rows_back = attn_grad.reshape(length, heads, HEAD_DIM)
    keys_all, values_all, key_docs = (
        lax.all_gather(attn_k, "ctx", axis=0, tiled=True),
        lax.all_gather(attn_v, "ctx", axis=0, tiled=True),
        lax.all_gather(doc_ids, "ctx", axis=0, tiled=True),
    )
    total = keys_all.shape[0]
    span = math.gcd(total, 512)
    nblocks = total // span
    my_pos = lax.axis_index("ctx") * length + jnp.arange(length, dtype=jnp.int32)
    blocks = (
        keys_all.reshape(nblocks, span, heads, HEAD_DIM),
        values_all.reshape(nblocks, span, heads, HEAD_DIM),
        key_docs.reshape(nblocks, span),
        jnp.arange(nblocks, dtype=jnp.int32) * span,
    )

    def scores_of(key_part, doc_part, start):
        scores = (
            jnp.einsum("thd,khd->htk", rows_q, key_part, preferred_element_type=jnp.float32) * scale
        )
        key_pos = start + jnp.arange(span, dtype=jnp.int32)
        valid = (key_pos[None, :] <= my_pos[:, None]) & (doc_part[None, :] == doc_ids[:, None])
        return (scores, valid[None])

    def first_work(carry, block):
        key_part, value_part, doc_part, start = block
        peak, totals, weighted = carry
        scores, valid = scores_of(key_part, doc_part, start)
        new_peak = jnp.maximum(peak, jnp.max(jnp.where(valid, scores, FLOOR_SCORE), axis=2))
        probability = jnp.exp(jnp.where(valid, scores - new_peak[..., None], FLOOR_SCORE))
        grad_prob = jnp.einsum(
            "thd,khd->htk", rows_back, value_part, preferred_element_type=jnp.float32
        )
        shrink = jnp.exp(peak - new_peak)
        return (
            new_peak,
            totals * shrink + jnp.sum(probability, axis=2),
            weighted * shrink + jnp.sum(probability * grad_prob, axis=2),
        )

    def first_step(carry, block):
        kept = first_work(carry, block)
        return (kept, None)

    row_shape = (heads, length)
    start_stats = (
        jnp.full(row_shape, FLOOR_SCORE, jnp.float32),
        jnp.zeros(row_shape, jnp.float32),
        jnp.zeros(row_shape, jnp.float32),
    )
    (peak, totals, weighted), _ = lax.scan(first_step, start_stats, blocks)
    log_total = peak + jnp.log(totals)
    centre = weighted / totals

    def second_work(grad_rows, block):
        key_part, value_part, doc_part, start = block
        scores, valid = scores_of(key_part, doc_part, start)
        probability = jnp.exp(jnp.where(valid, scores - log_total[..., None], FLOOR_SCORE))
        grad_prob = jnp.einsum(
            "thd,khd->htk", rows_back, value_part, preferred_element_type=jnp.float32
        )
        dscores = (probability * (grad_prob - centre[..., None])).astype(jnp.bfloat16)
        rounded = probability.astype(jnp.bfloat16)
        grad_rows = grad_rows + jnp.einsum(
            "htk,khd->thd", dscores, key_part, preferred_element_type=jnp.float32
        )
        key_grad = (
            scale * jnp.einsum("htk,thd->khd", dscores, rows_q, preferred_element_type=jnp.float32)
        ).astype(jnp.bfloat16)
        value_grad = jnp.einsum(
            "htk,thd->khd", rounded, rows_back, preferred_element_type=jnp.float32
        ).astype(jnp.bfloat16)
        pieces = (key_grad, value_grad)
        return (grad_rows, pieces)

    def second_step(grad_rows, block):
        result = second_work(grad_rows, block)
        return result

    grad_rows, pieces = lax.scan(
        second_step, jnp.zeros((length, heads, HEAD_DIM), jnp.float32), blocks
    )
    width_a = heads * HEAD_DIM
    grad_aq = (grad_rows * scale).astype(jnp.bfloat16).reshape(length, width_a)
    key_terms_all = pieces[0].reshape(total, width_a)
    value_terms_all = pieces[1].reshape(total, width_a)
    key_sum, value_sum = (
        lax.psum_scatter(key_terms_all, "ctx", scatter_dimension=0, tiled=True).astype(jnp.float32),
        lax.psum_scatter(value_terms_all, "ctx", scatter_dimension=0, tiled=True).astype(
            jnp.float32
        ),
    )
    grad_ak = key_sum.astype(jnp.bfloat16)
    grad_av = value_sum.astype(jnp.bfloat16)
    return (grad_hq, grad_hk, grad_hv, grad_residue, grad_gain, grad_aq, grad_ak, grad_av)


def solution(mesh):
    return jax.shard_map(
        body,
        mesh=mesh,
        in_specs=(
            P("ctx", "chan"),
            P("ctx", "chan"),
            P("ctx", "chan"),
            P("ctx", "chan"),
            P(None, "chan"),
            P(None, "chan"),
            P("chan"),
            P("ctx"),
            P("ctx", "chan"),
            P("ctx", "chan"),
            P("ctx", "chan"),
            P("ctx", "chan"),
        ),
        out_specs=(
            P("ctx", "chan"),
            P("ctx", "chan"),
            P("ctx", "chan"),
            P(None, "chan"),
            P("chan"),
            P("ctx", "chan"),
            P("ctx", "chan"),
            P("ctx", "chan"),
        ),
        check_vma=False,
    )
```

profile of v0, /device:TPU:1, one launch (start us, length us, event | category | flops | bytes accessed | tf_op | source)
XLA Modules:
  0.0 1205.0 jit_solution(15368875127635778406)
XLA Ops:
  24.5 23.7 %all-gather = s32[32,1,128]{2,1,0:T(1,128)S(1)} all-gather(s32[1,1,128]{2,1,0:T(1,128)} %bitcast.294), channel_id=1, replica_groups=mesh['ctx'=32,'chan'=4] {'ctx'}, dimensions={0}, use_global_device_ids=true | all-gather | bytes 16896 | tf_op jit(solution)/shard_map/all_gather | solution.py:148
  55.0 6.9 rev.14
  63.8 37.3 %while.131 = (s32[]{:T(128)}, f32[16,2048]{1,0:T(8,128)S(1)}, s32[]{:T(128)}, f32[4,32,2048]{2,1,0:T(8,128)}, s32[4,32]{1,0:T(4,128)}, /*index=5*/f32[4,32,2048]...) while((s32[]{:T(128)}, f32[16,2048]{1,0:T(8,128)S(1)}, ...), condition=%wide.region_2.3_spmd.clone.clone, body=%wide.region_0.2_spmd.clone.clone.sunk | while | flops 413076544 | bytes 6816653 | solution.py:64
  103.8 253.3 %while.125 = (s32[]{:T(128)}, f32[16,2048]{1,0:T(8,128)S(1)}, f32[16,2048]{1,0:T(8,128)}, s32[1]{0:T(128)}, pred[1]{0:T(512)(128)(4,1)}, /*index=5*/f32[16,2048]...) while((s32[]{:T(128)}, f32[16,2048]{1,0:T(8,128)S(1)}, f32[16,2048]{1,0:T(8,128)}, s32[1]{0:T(128)}, ...), condition=%wide.region_4.5_spmd, body=%wide.region_3.4_spmd.sunk | while | flops 98307 | bytes 1573042 | solution.py:33
  203.4 6.5 collective-permute-start
  212.5 6.5 collective-permute-start
  230.6 6.5 collective-permute-start
  239.6 6.5 collective-permute-start
  257.7 6.5 collective-permute-start
  359.8 23.2 %while.127 = (s32[]{:T(128)}, f32[4,32,2048]{2,1,0:T(8,128)}, f32[1,16,2048]{2,1,0:T(8,128)S(1)}, f32[4]{0:T(128)}, s32[4,32]{1,0:T(4,128)}, /*index=5*/s32[128]...) while((s32[]{:T(128)}, f32[4,32,2048]{2,1,0:T(8,128)}, ...), condition=%wide.region_7.8_spmd.clone, body=%wide.region_5.7_spmd.clone.sunk | while | flops 5177474 | bytes 1180417 | solution.py:85
  386.6 10.2 psum.28
  400.3 7.1 psum.29
  410.9 8.9 rev.13
  420.9 41.7 %while.132 = (s32[]{:T(128)}, f32[16,2048]{1,0:T(8,128)S(1)}, s32[]{:T(128)}, f32[16,2048]{1,0:T(8,128)S(1)}, f32[4,32,2048]{2,1,0:T(8,128)}, /*index=5*/s32[4,3...) while((s32[]{:T(128)}, f32[16,2048]{1,0:T(8,128)S(1)}, ...), condition=%wide.region_15.16_spmd.clone.clone.clone, body=%wide.region_12.15_spmd.clone.clone.clone.sunk | while | flops 415206464 | bytes 8127407 | solution.py:64
  464.7 303.8 %while.126 = (s32[]{:T(128)}, f32[16,2048]{1,0:T(8,128)S(1)}, f32[16,2048]{1,0:T(8,128)}, s32[1]{0:T(128)}, pred[1]{0:T(512)(128)(4,1)}, /*index=5*/f32[16,2048]...) while((s32[]{:T(128)}, f32[16,2048]{1,0:T(8,128)S(1)}, f32[16,2048]{1,0:T(8,128)}, ...), condition=%wide.region_17.18_spmd, body=%wide.region_16.17_spmd.sunk | while | flops 98307 | bytes 1573042 | solution.py:33
  467.2 10.3 collective-permute-done.1
  488.8 8.5 collective-permute-done.1
  508.6 8.5 collective-permute-done.1
  528.3 8.5 collective-permute-done.1
  771.8 29.6 %while.128 = (s32[]{:T(128)}, f32[4,32,2048]{2,1,0:T(8,128)}, f32[4,16,2048]{2,1,0:T(8,128)}, f32[1,16,2048]{2,1,0:T(8,128)S(1)}, f32[4]{0:T(128)}, /*index=5*/s...) while((s32[]{:T(128)}, f32[4,32,2048]{2,1,0:T(8,128)}, ...), condition=%wide.region_21.22_spmd.clone, body=%wide.region_18.21_spmd.clone.sunk | while | flops 7241858 | bytes 2360089 | solution.py:85
  803.6 8.7 copy.79
  812.3 8.9 copy.63
  821.3 8.7 copy.80
  830.0 8.9 copy.61
  838.9 50.8 %while.129 = (s32[]{:T(128)}, f32[8,128]{1,0:T(8,128)S(1)}, f32[8,128]{1,0:T(8,128)S(1)}, f32[8,128]{1,0:T(8,128)S(1)}, s32[8]{0:T(128)S(1)}, /*index=5*/s32[8,5...) while((s32[]{:T(128)}, f32[8,128]{1,0:T(8,128)S(1)}, ...), condition=%wide.region_30.31_spmd.clone, body=%wide.region_26.30_spmd.clone.sunk | while | flops 274931328 | bytes 9260728 | solution.py:195
  889.7 88.7 %while.130 = (s32[]{:T(128)}, f32[128,8,128]{0,2,1:T(8,128)S(1)}, bf16[8,512,8,128]{3,2,1,0:T(8,128)(2,1)}, bf16[8,512,8,128]{3,2,1,0:T(8,128)(2,1)}, bf16[8,512...) while((s32[]{:T(128)}, f32[128,8,128]{0,2,1:T(8,128)S(1)}, ...), condition=%wide.region_32.33_spmd.clone, body=%wide.region_31.32_spmd.clone.sunk | while | flops 676790912 | bytes 21122768 | solution.py:224
  978.4 8.8 copy.91
  987.2 8.8 copy.92
  998.6 6.8 rev.15
  1005.5 70.8 %psum.31 = f32[2048]{0:T(1024)} all-reduce(f32[2048]{0:T(1024)S(1)} %copy-done.12), channel_id=1, replica_groups=mesh['ctx'=32,'chan'=4] {'ctx'}, use_global_device_ids=true, to_apply=%region_25.26 | all-reduce | flops 2048 | bytes 16384 | tf_op jit(solution)/shard_map/psum | solution.py:140
  1079.5 21.1 %reduce-scatter.5.cloned.1.call-done = bf16[128,1024]{1,0:T(8,128)(2,1)} async-done(((bf16[4096,1024]{1,0:T(8,128)(2,1)}), bf16[128,1024]{1,0:T(8,128)(2,1)}) %reduce-scatter.5.cloned.1.call-update) | async-done | bytes 262160 | tf_op jit(solution)/shard_map/reduce_scatter | solution.py:233
  1100.6 96.1 %reduce-scatter.3.cloned.1.call-done = bf16[128,1024]{1,0:T(8,128)(2,1)} async-done(((bf16[4096,1024]{1,0:T(8,128)(2,1)}), bf16[128,1024]{1,0:T(8,128)(2,1)}) %reduce-scatter.3.cloned.1.call-update) | async-done | bytes 262160 | tf_op jit(solution)/shard_map/reduce_scatter | solution.py:232
  (678 shorter events, 746.3 us)
Async XLA Ops:
  7.2 796.4 %all-gather.4.cloned.1.call-start = ((), (), s32[]{:S(2)}) async-start(), calls=%async_computation.3 | async-start | bytes 8650752 | tf_op jit(solution)/shard_map/all_gather | solution.py:146
  7.9 813.3 %all-gather.6.cloned.1.call-start = ((), (), s32[]{:S(2)}) async-start(), calls=%async_computation.4 | async-start | bytes 8650752 | tf_op jit(solution)/shard_map/all_gather | solution.py:147
  9.3 92.5 %collective-permute-start.2 = (s32[1]{0:T(128)}, s32[1]{0:T(128)}, u32[]{:S(2)}, u32[]{:S(2)}) collective-permute-start(s32[1]{0:T(128)} %get-tuple-element.1850), channel_id=1, source_target_pairs={{0,4},{4,8},{8,12},{12,16},{16,20},{20,24},{24,28},{28,32},{32,36}... | collective-permute-start | bytes 20 | tf_op jit(solution)/shard_map/while/body/eval_jaxpr/ppermute | solution.py:20
  13.9 448.9 %collective-permute-start.3 = (s32[1]{0:T(128)}, s32[1]{0:T(128)}, u32[]{:S(2)}, u32[]{:S(2)}) collective-permute-start(s32[1]{0:T(128)} %get-tuple-element.1946), channel_id=1, source_target_pairs={{4,0},{8,4},{12,8},{16,12},{20,16},{24,20},{28,24},{32,28},{36,32}... | collective-permute-start | bytes 20 | tf_op jit(solution)/shard_map/while/body/eval_jaxpr/ppermute | solution.py:20
  15.8 1063.7 %all-reduce.2.cloned.1.call-start = ((), (), s32[]{:S(2)}) async-start(), calls=%async_computation.2 | async-start | bytes 262144 | tf_op jit(solution)/shard_map/psum | solution.py:140
  203.4 8.4 collective-permute-start
  212.5 8.4 collective-permute-start
  221.5 8.4 collective-permute-start
  230.6 8.4 collective-permute-start
  239.6 8.4 collective-permute-start
  248.6 8.4 collective-permute-start
  257.7 8.4 collective-permute-start
  266.7 8.4 collective-permute-start
  275.8 8.4 collective-permute-start
  284.8 8.4 collective-permute-start
  293.8 8.4 collective-permute-start
  302.9 8.4 collective-permute-start
  311.9 8.4 collective-permute-start
  321.0 8.4 collective-permute-start
  330.0 8.4 collective-permute-start
  339.0 8.4 collective-permute-start
  348.1 8.4 collective-permute-start
  464.7 12.9 %collective-permute-start.1 = (f32[16,2048]{1,0:T(8,128)S(1)}, f32[16,2048]{1,0:T(8,128)S(1)}, u32[]{:S(2)}, u32[]{:S(2)}) collective-permute-start(f32[16,2048]{1,0:T(8,128)S(1)} %get-tuple-element.1953), channel_id=1, source_target_pairs={{4,0},{8,4},{12,8},{16,12},{20,16},{24,20},{28,24},{32,28},{36,32}... | collective-permute-start | bytes 393224 | tf_op jit(solution)/shard_map/while/body/eval_jaxpr/ppermute | solution.py:20
  486.2 11.1 collective-permute-start.1
  506.0 11.1 collective-permute-start.1
  525.8 11.1 collective-permute-start.1
  538.1 8.4 collective-permute-start.1
  557.3 8.4 collective-permute-start.1
  566.9 8.4 collective-permute-start.1
  586.1 8.4 collective-permute-start.1
  803.3 297.2 %reduce-scatter.5.cloned.1.call-start = ((), (), s32[]{:S(2)}) async-start(), calls=%async_computation.6 | async-start | bytes 8650752 | tf_op jit(solution)/shard_map/reduce_scatter | solution.py:233
  987.2 209.5 %reduce-scatter.3.cloned.1.call-start = ((), (), s32[]{:S(2)}) async-start(), calls=%async_computation.5 | async-start | bytes 8650752 | tf_op jit(solution)/shard_map/reduce_scatter | solution.py:232
  (112 other events, 1356.9 us)
Sparse Core Ops, SparseCore 0:
  10.3 56.3 all-gather.3
  69.0 53.5 all-gather.5
  803.4 121.4 all-reduce.1
  987.3 113.2 reduce-scatter.4
  1104.7 91.9 reduce-scatter.2
where the time goes:
time: 1220 us; the launch traced here: 1210 us
  waiting for transfers between devices  350 us (29%)
  starting transfers between devices  235 us (19%)
  local copies, waits for them, and re-layouts  215 us (18%)
  matrix products  126 us (10%)
  blocking collectives  112 us (9%)
  other arithmetic  81.2 us (7%)
  loops' own time  64.1 us (5%)
  between operations  21.9 us (2%)
    ppermute x64, starting transfers between devices, from_behind(): lax.ppermute(value, axis, [(source, source + steps) for source in range(f...  234 us
    ppermute x64, waiting for transfers between devices, from_behind(): lax.ppermute(value, axis, [(source, source + steps) for source in range(f...  232 us
    reduce_scatter x1, waiting for transfers between devices, body(): lax.psum_scatter(key_terms_all, 'ctx', scatter_dimension=0, tiled=True)  96.1 us
    psum x1, blocking collectives, body(): grad_residue, grad_gain = lax.psum((residue_part, gain_part), 'ctx')  70.8 us
    unnamed x39, local copies, waits for them, and re-layouts  59.8 us
    another operation x2, loops' own time, pass_states(): lax.fori_loop(0, lax.axis_size('ctx') - 1, pass_advance, start)  57 us
    dot_general x8, matrix products, local_advance(): jnp.einsum('ts,spc->tpc', lower, rise * part[:, None, :], precision=SPLIT...  47.8 us
    while x140, local copies, waits for them, and re-layouts  39.4 us
  transfers between devices with their start and end apart: 69, of which 64 were waited for; matrix products, arithmetic and copies ran while one was open for 31% of the time, Pallas kernels for 0%

commit v1 on v0

v1 whole, which is shorter than its diff:
```python
import jax
import jax.numpy as jnp
from jax import lax
from jax.experimental import pallas as pl
from jax.experimental.pallas import tpu as pltpu
from jax.sharding import PartitionSpec as P

D = 8192
HEAD_DIM = 128
EPSILON = 1e-06
FLOOR_SCORE = -1e30

TOK = 128
CH = 2048
POLES = 16
LANES = 128
CHUNKS = CH // LANES
GROUP = 16
HALF = GROUP * TOK
SPAN = 8
SCALE = HEAD_DIM ** (-0.5)
LOG2E = 1.4426950408889634

ROW_LO, ROW_DOC, ROW_K, ROW_V, ROW_Q, ROW_G, ROWS_IN = 16, 32, 48, 112, 176, 240, 304
OUT_RES, OUT_GAIN, OUT_Q, OUT_KV, ROWS_OUT = 32, 64, 80, 144, 272

TILE = 256
N_TILES = 2 * HALF // TILE
Q_TILES = 4

F32 = jnp.float32
BF16 = jnp.bfloat16


def call(kernel, outs, *args, scratch=(), smem=(), flops=0, nbytes=0, vmem=24 << 20, specs=None):
    grid = (1,) if specs else ()
    specs = specs or {}
    ins = [
        pl.BlockSpec(memory_space=pltpu.SMEM) if i in smem
        else specs.get(i, pl.BlockSpec(memory_space=pltpu.VMEM))
        for i in range(len(args))
    ]
    shapes = [jax.ShapeDtypeStruct(shape, kind) for shape, kind in outs]
    return pl.pallas_call(
        kernel,
        out_shape=shapes,
        grid=grid,
        in_specs=ins,
        out_specs=[pl.BlockSpec(memory_space=pltpu.VMEM) for _ in outs],
        scratch_shapes=list(scratch),
        cost_estimate=pl.CostEstimate(flops=flops, bytes_accessed=nbytes, transcendentals=0),
        compiler_params=pltpu.CompilerParams(vmem_limit_bytes=vmem),
    )(*args)


def every(start, size):
    return pl.ds(start, size, stride=CHUNKS)


def lanes(j):
    return slice(LANES * j, LANES * (j + 1))


def split(value):
    high = value.astype(BF16)
    return high, (value - high.astype(F32)).astype(BF16)


def scaling_of(rate):
    y = 2.0 * rate
    series = 1.0 - y / 6.0
    for k in (5.0, 4.0, 3.0, 2.0):
        series = 1.0 - y / k * series
    return jnp.sqrt(y * series)


def forward_groups(docs, step, state):
    def group(i, state):
        first = i * SPAN

        def plain(state):
            for u in range(SPAN):
                state = step(first + u, state)
            return state

        def cut(state):
            for u in range(SPAN):
                t = first + u
                keep = jnp.where(docs[t] == docs[jnp.maximum(t - 1, 0)], 1.0, 0.0)
                state = step(t, tuple(s * keep for s in state))
            return state

        whole = docs[jnp.maximum(first - 1, 0)] == docs[first + SPAN - 1]
        return lax.cond(whole, plain, cut, state)

    return lax.fori_loop(0, TOK // SPAN, group, state)


def backward_groups(docs, step, state, count):
    def group(i, state):
        first = TOK - SPAN - i * SPAN

        def plain(state):
            for u in reversed(range(SPAN)):
                state = step(first + u, state)
            return state

        def cut(state):
            for u in reversed(range(SPAN)):
                t = first + u
                keep = jnp.where(docs[t] == docs[jnp.minimum(t + 1, TOK - 1)], 1.0, 0.0)
                state = tuple(s * keep for s in state[:count]) + tuple(state[count:])
                state = step(t, state)
            return state

        whole = docs[first] == docs[jnp.minimum(first + SPAN, TOK - 1)]
        return lax.cond(whole, plain, cut, state)

    return lax.fori_loop(0, TOK // SPAN, group, state)


def first_kernel(docs, doc_row, hk, hv, rate, res, aq, ak, av, ag, send, m, dec, wgt, ends):
    rates = rate[...]
    decay = jnp.exp(-rates)
    weight = res[...] * scaling_of(rates)
    for j in range(CHUNKS):
        dec[every(j, POLES), :] = decay[:, lanes(j)]
        wgt[every(j, POLES), :] = weight[:, lanes(j)]
    for j in range(CHUNKS):
        m[every(j, TOK), :] = hk[:, lanes(j)].astype(F32) * hv[:, lanes(j)].astype(F32)
    for g in range(2):
        kept = [dec[n * 16 + 8 * g : n * 16 + 8 * g + 8, :] for n in range(POLES)]

        def step(t, state):
            x = m[pl.ds(pl.multiple_of(t * 16 + 8 * g, 8), 8), :]
            return tuple(d * s + x for d, s in zip(kept, state))

        state = forward_groups(docs, step, (jnp.zeros((8, LANES), F32),) * POLES)
        for n in range(POLES):
            ends[n * 16 + 8 * g : n * 16 + 8 * g + 8, :] = state[n]
    ids = jnp.broadcast_to(doc_row[...].astype(F32), (16, LANES)).astype(BF16)
    for p in range(GROUP):
        high, low = split(ends[every(p, POLES), :])
        send[p, 0:ROW_LO, :] = high
        send[p, ROW_LO:ROW_DOC, :] = low
        send[p, ROW_DOC:ROW_K, :] = ids
        head, part = p // 2, p % 2
        for row, ref in ((ROW_K, ak), (ROW_V, av), (ROW_Q, aq), (ROW_G, ag)):
            send[p, row : row + 64, :] = ref[64 * part : 64 * part + 64, lanes(head)]


def block_docs(got):
    return jnp.concatenate([got[b, ROW_DOC:ROW_K, :].astype(F32)[0:1] for b in range(GROUP)], axis=0)


def end_state(got, b):
    return got[b, 0:ROW_LO, :].astype(F32) + got[b, ROW_LO:ROW_DOC, :].astype(F32)


def spread(value):
    return jnp.broadcast_to(value, (POLES, LANES))


def flags_of(ids):
    first, last = ids[:, 0:1], ids[:, LANES - 1 : LANES]
    same = [spread((first[b : b + 1] == last[b : b + 1]).astype(F32)) for b in range(GROUP)]
    join = [
        spread((last[b : b + 1] == first[b + 1 : b + 2]).astype(F32)) for b in range(GROUP - 1)
    ]
    return same, join


def half_state_kernel(got, rate, out):
    ids = block_docs(got)
    same, join = flags_of(ids)
    through = jnp.exp(-float(TOK) * rate[...])
    carry = jnp.zeros((POLES, LANES), F32)
    for b in range(GROUP):
        carry = end_state(got, b) + same[b] * through * carry
        if b < GROUP - 1:
            carry = join[b] * carry
    out[0:16, :] = carry
    out[16:32, :] = ids


def carry_kernel(got, rate, other, out):
    ids = block_docs(got)
    same, join = flags_of(ids)
    through = jnp.exp(-float(TOK) * rate[...])
    late = jnp.where(lax.axis_index("ctx") >= GROUP, 1.0, 0.0)
    met = spread((other[31:32, LANES - 1 : LANES] == ids[0:1, 0:1]).astype(F32))
    carry = other[0:16, :] * met * late
    for b in range(GROUP):
        out[b] = carry
        if b < GROUP - 1:
            carry = join[b] * (end_state(got, b) + same[b] * through * carry)


def forward_kernel(docs, carry, m, dec, wgt, hq, hg, gain, f, sums):
    for g in range(2):
        kept = [dec[n * 16 + 8 * g : n * 16 + 8 * g + 8, :] for n in range(POLES)]
        weights = [wgt[n * 16 + 8 * g : n * 16 + 8 * g + 8, :] for n in range(POLES)]

        def step(t, state):
            at = pl.ds(pl.multiple_of(t * 16 + 8 * g, 8), 8)
            x = m[at, :]
            state = tuple(d * s + x for d, s in zip(kept, state))
            terms = [w * s for w, s in zip(weights, state)]
            while len(terms) > 1:
                terms = [a + b for a, b in zip(terms[::2], terms[1::2])]
            f[at, :] = terms[0]
            return state

        forward_groups(docs, step, tuple(carry[every(8 * g * 16 + n, 8), :] for n in range(POLES)))
    squares = jnp.zeros((TOK, LANES), F32)
    along = jnp.zeros((TOK, LANES), F32)
    for j in range(CHUNKS):
        out_y = hq[:, lanes(j)].astype(F32) * f[every(j, TOK), :]
        squares = squares + out_y * out_y
        along = along + hg[:, lanes(j)].astype(F32) * gain[:, lanes(j)] * out_y
    sums[0:1, :] = jnp.sum(squares.T, axis=0, keepdims=True)
    sums[1:2, :] = jnp.sum(along.T, axis=0, keepdims=True)
    sums[2:8, :] = jnp.zeros((6, LANES), F32)


def backward_kernel(docs, s0, s1, s2, s3, f, m, dec, hq, hg, gain, ghq, gf, send, starts, totals):
    total = s0[...] + s1[...] + s2[...] + s3[...]
    inv = lax.rsqrt(total[0:1, :] / D + EPSILON)
    slope = inv * inv * inv * total[1:2, :] / D
    inv = jnp.broadcast_to(inv, (TOK, LANES)).T
    slope = jnp.broadcast_to(slope, (TOK, LANES)).T
    for j in range(CHUNKS):
        q = hq[:, lanes(j)].astype(F32)
        back = hg[:, lanes(j)].astype(F32)
        row = f[every(j, TOK), :]
        out_y = q * row
        grad_y = inv * (back * gain[:, lanes(j)]) - out_y * slope
        ghq[:, lanes(j)] = (grad_y * row).astype(BF16)
        gf[every(j, TOK), :] = grad_y * q
        send[j, 32:40, :] = jnp.broadcast_to(
            jnp.sum(back * out_y * inv, axis=0, keepdims=True), (8, LANES)
        )
    for g in range(2):
        kept = [dec[n * 16 + 8 * g : n * 16 + 8 * g + 8, :] for n in range(POLES)]

        def step(t, carry):
            at = pl.ds(pl.multiple_of(t * 16 + 8 * g, 8), 8)
            x, feed = gf[at, :], m[at, :]
            state = tuple(d * s + x for d, s in zip(kept, carry[:POLES]))
            return state + tuple(k + feed * s for k, s in zip(carry[POLES:], state))

        zero = (jnp.zeros((8, LANES), F32),) * (2 * POLES)
        carry = backward_groups(docs, step, zero, POLES)
        for n in range(POLES):
            starts[n * 16 + 8 * g : n * 16 + 8 * g + 8, :] = carry[n]
            totals[n * 16 + 8 * g : n * 16 + 8 * g + 8, :] = carry[POLES + n]
    for p in range(GROUP):
        send[p, 0:16, :] = starts[every(p, POLES), :]
        send[p, 16:32, :] = totals[every(p, POLES), :]


def half_adjoint_kernel(got, back, rate, other, out):
    ids = block_docs(got)
    same, join = flags_of(ids)
    rates = rate[...]
    through = jnp.exp(-float(TOK) * rates)
    decay = jnp.exp(-rates)
    early = jnp.where(lax.axis_index("ctx") < GROUP, 1.0, 0.0)
    met = spread((other[16:17, 0:1] == ids[15:16, LANES - 1 : LANES]).astype(F32)) * early
    total = jnp.zeros((POLES, LANES), F32)
    reach = jnp.zeros((POLES, LANES), F32)
    gains = jnp.zeros((8, LANES), F32)
    carry = jnp.zeros((POLES, LANES), F32)
    unit = met
    for b in reversed(range(GROUP)):
        end = decay * end_state(got, b)
        total = total + back[b, 16:32, :] + end * carry
        reach = reach + end * unit
        gains = gains + back[b, 32:40, :]
        carry = back[b, 0:16, :] + same[b] * through * carry
        unit = same[b] * through * unit
        if b > 0:
            carry = join[b - 1] * carry
            unit = join[b - 1] * unit
    out[0:16, :] = carry
    out[16:32, :] = total
    out[32:48, :] = reach
    out[48:56, :] = gains


def last_pack_kernel(got, back, rate, other, mine, theirs, dq, own, own_got, prev_got, send):
    ids = block_docs(got)
    same, join = flags_of(ids)
    rates = rate[...]
    through = jnp.exp(-float(TOK) * rates)
    early = jnp.where(lax.axis_index("ctx") < GROUP, 1.0, 0.0)
    met = spread((other[16:17, 0:1] == ids[15:16, LANES - 1 : LANES]).astype(F32)) * early
    late_start = mine[0:16, :] * (1.0 - early) + theirs[0:16, :] * early
    early_reach = mine[32:48, :] * early + theirs[32:48, :] * (1.0 - early)
    residue = mine[16:32, :] + theirs[16:32, :] + late_start * early_reach
    residue = scaling_of(rates) * residue
    gains = mine[48:56, :] + theirs[48:56, :]
    res_high, res_low = split(residue)
    gain_high, gain_low = split(gains)
    pair = jnp.concatenate([gain_high.astype(F32), gain_low.astype(F32)], axis=0).astype(BF16)
    carry = theirs[0:16, :] * met
    for b in reversed(range(GROUP)):
        high, low = split(carry)
        send[b, 0:16, :] = high
        send[b, 16:32, :] = low
        send[b, OUT_RES : OUT_RES + 16, :] = res_high
        send[b, OUT_RES + 16 : OUT_GAIN, :] = res_low
        send[b, OUT_GAIN:OUT_Q, :] = pair
        send[b, OUT_Q:OUT_KV, :] = dq[b]
        kv = own[b].astype(F32) + own_got[b].astype(F32) + prev_got[b].astype(F32) * early
        send[b, OUT_KV:ROWS_OUT, :] = kv.astype(BF16)
        if b > 0:
            carry = join[b - 1] * (back[b, 0:16, :] + same[b] * through * carry)


def final_kernel(
    docs, got, gf, dec, wgt, hk, hv, ghk, ghv, gres, ggain, gaq, gak, gav, gm, entry
):
    for p in range(GROUP):
        entry[16 * p : 16 * p + 16, :] = got[p, 0:16, :].astype(F32) + got[p, 16:32, :].astype(F32)
        gres[:, lanes(p)] = got[p, OUT_RES : OUT_RES + 16, :].astype(F32) + got[
            p, OUT_RES + 16 : OUT_GAIN, :
        ].astype(F32)
        pair = got[p, OUT_GAIN:OUT_Q, :].astype(F32)
        ggain[:, lanes(p)] = pair[0:1] + pair[8:9]
        rows = slice(64 * (p % 2), 64 * (p % 2) + 64)
        gaq[rows, lanes(p // 2)] = got[p, OUT_Q:OUT_KV, :]
        gak[rows, lanes(p // 2)] = got[p, OUT_KV : OUT_KV + 64, :]
        gav[rows, lanes(p // 2)] = got[p, OUT_KV + 64 : ROWS_OUT, :]
    for g in range(2):
        kept = [dec[n * 16 + 8 * g : n * 16 + 8 * g + 8, :] for n in range(POLES)]
        weights = [wgt[n * 16 + 8 * g : n * 16 + 8 * g + 8, :] for n in range(POLES)]

        def step(t, state):
            at = pl.ds(pl.multiple_of(t * 16 + 8 * g, 8), 8)
            x = gf[at, :]
            state = tuple(d * s + x for d, s in zip(kept, state))
            terms = [w * s for w, s in zip(weights, state)]
            while len(terms) > 1:
                terms = [a + b for a, b in zip(terms[::2], terms[1::2])]
            gm[at, :] = terms[0]
            return state

        start = tuple(entry[every(8 * g * 16 + n, 8), :] for n in range(POLES))
        backward_groups(docs, step, start, POLES)
    for j in range(CHUNKS):
        row = gm[every(j, TOK), :]
        ghk[:, lanes(j)] = (row * hv[:, lanes(j)].astype(F32)).astype(BF16)
        ghv[:, lanes(j)] = (row * hk[:, lanes(j)].astype(F32)).astype(BF16)


def attention_kernel(
    got, kv_core, kv_half, kv_half_core, ids_mine, ids_other,
    dq, own, own_send, prev, prev_send,
    kbuf, vbuf, kturned, scores, products, dk, dv,
):
    me = lax.axis_index("ctx")
    core = lax.rem(me, 2)
    late = me >= GROUP

    def place(base, b, at_core, keys, values):
        at = pl.ds(pl.multiple_of(base + TOK * b + 64 * at_core, 64), 64)
        kbuf[at, :] = keys
        vbuf[at, :] = values

    for b in range(GROUP):
        place(HALF, b, core, got[b, ROW_K:ROW_V, :], got[b, ROW_V:ROW_Q, :])
        place(HALF, b, 1 - core, kv_core[b, 0:64, :], kv_core[b, 64:128, :])

    @pl.when(late)
    def _():
        for b in range(GROUP):
            place(0, b, core, kv_half[b, 0:64, :], kv_half[b, 64:128, :])
            place(0, b, 1 - core, kv_half_core[b, 0:64, :], kv_half_core[b, 64:128, :])

    first_tile = jnp.where(late, 0, N_TILES // 2)

    def prepare(t, _):
        at = pl.ds(pl.multiple_of(t * TILE, TILE), TILE)
        kturned[t] = kbuf[at, :].astype(F32).T.astype(BF16)
        dk[at, :] = jnp.zeros((TILE, HEAD_DIM), F32)
        dv[at, :] = jnp.zeros((TILE, HEAD_DIM), F32)
        return 0

    lax.fori_loop(first_tile, N_TILES, prepare, 0)

    own_ids, other_ids = ids_mine[16:32, :], ids_other[16:32, :]
    base = jnp.where(late, 0, HALF)
    starts = []
    for d in (1, 2, 3):
        before = jnp.sum((own_ids < d).astype(F32)).astype(jnp.int32)
        behind = jnp.sum((other_ids < d).astype(F32)).astype(jnp.int32)
        starts.append(before + jnp.where(late, behind, HALF))

    def start_of(pos):
        result = jnp.where(pos >= starts[0], starts[0], base)
        for start in starts[1:]:
            result = jnp.where(pos >= start, start, result)
        return result

    def query_tile(i, _):
        rows_q = jnp.concatenate([got[4 * i + u, ROW_Q:ROW_G, :] for u in range(4)], axis=0)
        rows_g = jnp.concatenate([got[4 * i + u, ROW_G:ROWS_IN, :] for u in range(4)], axis=0)
        turned_q = rows_q.astype(F32).T.astype(BF16)
        turned_g = rows_g.astype(F32).T.astype(BF16)
        lane = lax.broadcasted_iota(jnp.int32, (1, TILE), 1)
        qpos = HALF + 512 * i + 128 * (lane // 64) + 64 * core + lax.rem(lane, 64)
        qstart = start_of(qpos)
        low = start_of(HALF + 512 * i + 64 * core) // TILE
        high = HALF // TILE + 2 * i + 2

        def first_pass(t, peak):
            at = pl.ds(pl.multiple_of(t * TILE, TILE), TILE)
            kpos = t * TILE + lax.broadcasted_iota(jnp.int32, (TILE, TILE), 0)
            s = jnp.dot(kbuf[at, :], turned_q, preferred_element_type=F32) * (SCALE * LOG2E)
            s = jnp.where((kpos <= qpos) & (kpos >= qstart), s, FLOOR_SCORE)
            scores[t] = s
            products[t] = jnp.dot(vbuf[at, :], turned_g, preferred_element_type=F32)
            return jnp.maximum(peak, jnp.max(s.reshape(TILE // 8, 8, TILE), axis=0))

        peak = lax.fori_loop(low, high, first_pass, jnp.full((8, TILE), FLOOR_SCORE, F32))
        peak = jnp.max(peak, axis=0, keepdims=True)

        def second_pass(t, carry):
            total, weighted = carry
            p = jnp.exp2(scores[t] - peak)
            scores[t] = p
            total = total + jnp.sum(p.reshape(TILE // 8, 8, TILE), axis=0)
            q = p * products[t]
            return total, weighted + jnp.sum(q.reshape(TILE // 8, 8, TILE), axis=0)

        zero = jnp.zeros((8, TILE), F32)
        total, weighted = lax.fori_loop(low, high, second_pass, (zero, zero))
        inv = 1.0 / jnp.sum(total, axis=0, keepdims=True)
        centre = jnp.sum(weighted, axis=0, keepdims=True) * inv

        def third_pass(t, turned_dq):
            at = pl.ds(pl.multiple_of(t * TILE, TILE), TILE)
            p = scores[t] * inv
            ds = (p * (products[t] - centre)).astype(BF16)
            dk[at, :] += jnp.dot(ds, rows_q, preferred_element_type=F32)
            dv[at, :] += jnp.dot(p.astype(BF16), rows_g, preferred_element_type=F32)
            return turned_dq + jnp.dot(kturned[t], ds, preferred_element_type=F32)

        turned_dq = lax.fori_loop(low, high, third_pass, jnp.zeros((HEAD_DIM, TILE), F32))
        rows = (turned_dq * SCALE).T.astype(BF16)
        for u in range(4):
            dq[4 * i + u] = rows[64 * u : 64 * u + 64]
        return 0

    lax.fori_loop(0, Q_TILES, query_tile, 0)

    def leave(base, target, target_send):
        for b in range(GROUP):
            for at_core, ref in ((core, target), (1 - core, target_send)):
                at = pl.ds(pl.multiple_of(base + TOK * b + 64 * at_core, 64), 64)
                ref[b, 0:64, :] = (dk[at, :] * SCALE).astype(BF16)
                ref[b, 64:128, :] = dv[at, :].astype(BF16)

    leave(HALF, own, own_send)

    @pl.when(late)
    def _():
        leave(0, prev, prev_send)

    @pl.when(jnp.logical_not(late))
    def _():
        prev[...] = jnp.zeros(prev.shape, BF16)
        prev_send[...] = jnp.zeros(prev_send.shape, BF16)


def body(
    hyena_q, hyena_k, hyena_v, hyena_grad, pole_rate, residue, norm_gain, doc_ids,
    attn_q, attn_k, attn_v, attn_grad,
):
    count = 2 * GROUP
    halves = [list(range(GROUP)), list(range(GROUP, count))]
    swap_core = [(i, i ^ 1) for i in range(count)]
    swap_half = [(i, (i + GROUP) % count) for i in range(count)]
    up_half = [(i, i + GROUP) for i in range(GROUP)]
    down_half = [(i + GROUP, i) for i in range(GROUP)]

    def exchange(x):
        return lax.all_to_all(x, "ctx", 0, 0, tiled=True, axis_index_groups=halves)

    gain = norm_gain.reshape(1, CH)
    sweep = (TOK * CHUNKS, LANES)
    params = (POLES * CHUNKS, LANES)
    vmem = pltpu.VMEM
    send, m, dec, wgt = call(
        first_kernel,
        [((GROUP, ROWS_IN, LANES), BF16), (sweep, F32), (params, F32), (params, F32)],
        doc_ids, doc_ids.reshape(1, TOK), hyena_k, hyena_v, pole_rate, residue,
        attn_q, attn_k, attn_v, attn_grad,
        smem=(0,), scratch=[vmem(params, F32)], flops=40_000_000, nbytes=6_000_000,
    )
    got = exchange(send)
    slot = lax.rem(lax.axis_index("ctx"), GROUP)
    rate_part = lax.dynamic_slice_in_dim(pole_rate, slot * LANES, LANES, axis=1)
    head_spec = {0: pl.BlockSpec((GROUP, ROW_K, LANES), lambda i: (0, 0, 0))}

    kv = got[:, ROW_K:ROW_Q, :]
    kv_core = lax.ppermute(kv, "ctx", swap_core)
    kv_half = lax.ppermute(kv, "ctx", up_half)
    (mine,) = call(
        half_state_kernel, [((32, LANES), F32)], got, rate_part, specs=head_spec,
        flops=1_000_000, nbytes=300_000,
    )
    other = lax.ppermute(mine, "ctx", swap_half)
    (carry,) = call(
        carry_kernel, [((GROUP, POLES, LANES), F32)], got, rate_part, other, specs=head_spec,
        flops=1_000_000, nbytes=300_000,
    )
    carry = exchange(carry).reshape(params)
    f, sums = call(
        forward_kernel, [(sweep, F32), ((8, LANES), F32)],
        doc_ids, carry, m, dec, wgt, hyena_q, hyena_grad, gain,
        smem=(0,), flops=40_000_000, nbytes=6_000_000,
    )
    shared = [
        lax.ppermute(sums, "chan", [(i, (i + k) % 4) for i in range(4)]) for k in (1, 2, 3)
    ]
    kv_half_core = lax.ppermute(kv_half, "ctx", swap_core)
    part = (GROUP, TOK, HEAD_DIM)
    dq, own, own_send, prev, prev_send = call(
        attention_kernel,
        [((GROUP, 64, HEAD_DIM), BF16)] + [(part, BF16)] * 4,
        got, kv_core, kv_half, kv_half_core, mine, other,
        scratch=[
            vmem((2 * HALF, HEAD_DIM), BF16),
            vmem((2 * HALF, HEAD_DIM), BF16),
            vmem((N_TILES, HEAD_DIM, TILE), BF16),
            vmem((N_TILES, TILE, TILE), F32),
            vmem((N_TILES, TILE, TILE), F32),
            vmem((2 * HALF, HEAD_DIM), F32),
            vmem((2 * HALF, HEAD_DIM), F32),
        ],
        flops=2_000_000_000, nbytes=6_000_000, vmem=40 << 20,
    )
    own_got = lax.ppermute(own_send, "ctx", swap_core)
    prev_got = lax.ppermute(prev_send, "ctx", swap_core)
    prev_sum = (prev.astype(F32) + prev_got.astype(F32)).astype(BF16)
    prev_home = lax.ppermute(prev_sum, "ctx", down_half)

    ghq, gf, back_send = call(
        backward_kernel,
        [((TOK, CH), BF16), (sweep, F32), ((GROUP, 40, LANES), F32)],
        doc_ids, sums, *shared, f, m, dec, hyena_q, hyena_grad, gain,
        smem=(0,), scratch=[vmem(params, F32), vmem(params, F32)],
        flops=40_000_000, nbytes=6_000_000,
    )
    back = exchange(back_send)
    (half_mine,) = call(
        half_adjoint_kernel, [((56, LANES), F32)], got, back, rate_part, other, specs=head_spec,
        flops=1_000_000, nbytes=300_000,
    )
    half_other = lax.ppermute(half_mine, "ctx", swap_half)
    (last_send,) = call(
        last_pack_kernel, [((GROUP, ROWS_OUT, LANES), BF16)],
        got, back, rate_part, other, half_mine, half_other, dq, own, own_got, prev_home,
        specs=head_spec, flops=1_000_000, nbytes=3_000_000,
    )
    last = exchange(last_send)
    ghk, ghv, gres, ggain, gaq, gak, gav = call(
        final_kernel,
        [((TOK, CH), BF16), ((TOK, CH), BF16), ((POLES, CH), F32), ((1, CH), F32)]
        + [((TOK, 1024), BF16)] * 3,
        doc_ids, last, gf, dec, wgt, hyena_k, hyena_v,
        smem=(0,), scratch=[vmem(sweep, F32), vmem(params, F32)],
        flops=40_000_000, nbytes=6_000_000,
    )
    return (ghq, ghk, ghv, gres, ggain.reshape(CH), gaq, gak, gav)


def solution(mesh):
    wide, deep, one = P("ctx", "chan"), P(None, "chan"), P("chan")
    return jax.shard_map(
        body,
        mesh=mesh,
        in_specs=(wide,) * 4 + (deep, deep, one, P("ctx")) + (wide,) * 4,
        out_specs=(wide, wide, wide, deep, one, wide, wide, wide),
        check_vma=False,
    )
```

time: 1220 us -> 156 us (0.13); the launches traced: 1210 us -> 157 us
  waiting for transfers between devices: 350 us -> 17.5 us
  local copies, waits for them, and re-layouts: 215 us -> 9.91 us
  starting transfers between devices: 235 us -> 34.1 us
  matrix products: 126 us -> 0 us
  other arithmetic: 81.2 us -> 0.18 us
  loops' own time: 64.1 us -> 0 us
  blocking collectives: 112 us -> 66.6 us
  Pallas kernels: 0 us -> 28 us
  between operations: 21.9 us -> 0.74 us
    ppermute x64 -> x11, waiting for transfers between devices: 232 us -> 17.5 us  [the longest x1 10.1 us: body(): kv_half = lax.ppermute(kv, 'ctx', up_half)]
    ppermute x64 -> x11, starting transfers between devices: 234 us -> 34.1 us  [the longest x1 14.5 us: body(): half_other = lax.ppermute(half_mine, 'ctx', swap_half)]
    dot_general x64 -> x0, matrix products: 126 us -> none  [the longest x8 47.8 us: local_advance(): jnp.einsum('ts,spc->tpc', lower, rise * part[:, None, :], precision=SPLIT...]
    reduce_scatter x2 -> x0, waiting for transfers between devices: 117 us -> none  [the longest x1 96.1 us: body(): lax.psum_scatter(key_terms_all, 'ctx', scatter_dimension=0, tiled=True)]
    psum x3 -> x0, blocking collectives: 88.1 us -> none  [the longest x1 70.8 us: body(): grad_residue, grad_gain = lax.psum((residue_part, gain_part), 'ctx')]
    all_to_all x0 -> x4, blocking collectives: none -> 66.6 us  [exchange(): return lax.all_to_all(x, 'ctx', 0, 0, tiled=True, axis_index_groups=halves)]
    another operation x8 -> x0, loops' own time: 64.1 us -> none  [the longest x2 57 us: pass_states(): lax.fori_loop(0, lax.axis_size('ctx') - 1, pass_advance, start)]
    unnamed x39 -> x30, local copies, waits for them, and re-layouts: 59.8 us -> 8.37 us
  transfers between devices with their start and end apart: 69 -> 11, of which waited for: 64 -> 5; matrix products, arithmetic and copies ran while one was open for 31% -> 1% of each run, Pallas kernels for 0% -> 7%
where the time goes in v1:
time: 156 us; the launch traced here: 157 us
  blocking collectives  66.6 us (43%)
  starting transfers between devices  34.1 us (22%)
  Pallas kernels  28 us (18%)
  waiting for transfers between devices  17.5 us (11%)
  local copies, waits for them, and re-layouts  9.91 us (6%)
    all_to_all x4, blocking collectives, exchange(): return lax.all_to_all(x, 'ctx', 0, 0, tiled=True, axis_index_groups=halves)  66.6 us
    pallas_call x9, Pallas kernels, call(): pl.pallas_call(kernel, out_shape=shapes, grid=grid, in_specs=ins, out_spe...  28 us
    ppermute x1, starting transfers between devices, body(): half_other = lax.ppermute(half_mine, 'ctx', swap_half)  14.5 us
    ppermute x1, waiting for transfers between devices, body(): kv_half = lax.ppermute(kv, 'ctx', up_half)  10.1 us
    unnamed x30, local copies, waits for them, and re-layouts  8.37 us
    ppermute x1, starting transfers between devices, body(): kv_half = lax.ppermute(kv, 'ctx', up_half)  4.54 us
    ppermute x3, starting transfers between devices, body(): lax.ppermute(sums, 'chan', [(i, (i + k) % 4) for i in range(4)])  4.53 us
    ppermute x1, starting transfers between devices, body(): other = lax.ppermute(mine, 'ctx', swap_half)  3.68 us
  transfers between devices with their start and end apart: 11, of which 5 were waited for; matrix products, arithmetic and copies ran while one was open for 1% of the time, Pallas kernels for 7%

profile of v1, /device:TPU:1, one launch (start us, length us, event | category | flops | bytes accessed | tf_op | source)
XLA Modules:
  0.0 157.0 jit_solution(16599150993804291548)
XLA Ops:
  0.6 1.0 copy-done.2
  1.7 1.0 copy-done.4
  2.7 0.9 copy-done.6
  3.7 0.9 copy-done.7
  4.6 0.9 copy-done.8
  5.6 0.9 copy-done.9
  6.5 0.9 copy-done.10
  7.4 0.9 copy-done.11
  9.0 3.2 %shard_map.179 = (bf16[16,304,128]{2,1,0:T(8,128)(2,1)S(1)}, f32[2048,128]{1,0:T(8,128)S(1)}, f32[256,128]{1,0:T(8,128)S(1)}, f32[256,128]{1,0:T(8,128)S(1)}) custom-call(s32[128]{0:T(128)S(1)} %copy-done.13, s32[1,128]{1,0:T(1,128)S(1)} %bitcast.7, bf16[128,2048]{1,0:T(8,128)(2,1)S(1)} %copy-done.2, bf16[128,2048]{1,0:T(8,128)(2,1)S(1)} %copy-done.4, ...), custom_call_target="tpu_custom_call" | custom-call | flops 40000000 | bytes 6000000 | tf_op jit(solution)/shard_map/pallas_call | solution.py:44
  12.2 24.5 %all_to_all.20.got = bf16[16,304,128]{2,1,0:T(8,128)(2,1)S(1)} all-to-all(bf16[16,304,128]{2,1,0:T(8,128)(2,1)S(1)} %get-tuple-element.29), channel_id=1, replica_groups={{0,4,8,12,16,20,24,28,32,36,40,44,48,52,56,60},{64,68,72,76,80,84,88,92..., dimensions={0} | all-to-all | bytes 2490368 | tf_op jit(solution)/shard_map/all_to_all | solution.py:489
  36.7 0.8 slice.4
  37.6 4.5 %collective-permute-start.6 = (bf16[16,128,128]{2,1,0:T(8,128)(2,1)}, bf16[16,128,128]{2,1,0:T(8,128)(2,1)S(1)}, u32[]{:S(2)}, u32[]{:S(2)}) collective-permute-start(bf16[16,128,128]{2,1,0:T(8,128)(2,1)} %slice.4), channel_id=1, source_target_pairs={{0,64},{4,68},{8,72},{12,76},{16,80},{20,84},{24,88},{28,92},{32,9... | collective-permute-start | bytes 1572872 | tf_op jit(solution)/shard_map/ppermute | solution.py:509
  42.1 0.9 collective-permute-start.5
  43.0 10.1 %collective-permute-done.6.kv_half = bf16[16,128,128]{2,1,0:T(8,128)(2,1)S(1)} collective-permute-done((bf16[16,128,128]{2,1,0:T(8,128)(2,1)}, bf16[16,128,128]{2,1,0:T(8,128)(2,1)S(1)}, u32[]{:S(2)}, u32[]{:S(2)}) %collective-permute-start.6) | collective-permute-done | bytes 524320 | tf_op jit(solution)/shard_map/ppermute | solution.py:509
  53.1 1.4 collective-permute-start.7
  55.5 3.7 %collective-permute-start = (f32[32,128]{1,0:T(8,128)S(1)}, f32[32,128]{1,0:T(8,128)S(1)}, u32[]{:S(2)}, u32[]{:S(2)}) collective-permute-start(f32[32,128]{1,0:T(8,128)S(1)} %shard_map.180.ids_mine), channel_id=1, source_target_pairs={{0,64},{4,68},{8,72},{12,76},{16,80},{20,84},{24,88},{28,92},{32,9... | collective-permute-start | bytes 49160 | tf_op jit(solution)/shard_map/ppermute | solution.py:514
  59.1 1.1 collective-permute-done.other.ids_other
  60.3 9.0 %shard_map.185 = (bf16[16,64,128]{2,1,0:T(8,128)(2,1)S(1)}, bf16[16,128,128]{2,1,0:T(8,128)(2,1)S(1)}, bf16[16,128,128]{2,1,0:T(8,128)(2,1)S(1)}, bf16[16,128,12...) custom-call(bf16[16,304,128]{2,1,0:T(8,128)(2,1)S(1)} %all_to_all.20.got, ...), custom_call_target="tpu_custom_call" | custom-call | flops 2000000000 | bytes 6000000 | tf_op jit(solution)/shard_map/pallas_call | solution.py:44
  69.3 3.0 %collective-permute-start.9 = (bf16[16,128,128]{2,1,0:T(8,128)(2,1)S(1)}, bf16[16,128,128]{2,1,0:T(8,128)(2,1)S(1)}, u32[]{:S(2)}, u32[]{:S(2)}) collective-permute-start(bf16[16,128,128]{2,1,0:T(8,128)(2,1)S(1)} %get-tuple-element.41), channel_id=1, source_target_pairs={{0,4},{4,0},{8,12},{12,8},{16,20},{20,16},{24,28},{28,24},{32,36},... | collective-permute-start | bytes 1572872 | tf_op jit(solution)/shard_map/ppermute | solution.py:546
  72.4 1.4 collective-permute-done.9
  74.1 1.4 collective-permute-start.10
  75.8 9.0 %all_to_all.21 = f32[16,16,128]{2,1,0:T(8,128)S(1)} all-to-all(f32[16,16,128]{2,1,0:T(8,128)S(1)} %shard_map.181), channel_id=1, replica_groups={{0,4,8,12,16,20,24,28,32,36,40,44,48,52,56,60},{64,68,72,76,80,84,88,92..., dimensions={0} | all-to-all | bytes 262144 | tf_op jit(solution)/shard_map/all_to_all | solution.py:489
  84.8 3.8 %shard_map.182 = (f32[2048,128]{1,0:T(8,128)S(1)}, f32[8,128]{1,0:T(8,128)S(1)}) custom-call(s32[128]{0:T(128)S(1)} %copy-done.14, f32[256,128]{1,0:T(8,128)S(1)} %bitcast.4, f32[2048,128]{1,0:T(8,128)S(1)} %get-tuple-element.30.m, f32[256,128]{1,0:T(8,128)S(1)} %get-tuple-element.31.dec, f32[256,128]{1,0:T(8,128)S(1)} %get-tuple-element.32.wgt, ...), custom_call_target="tpu_custom_call" | custom-call | flops 40000000 | bytes 6000000 | tf_op jit(solution)/shard_map/pallas_call | solution.py:44
  88.5 3.8 %collective-permute-start.3 = (f32[8,128]{1,0:T(8,128)S(1)}, f32[8,128]{1,0:T(8,128)S(1)}, u32[]{:S(2)}, u32[]{:S(2)}) collective-permute-start(f32[8,128]{1,0:T(8,128)S(1)} %get-tuple-element.33.s0), channel_id=1, source_target_pairs={{0,3},{1,0},{2,1},{3,2},{4,7},{5,4},{6,5},{7,6},{8,11},{9,8},{10,9... | collective-permute-start | bytes 12296 | tf_op jit(solution)/shard_map/ppermute | solution.py:526
  92.3 0.7 collective-permute-start.1
  93.1 3.5 %collective-permute-done.2.s2 = f32[8,128]{1,0:T(8,128)S(1)} collective-permute-done((f32[8,128]{1,0:T(8,128)S(1)}, f32[8,128]{1,0:T(8,128)S(1)}, u32[]{:S(2)}, u32[]{:S(2)}) %collective-permute-start.2) | collective-permute-done | bytes 4128 | tf_op jit(solution)/shard_map/ppermute | solution.py:526
  96.6 5.7 %shard_map.183 = (bf16[128,2048]{1,0:T(8,128)(2,1)}, f32[2048,128]{1,0:T(8,128)S(1)}, f32[16,40,128]{2,1,0:T(8,128)S(1)}) custom-call(s32[128]{0:T(128)S(1)} %copy-done.14, f32[8,128]{1,0:T(8,128)S(1)} %get-tuple-element.33.s0, f32[8,128]{1,0:T(8,128)S(1)} %collective-permute-done.1.s1, f32[8,128]{1,0:T(8,128)S(1)} %collective-permute-done.2.s2, ...), custom_call_target="tpu_custom_call" | custom-call | flops 40000000 | bytes 6000000 | tf_op jit(solution)/shard_map/pallas_call | solution.py:44
  102.3 11.7 %all_to_all.22.back = f32[16,40,128]{2,1,0:T(8,128)S(1)} all-to-all(f32[16,40,128]{2,1,0:T(8,128)S(1)} %get-tuple-element.36), channel_id=1, replica_groups={{0,4,8,12,16,20,24,28,32,36,40,44,48,52,56,60},{64,68,72,76,80,84,88,92..., dimensions={0} | all-to-all | bytes 655360 | tf_op jit(solution)/shard_map/all_to_all | solution.py:489
  114.3 14.5 %collective-permute-start.4 = (f32[56,128]{1,0:T(8,128)S(1)}, f32[56,128]{1,0:T(8,128)S(1)}, u32[]{:S(2)}, u32[]{:S(2)}) collective-permute-start(f32[56,128]{1,0:T(8,128)S(1)} %shard_map.184.mine), channel_id=1, source_target_pairs={{0,64},{4,68},{8,72},{12,76},{16,80},{20,84},{24,88},{28,92},{32,9... | collective-permute-start | bytes 86024 | tf_op jit(solution)/shard_map/ppermute | solution.py:562
  128.8 1.3 collective-permute-done.4.theirs
  130.6 21.4 %all_to_all.23.got = bf16[16,272,128]{2,1,0:T(8,128)(2,1)S(1)} all-to-all(bf16[16,272,128]{2,1,0:T(8,128)(2,1)S(1)} %shard_map.186), channel_id=1, replica_groups={{0,4,8,12,16,20,24,28,32,36,40,44,48,52,56,60},{64,68,72,76,80,84,88,92..., dimensions={0} | all-to-all | bytes 2228224 | tf_op jit(solution)/shard_map/all_to_all | solution.py:489
  151.9 5.1 %shard_map.187 = (bf16[128,2048]{1,0:T(8,128)(2,1)}, bf16[128,2048]{1,0:T(8,128)(2,1)}, f32[16,2048]{1,0:T(8,128)}, f32[1,2048]{1,0:T(1,128)}, bf16[128,1024]{1,...) custom-call(s32[128]{0:T(128)S(1)} %copy-done.14, bf16[16,272,128]{2,1,0:T(8,128)(2,1)S(1)} %all_to_all.23.got, ...), custom_call_target="tpu_custom_call" | custom-call | flops 40000000 | bytes 6000000 | tf_op jit(solution)/shard_map/pallas_call | solution.py:44
  (36 shorter events, 2.9 us)
Async XLA Ops:
  0.6 1.0 copy-start.2
  1.7 1.0 copy-start.4
  2.7 0.9 copy-start.6
  3.7 0.9 copy-start.7
  4.6 0.9 copy-start.8
  5.6 0.9 copy-start.9
  6.5 0.9 copy-start.10
  7.4 0.9 copy-start.11
  8.3 0.7 copy-start.13
  37.6 15.6 %collective-permute-start.6 = (bf16[16,128,128]{2,1,0:T(8,128)(2,1)}, bf16[16,128,128]{2,1,0:T(8,128)(2,1)S(1)}, u32[]{:S(2)}, u32[]{:S(2)}) collective-permute-start(bf16[16,128,128]{2,1,0:T(8,128)(2,1)} %slice.4), channel_id=1, source_target_pairs={{0,64},{4,68},{8,72},{12,76},{16,80},{20,84},{24,88},{28,92},{32,9... | collective-permute-start | bytes 1572872 | tf_op jit(solution)/shard_map/ppermute | solution.py:509
  42.1 18.1 %collective-permute-start.5 = (bf16[16,128,128]{2,1,0:T(8,128)(2,1)}, bf16[16,128,128]{2,1,0:T(8,128)(2,1)}, u32[]{:S(2)}, u32[]{:S(2)}) collective-permute-start(bf16[16,128,128]{2,1,0:T(8,128)(2,1)} %slice.4), channel_id=1, source_target_pairs={{0,4},{4,0},{8,12},{12,8},{16,20},{20,16},{24,28},{28,24},{32,36},... | collective-permute-start | bytes 1572872 | tf_op jit(solution)/shard_map/ppermute | solution.py:508
  53.1 7.1 %collective-permute-start.7 = (bf16[16,128,128]{2,1,0:T(8,128)(2,1)S(1)}, bf16[16,128,128]{2,1,0:T(8,128)(2,1)}, u32[]{:S(2)}, u32[]{:S(2)}) collective-permute-start(bf16[16,128,128]{2,1,0:T(8,128)(2,1)S(1)} %collective-permute-done.6.kv_half), channel_id=1, source_target_pairs={{0,4},{4,0},{8,12},{12,8},{16,20},{20,16},{24,28},{28,24},{32,36},... | collective-permute-start | bytes 1572872 | tf_op jit(solution)/shard_map/ppermute | solution.py:528
  55.5 4.8 %collective-permute-start = (f32[32,128]{1,0:T(8,128)S(1)}, f32[32,128]{1,0:T(8,128)S(1)}, u32[]{:S(2)}, u32[]{:S(2)}) collective-permute-start(f32[32,128]{1,0:T(8,128)S(1)} %shard_map.180.ids_mine), channel_id=1, source_target_pairs={{0,64},{4,68},{8,72},{12,76},{16,80},{20,84},{24,88},{28,92},{32,9... | collective-permute-start | bytes 49160 | tf_op jit(solution)/shard_map/ppermute | solution.py:514
  69.3 4.5 %collective-permute-start.9 = (bf16[16,128,128]{2,1,0:T(8,128)(2,1)S(1)}, bf16[16,128,128]{2,1,0:T(8,128)(2,1)S(1)}, u32[]{:S(2)}, u32[]{:S(2)}) collective-permute-start(bf16[16,128,128]{2,1,0:T(8,128)(2,1)S(1)} %get-tuple-element.41), channel_id=1, source_target_pairs={{0,4},{4,0},{8,12},{12,8},{16,20},{20,16},{24,28},{28,24},{32,36},... | collective-permute-start | bytes 1572872 | tf_op jit(solution)/shard_map/ppermute | solution.py:546
  72.3 57.8 %collective-permute-start.8 = (bf16[16,128,128]{2,1,0:T(8,128)(2,1)S(1)}, bf16[16,128,128]{2,1,0:T(8,128)(2,1)S(1)}, u32[]{:S(2)}, u32[]{:S(2)}) collective-permute-start(bf16[16,128,128]{2,1,0:T(8,128)(2,1)S(1)} %get-tuple-element.39), channel_id=1, source_target_pairs={{0,4},{4,0},{8,12},{12,8},{16,20},{20,16},{24,28},{28,24},{32,36},... | collective-permute-start | bytes 1572872 | tf_op jit(solution)/shard_map/ppermute | solution.py:545
  73.9 10.9 %copy-start = (bf16[128,2048]{1,0:T(8,128)(2,1)S(1)}, bf16[128,2048]{1,0:T(8,128)(2,1)}, u32[]{:S(2)}) copy-start(bf16[128,2048]{1,0:T(8,128)(2,1)} %hq.3) | copy-start | bytes 1572868
  73.9 10.9 %copy-start.1 = (bf16[128,2048]{1,0:T(8,128)(2,1)S(1)}, bf16[128,2048]{1,0:T(8,128)(2,1)}, u32[]{:S(2)}) copy-start(bf16[128,2048]{1,0:T(8,128)(2,1)} %hg.3) | copy-start | bytes 1572868
  73.9 10.9 %copy-start.12 = (f32[2048]{0:T(1024)S(1)}, f32[2048]{0:T(1024)}, u32[]{:S(2)}) copy-start(f32[2048]{0:T(1024)} %param.18) | copy-start | bytes 24580
  73.9 10.9 %copy-start.14 = (s32[128]{0:T(128)S(1)}, s32[128]{0:T(128)}, u32[]{:S(2)}) copy-start(s32[128]{0:T(128)} %docs.7) | copy-start | bytes 1540
  74.1 56.0 %collective-permute-start.10 = (bf16[16,128,128]{2,1,0:T(8,128)(2,1)S(1)}, bf16[16,128,128]{2,1,0:T(8,128)(2,1)S(1)}, u32[]{:S(2)}, u32[]{:S(2)}) collective-permute-start(bf16[16,128,128]{2,1,0:T(8,128)(2,1)S(1)} %add_convert_fusion), channel_id=1, source_target_pairs={{64,0},{68,4},{72,8},{76,12},{80,16},{84,20},{88,24},{92,28},{96,3... | collective-permute-start | bytes 1572872 | tf_op jit(solution)/shard_map/ppermute | solution.py:548
  88.5 4.6 %collective-permute-start.3 = (f32[8,128]{1,0:T(8,128)S(1)}, f32[8,128]{1,0:T(8,128)S(1)}, u32[]{:S(2)}, u32[]{:S(2)}) collective-permute-start(f32[8,128]{1,0:T(8,128)S(1)} %get-tuple-element.33.s0), channel_id=1, source_target_pairs={{0,3},{1,0},{2,1},{3,2},{4,7},{5,4},{6,5},{7,6},{8,11},{9,8},{10,9... | collective-permute-start | bytes 12296 | tf_op jit(solution)/shard_map/ppermute | solution.py:526
  92.3 4.3 %collective-permute-start.2 = (f32[8,128]{1,0:T(8,128)S(1)}, f32[8,128]{1,0:T(8,128)S(1)}, u32[]{:S(2)}, u32[]{:S(2)}) collective-permute-start(f32[8,128]{1,0:T(8,128)S(1)} %get-tuple-element.33.s0), channel_id=1, source_target_pairs={{0,2},{1,3},{2,0},{3,1},{4,6},{5,7},{6,4},{7,5},{8,10},{9,11},{10,... | collective-permute-start | bytes 12296 | tf_op jit(solution)/shard_map/ppermute | solution.py:526
  92.3 4.3 %collective-permute-start.1 = (f32[8,128]{1,0:T(8,128)S(1)}, f32[8,128]{1,0:T(8,128)S(1)}, u32[]{:S(2)}, u32[]{:S(2)}) collective-permute-start(f32[8,128]{1,0:T(8,128)S(1)} %get-tuple-element.33.s0), channel_id=1, source_target_pairs={{0,1},{1,2},{2,3},{3,0},{4,5},{5,6},{6,7},{7,4},{8,9},{9,10},{10,1... | collective-permute-start | bytes 12296 | tf_op jit(solution)/shard_map/ppermute | solution.py:526
  114.3 15.8 %collective-permute-start.4 = (f32[56,128]{1,0:T(8,128)S(1)}, f32[56,128]{1,0:T(8,128)S(1)}, u32[]{:S(2)}, u32[]{:S(2)}) collective-permute-start(f32[56,128]{1,0:T(8,128)S(1)} %shard_map.184.mine), channel_id=1, source_target_pairs={{0,64},{4,68},{8,72},{12,76},{16,80},{20,84},{24,88},{28,92},{32,9... | collective-permute-start | bytes 86024 | tf_op jit(solution)/shard_map/ppermute | solution.py:562
  130.5 21.4 %copy-start.3 = (bf16[128,2048]{1,0:T(8,128)(2,1)S(1)}, bf16[128,2048]{1,0:T(8,128)(2,1)}, u32[]{:S(2)}) copy-start(bf16[128,2048]{1,0:T(8,128)(2,1)} %hk.3) | copy-start | bytes 1572868
  130.6 21.4 %copy-start.5 = (bf16[128,2048]{1,0:T(8,128)(2,1)S(1)}, bf16[128,2048]{1,0:T(8,128)(2,1)}, u32[]{:S(2)}) copy-start(bf16[128,2048]{1,0:T(8,128)(2,1)} %hv.3) | copy-start | bytes 1572868

commit v2 on v1

--- a/solution.py
+++ b/solution.py
@@ -23,16 +23,18 @@
 
 ROW_LO, ROW_DOC, ROW_K, ROW_V, ROW_Q, ROW_G, ROWS_IN = 16, 32, 48, 112, 176, 240, 304
 OUT_RES, OUT_GAIN, OUT_Q, OUT_KV, ROWS_OUT = 32, 64, 80, 144, 272
-
-TILE = 256
-N_TILES = 2 * HALF // TILE
+ROWS_BACK = 40
+
+ROWS_TILE = 256
+KEYS_TILE = 512
+N_TILES = 2 * HALF // KEYS_TILE
 Q_TILES = 4
 
 F32 = jnp.float32
 BF16 = jnp.bfloat16
 
 
-def call(kernel, outs, *args, scratch=(), smem=(), flops=0, nbytes=0, vmem=24 << 20, specs=None):
+def call(kernel, outs, *args, scratch=(), smem=(), flops=0, nbytes=0, vmem=24 << 20, specs=None, far=()):
     grid = (1,) if specs else ()
     specs = specs or {}
     ins = [
@@ -46,7 +48,9 @@
         out_shape=shapes,
         grid=grid,
         in_specs=ins,
-        out_specs=[pl.BlockSpec(memory_space=pltpu.VMEM) for _ in outs],
+        out_specs=[
+            pl.BlockSpec(memory_space=pltpu.HBM if i in far else pltpu.VMEM) for i in range(len(outs))
+        ],
         scratch_shapes=list(scratch),
         cost_estimate=pl.CostEstimate(flops=flops, bytes_accessed=nbytes, transcendentals=0),
         compiler_params=pltpu.CompilerParams(vmem_limit_bytes=vmem),
@@ -119,13 +123,43 @@
     return lax.fori_loop(0, TOK // SPAN, group, state)
 
 
-def first_kernel(docs, doc_row, hk, hv, rate, res, aq, ak, av, ag, send, m, dec, wgt, ends):
+def split(value):
+    high = value.astype(BF16)
+    return high, (value - high.astype(F32)).astype(BF16)
+
+
+def joined(ref, index, row):
+    return ref[index, row : row + 16, :].astype(F32) + ref[index, row + 16 : row + 32, :].astype(F32)
+
+
+def first_kernel(
+    docs, doc_row, rate_hbm, res_hbm, hk_hbm, hv_hbm, ak_hbm, av_hbm, aq_hbm, ag_hbm,
+    send, m, dec, wgt, rate_part, ends, rate, res, hk, hv, ak, av, aq, ag, sems,
+):
+    pairs = (
+        (rate_hbm, rate), (res_hbm, res), (hk_hbm, hk), (hv_hbm, hv),
+        (ak_hbm, ak), (av_hbm, av), (aq_hbm, aq), (ag_hbm, ag),
+    )
+    copies = [
+        pltpu.make_async_copy(source, target, sems.at[i])
+        for i, (source, target) in enumerate(pairs)
+    ]
+    for copy in copies:
+        copy.start()
+    ids = jnp.broadcast_to(doc_row[...].astype(F32), (16, LANES)).astype(BF16)
+    for p in range(GROUP):
+        send[p, ROW_DOC:ROW_K, :] = ids
+    copies[0].wait()
+    copies[1].wait()
     rates = rate[...]
+    rate_part[...] = rate[:, pl.ds(pl.multiple_of(position() * LANES, LANES), LANES)]
     decay = jnp.exp(-rates)
     weight = res[...] * scaling_of(rates)
     for j in range(CHUNKS):
         dec[every(j, POLES), :] = decay[:, lanes(j)]
         wgt[every(j, POLES), :] = weight[:, lanes(j)]
+    copies[2].wait()
+    copies[3].wait()
     for j in range(CHUNKS):
         m[every(j, TOK), :] = hk[:, lanes(j)].astype(F32) * hv[:, lanes(j)].astype(F32)
     for g in range(2):
@@ -138,23 +172,35 @@
         state = forward_groups(docs, step, (jnp.zeros((8, LANES), F32),) * POLES)
         for n in range(POLES):
             ends[n * 16 + 8 * g : n * 16 + 8 * g + 8, :] = state[n]
-    ids = jnp.broadcast_to(doc_row[...].astype(F32), (16, LANES)).astype(BF16)
     for p in range(GROUP):
         high, low = split(ends[every(p, POLES), :])
         send[p, 0:ROW_LO, :] = high
         send[p, ROW_LO:ROW_DOC, :] = low
-        send[p, ROW_DOC:ROW_K, :] = ids
-        head, part = p // 2, p % 2
-        for row, ref in ((ROW_K, ak), (ROW_V, av), (ROW_Q, aq), (ROW_G, ag)):
-            send[p, row : row + 64, :] = ref[64 * part : 64 * part + 64, lanes(head)]
+    for copy, row, ref in zip(copies[4:], (ROW_K, ROW_V, ROW_Q, ROW_G), (ak, av, aq, ag)):
+        copy.wait()
+        for p in range(GROUP):
+            part = slice(64 * (p % 2), 64 * (p % 2) + 64)
+            send[p, row : row + 64, :] = ref[part, lanes(p // 2)]
+
+
+def is_late():
+    return lax.axis_index("ctx") >= GROUP
+
+
+def block_at(b):
+    return lax.rem(b + jnp.where(is_late(), 8, 0), GROUP)
+
+
+def position():
+    return block_at(lax.rem(lax.axis_index("ctx"), GROUP))
 
 
 def block_docs(got):
-    return jnp.concatenate([got[b, ROW_DOC:ROW_K, :].astype(F32)[0:1] for b in range(GROUP)], axis=0)
+    return jnp.concatenate([got[block_at(b), ROW_DOC:ROW_K, :].astype(F32)[0:1] for b in range(GROUP)], axis=0)
 
 
 def end_state(got, b):
-    return got[b, 0:ROW_LO, :].astype(F32) + got[b, ROW_LO:ROW_DOC, :].astype(F32)
+    return joined(got, block_at(b), 0)
 
 
 def spread(value):
@@ -187,11 +233,11 @@
     ids = block_docs(got)
     same, join = flags_of(ids)
     through = jnp.exp(-float(TOK) * rate[...])
-    late = jnp.where(lax.axis_index("ctx") >= GROUP, 1.0, 0.0)
+    late = jnp.where(is_late(), 1.0, 0.0)
     met = spread((other[31:32, LANES - 1 : LANES] == ids[0:1, 0:1]).astype(F32))
     carry = other[0:16, :] * met * late
     for b in range(GROUP):
-        out[b] = carry
+        out[block_at(b)] = carry
         if b < GROUP - 1:
             carry = join[b] * (end_state(got, b) + same[b] * through * carry)
 
@@ -265,7 +311,7 @@
     rates = rate[...]
     through = jnp.exp(-float(TOK) * rates)
     decay = jnp.exp(-rates)
-    early = jnp.where(lax.axis_index("ctx") < GROUP, 1.0, 0.0)
+    early = jnp.where(is_late(), 0.0, 1.0)
     met = spread((other[16:17, 0:1] == ids[15:16, LANES - 1 : LANES]).astype(F32)) * early
     total = jnp.zeros((POLES, LANES), F32)
     reach = jnp.zeros((POLES, LANES), F32)
@@ -274,10 +320,10 @@
     unit = met
     for b in reversed(range(GROUP)):
         end = decay * end_state(got, b)
-        total = total + back[b, 16:32, :] + end * carry
+        total = total + back[block_at(b), 16:32, :] + end * carry
         reach = reach + end * unit
-        gains = gains + back[b, 32:40, :]
-        carry = back[b, 0:16, :] + same[b] * through * carry
+        gains = gains + back[block_at(b), 32:40, :]
+        carry = back[block_at(b), 0:16, :] + same[b] * through * carry
         unit = same[b] * through * unit
         if b > 0:
             carry = join[b - 1] * carry
@@ -293,39 +339,36 @@
     same, join = flags_of(ids)
     rates = rate[...]
     through = jnp.exp(-float(TOK) * rates)
-    early = jnp.where(lax.axis_index("ctx") < GROUP, 1.0, 0.0)
+    early = jnp.where(is_late(), 0.0, 1.0)
     met = spread((other[16:17, 0:1] == ids[15:16, LANES - 1 : LANES]).astype(F32)) * early
     late_start = mine[0:16, :] * (1.0 - early) + theirs[0:16, :] * early
     early_reach = mine[32:48, :] * early + theirs[32:48, :] * (1.0 - early)
     residue = mine[16:32, :] + theirs[16:32, :] + late_start * early_reach
-    residue = scaling_of(rates) * residue
-    gains = mine[48:56, :] + theirs[48:56, :]
-    res_high, res_low = split(residue)
-    gain_high, gain_low = split(gains)
+    res_high, res_low = split(scaling_of(rates) * residue)
+    gain_high, gain_low = split(mine[48:56, :] + theirs[48:56, :])
     pair = jnp.concatenate([gain_high.astype(F32), gain_low.astype(F32)], axis=0).astype(BF16)
     carry = theirs[0:16, :] * met
     for b in reversed(range(GROUP)):
+        at = block_at(b)
         high, low = split(carry)
-        send[b, 0:16, :] = high
-        send[b, 16:32, :] = low
-        send[b, OUT_RES : OUT_RES + 16, :] = res_high
-        send[b, OUT_RES + 16 : OUT_GAIN, :] = res_low
-        send[b, OUT_GAIN:OUT_Q, :] = pair
-        send[b, OUT_Q:OUT_KV, :] = dq[b]
-        kv = own[b].astype(F32) + own_got[b].astype(F32) + prev_got[b].astype(F32) * early
-        send[b, OUT_KV:ROWS_OUT, :] = kv.astype(BF16)
+        send[at, 0:16, :] = high
+        send[at, 16:OUT_RES, :] = low
+        send[at, OUT_RES : OUT_RES + 16, :] = res_high
+        send[at, OUT_RES + 16 : OUT_GAIN, :] = res_low
+        send[at, OUT_GAIN:OUT_Q, :] = pair
+        send[at, OUT_Q:OUT_KV, :] = dq[at]
+        kv = own[at].astype(F32) + own_got[at].astype(F32) + prev_got[at].astype(F32) * early
+        send[at, OUT_KV:ROWS_OUT, :] = kv.astype(BF16)
         if b > 0:
-            carry = join[b - 1] * (back[b, 0:16, :] + same[b] * through * carry)
+            carry = join[b - 1] * (back[at, 0:16, :] + same[b] * through * carry)
 
 
 def final_kernel(
     docs, got, gf, dec, wgt, hk, hv, ghk, ghv, gres, ggain, gaq, gak, gav, gm, entry
 ):
     for p in range(GROUP):
-        entry[16 * p : 16 * p + 16, :] = got[p, 0:16, :].astype(F32) + got[p, 16:32, :].astype(F32)
-        gres[:, lanes(p)] = got[p, OUT_RES : OUT_RES + 16, :].astype(F32) + got[
-            p, OUT_RES + 16 : OUT_GAIN, :
-        ].astype(F32)
+        entry[16 * p : 16 * p + 16, :] = joined(got, p, 0)
+        gres[:, lanes(p)] = joined(got, p, OUT_RES)
         pair = got[p, OUT_GAIN:OUT_Q, :].astype(F32)
         ggain[:, lanes(p)] = pair[0:1] + pair[8:9]
         rows = slice(64 * (p % 2), 64 * (p % 2) + 64)
@@ -355,13 +398,12 @@
 
 
 def attention_kernel(
-    got, kv_core, kv_half, kv_half_core, ids_mine, ids_other,
+    got, kv_core, kv_half, kv_half_core, ids_mine, ids_other, after,
     dq, own, own_send, prev, prev_send,
-    kbuf, vbuf, kturned, scores, products, dk, dv,
+    kbuf, vbuf, kturned, scores, products, peaks, dk, dv,
 ):
-    me = lax.axis_index("ctx")
-    core = lax.rem(me, 2)
-    late = me >= GROUP
+    core = lax.rem(lax.axis_index("ctx"), 2)
+    late = is_late()
 
     def place(base, b, at_core, keys, values):
         at = pl.ds(pl.multiple_of(base + TOK * b + 64 * at_core, 64), 64)
@@ -369,8 +411,9 @@
         vbuf[at, :] = values
 
     for b in range(GROUP):
-        place(HALF, b, core, got[b, ROW_K:ROW_V, :], got[b, ROW_V:ROW_Q, :])
-        place(HALF, b, 1 - core, kv_core[b, 0:64, :], kv_core[b, 64:128, :])
+        s = block_at(b)
+        place(HALF, b, core, got[s, ROW_K:ROW_V, :], got[s, ROW_V:ROW_Q, :])
+        place(HALF, b, 1 - core, kv_core[s, 0:64, :], kv_core[s, 64:128, :])
 
     @pl.when(late)
     def _():
@@ -381,10 +424,10 @@
     first_tile = jnp.where(late, 0, N_TILES // 2)
 
     def prepare(t, _):
-        at = pl.ds(pl.multiple_of(t * TILE, TILE), TILE)
+        at = pl.ds(pl.multiple_of(t * KEYS_TILE, KEYS_TILE), KEYS_TILE)
         kturned[t] = kbuf[at, :].astype(F32).T.astype(BF16)
-        dk[at, :] = jnp.zeros((TILE, HEAD_DIM), F32)
-        dv[at, :] = jnp.zeros((TILE, HEAD_DIM), F32)
+        dk[at, :] = jnp.zeros((KEYS_TILE, HEAD_DIM), F32)
+        dv[at, :] = jnp.zeros((KEYS_TILE, HEAD_DIM), F32)
         return 0
 
     lax.fori_loop(first_tile, N_TILES, prepare, 0)
@@ -404,69 +447,71 @@
         return result
 
     def query_tile(i, _):
-        rows_q = jnp.concatenate([got[4 * i + u, ROW_Q:ROW_G, :] for u in range(4)], axis=0)
-        rows_g = jnp.concatenate([got[4 * i + u, ROW_G:ROWS_IN, :] for u in range(4)], axis=0)
+        rows_q = jnp.concatenate([got[block_at(4 * i + u), ROW_Q:ROW_G, :] for u in range(4)], axis=0)
+        rows_g = jnp.concatenate([got[block_at(4 * i + u), ROW_G:ROWS_IN, :] for u in range(4)], axis=0)
         turned_q = rows_q.astype(F32).T.astype(BF16)
         turned_g = rows_g.astype(F32).T.astype(BF16)
-        lane = lax.broadcasted_iota(jnp.int32, (1, TILE), 1)
+        lane = lax.broadcasted_iota(jnp.int32, (1, ROWS_TILE), 1)
         qpos = HALF + 512 * i + 128 * (lane // 64) + 64 * core + lax.rem(lane, 64)
         qstart = start_of(qpos)
-        low = start_of(HALF + 512 * i + 64 * core) // TILE
-        high = HALF // TILE + 2 * i + 2
-
-        def first_pass(t, peak):
-            at = pl.ds(pl.multiple_of(t * TILE, TILE), TILE)
-            kpos = t * TILE + lax.broadcasted_iota(jnp.int32, (TILE, TILE), 0)
-            s = jnp.dot(kbuf[at, :], turned_q, preferred_element_type=F32) * (SCALE * LOG2E)
-            s = jnp.where((kpos <= qpos) & (kpos >= qstart), s, FLOOR_SCORE)
-            scores[t] = s
-            products[t] = jnp.dot(vbuf[at, :], turned_g, preferred_element_type=F32)
-            return jnp.maximum(peak, jnp.max(s.reshape(TILE // 8, 8, TILE), axis=0))
-
-        peak = lax.fori_loop(low, high, first_pass, jnp.full((8, TILE), FLOOR_SCORE, F32))
-        peak = jnp.max(peak, axis=0, keepdims=True)
-
-        def second_pass(t, carry):
-            total, weighted = carry
-            p = jnp.exp2(scores[t] - peak)
+        low = start_of(HALF + 512 * i + 64 * core) // KEYS_TILE
+        high = HALF // KEYS_TILE + i + 1
+        row = lax.broadcasted_iota(jnp.int32, (KEYS_TILE, ROWS_TILE), 0)
+
+        def fold(value, by):
+            return by(value.reshape(KEYS_TILE // 8, 8, ROWS_TILE), axis=0)
+
+        def first_pass(t, carry):
+            peak, total, weighted = carry
+            at = pl.ds(pl.multiple_of(t * KEYS_TILE, KEYS_TILE), KEYS_TILE)
+            s = jnp.dot(kbuf[at, :], turned_q, preferred_element_type=F32)
+            gp = jnp.dot(vbuf[at, :], turned_g, preferred_element_type=F32)
+            first = t * KEYS_TILE
+            s = jnp.where((row <= qpos - first) & (row >= qstart - first), s, FLOOR_SCORE)
+            top = jnp.maximum(peak, jnp.max(fold(s, jnp.max), axis=0, keepdims=True))
+            p = jnp.exp2((s - top) * (SCALE * LOG2E))
             scores[t] = p
-            total = total + jnp.sum(p.reshape(TILE // 8, 8, TILE), axis=0)
-            q = p * products[t]
-            return total, weighted + jnp.sum(q.reshape(TILE // 8, 8, TILE), axis=0)
-
-        zero = jnp.zeros((8, TILE), F32)
-        total, weighted = lax.fori_loop(low, high, second_pass, (zero, zero))
+            products[t] = gp
+            peaks[t] = jnp.broadcast_to(top, (8, ROWS_TILE))
+            shrink = jnp.exp2((peak - top) * (SCALE * LOG2E))
+            return top, total * shrink + fold(p, jnp.sum), weighted * shrink + fold(p * gp, jnp.sum)
+
+        zero = jnp.zeros((8, ROWS_TILE), F32)
+        floor = jnp.full((1, ROWS_TILE), FLOOR_SCORE, F32)
+        peak, total, weighted = lax.fori_loop(low, high, first_pass, (floor, zero, zero))
         inv = 1.0 / jnp.sum(total, axis=0, keepdims=True)
         centre = jnp.sum(weighted, axis=0, keepdims=True) * inv
 
-        def third_pass(t, turned_dq):
-            at = pl.ds(pl.multiple_of(t * TILE, TILE), TILE)
-            p = scores[t] * inv
+        def second_pass(t, turned_dq):
+            at = pl.ds(pl.multiple_of(t * KEYS_TILE, KEYS_TILE), KEYS_TILE)
+            p = scores[t] * (jnp.exp2((peaks[t][0:1] - peak) * (SCALE * LOG2E)) * inv)
             ds = (p * (products[t] - centre)).astype(BF16)
             dk[at, :] += jnp.dot(ds, rows_q, preferred_element_type=F32)
             dv[at, :] += jnp.dot(p.astype(BF16), rows_g, preferred_element_type=F32)
             return turned_dq + jnp.dot(kturned[t], ds, preferred_element_type=F32)
 
-        turned_dq = lax.fori_loop(low, high, third_pass, jnp.zeros((HEAD_DIM, TILE), F32))
+        zero = jnp.zeros((HEAD_DIM, ROWS_TILE), F32)
+        turned_dq = lax.fori_loop(low, high, second_pass, zero)
         rows = (turned_dq * SCALE).T.astype(BF16)
         for u in range(4):
-            dq[4 * i + u] = rows[64 * u : 64 * u + 64]
+            dq[block_at(4 * i + u)] = rows[64 * u : 64 * u + 64]
         return 0
 
     lax.fori_loop(0, Q_TILES, query_tile, 0)
 
-    def leave(base, target, target_send):
+    def leave(base, target, target_send, order):
         for b in range(GROUP):
+            s = order(b)
             for at_core, ref in ((core, target), (1 - core, target_send)):
                 at = pl.ds(pl.multiple_of(base + TOK * b + 64 * at_core, 64), 64)
-                ref[b, 0:64, :] = (dk[at, :] * SCALE).astype(BF16)
-                ref[b, 64:128, :] = dv[at, :].astype(BF16)
-
-    leave(HALF, own, own_send)
+                ref[s, 0:64, :] = (dk[at, :] * SCALE).astype(BF16)
+                ref[s, 64:128, :] = dv[at, :].astype(BF16)
+
+    leave(HALF, own, own_send, block_at)
 
     @pl.when(late)
     def _():
-        leave(0, prev, prev_send)
+        leave(0, prev, prev_send, lambda b: b)
 
     @pl.when(jnp.logical_not(late))
     def _():
@@ -479,44 +524,50 @@
     attn_q, attn_k, attn_v, attn_grad,
 ):
     count = 2 * GROUP
-    halves = [list(range(GROUP)), list(range(GROUP, count))]
+    early = list(range(GROUP))
+    late = [GROUP + (p ^ 8) for p in early]
     swap_core = [(i, i ^ 1) for i in range(count)]
-    swap_half = [(i, (i + GROUP) % count) for i in range(count)]
-    up_half = [(i, i + GROUP) for i in range(GROUP)]
-    down_half = [(i + GROUP, i) for i in range(GROUP)]
+    up_half = list(zip(early, late))
+    down_half = list(zip(late, early))
+    swap_half = up_half + down_half
 
     def exchange(x):
-        return lax.all_to_all(x, "ctx", 0, 0, tiled=True, axis_index_groups=halves)
+        return lax.all_to_all(x, "ctx", 0, 0, tiled=True, axis_index_groups=[early, late])
 
     gain = norm_gain.reshape(1, CH)
     sweep = (TOK * CHUNKS, LANES)
     params = (POLES * CHUNKS, LANES)
     vmem = pltpu.VMEM
-    send, m, dec, wgt = call(
+    hbm = pl.BlockSpec(memory_space=pltpu.HBM)
+    send, m, dec, wgt, rate_part = call(
         first_kernel,
-        [((GROUP, ROWS_IN, LANES), BF16), (sweep, F32), (params, F32), (params, F32)],
-        doc_ids, doc_ids.reshape(1, TOK), hyena_k, hyena_v, pole_rate, residue,
-        attn_q, attn_k, attn_v, attn_grad,
-        smem=(0,), scratch=[vmem(params, F32)], flops=40_000_000, nbytes=6_000_000,
+        [((GROUP, ROWS_IN, LANES), BF16), (sweep, F32), (params, F32), (params, F32)]
+        + [((POLES, LANES), F32)],
+        doc_ids, doc_ids.reshape(1, TOK), pole_rate, residue, hyena_k, hyena_v,
+        attn_k, attn_v, attn_q, attn_grad,
+        smem=(0,), specs={i: hbm for i in range(2, 10)},
+        scratch=[vmem(params, F32)] + [vmem((POLES, CH), F32)] * 2 + [vmem((TOK, CH), BF16)] * 2
+        + [vmem((TOK, 1024), BF16)] * 4 + [pltpu.SemaphoreType.DMA((8,))],
+        flops=40_000_000, nbytes=6_000_000, vmem=60 << 20,
     )
     got = exchange(send)
-    slot = lax.rem(lax.axis_index("ctx"), GROUP)
-    rate_part = lax.dynamic_slice_in_dim(pole_rate, slot * LANES, LANES, axis=1)
     head_spec = {0: pl.BlockSpec((GROUP, ROW_K, LANES), lambda i: (0, 0, 0))}
-
-    kv = got[:, ROW_K:ROW_Q, :]
-    kv_core = lax.ppermute(kv, "ctx", swap_core)
-    kv_half = lax.ppermute(kv, "ctx", up_half)
     (mine,) = call(
         half_state_kernel, [((32, LANES), F32)], got, rate_part, specs=head_spec,
         flops=1_000_000, nbytes=300_000,
     )
+    kv = got[:, ROW_K:ROW_Q, :]
+    kv_core = lax.ppermute(kv, "ctx", swap_core)
     other = lax.ppermute(mine, "ctx", swap_half)
+    other, kv = lax.optimization_barrier((other, kv))
+    kv_half = lax.ppermute(kv, "ctx", up_half)
     (carry,) = call(
         carry_kernel, [((GROUP, POLES, LANES), F32)], got, rate_part, other, specs=head_spec,
         flops=1_000_000, nbytes=300_000,
     )
     carry = exchange(carry).reshape(params)
+    carry, kv_half = lax.optimization_barrier((carry, kv_half))
+    kv_half_core = lax.ppermute(kv_half, "ctx", swap_core)
     f, sums = call(
         forward_kernel, [(sweep, F32), ((8, LANES), F32)],
         doc_ids, carry, m, dec, wgt, hyena_q, hyena_grad, gain,
@@ -525,35 +576,36 @@
     shared = [
         lax.ppermute(sums, "chan", [(i, (i + k) % 4) for i in range(4)]) for k in (1, 2, 3)
     ]
-    kv_half_core = lax.ppermute(kv_half, "ctx", swap_core)
     part = (GROUP, TOK, HEAD_DIM)
     dq, own, own_send, prev, prev_send = call(
         attention_kernel,
         [((GROUP, 64, HEAD_DIM), BF16)] + [(part, BF16)] * 4,
-        got, kv_core, kv_half, kv_half_core, mine, other,
+        got, kv_core, kv_half, kv_half_core, mine, other, sums,
         scratch=[
             vmem((2 * HALF, HEAD_DIM), BF16),
             vmem((2 * HALF, HEAD_DIM), BF16),
-            vmem((N_TILES, HEAD_DIM, TILE), BF16),
-            vmem((N_TILES, TILE, TILE), F32),
-            vmem((N_TILES, TILE, TILE), F32),
+            vmem((N_TILES, HEAD_DIM, KEYS_TILE), BF16),
+            vmem((N_TILES, KEYS_TILE, ROWS_TILE), F32),
+            vmem((N_TILES, KEYS_TILE, ROWS_TILE), F32),
+            vmem((N_TILES, 8, ROWS_TILE), F32),
             vmem((2 * HALF, HEAD_DIM), F32),
             vmem((2 * HALF, HEAD_DIM), F32),
         ],
-        flops=2_000_000_000, nbytes=6_000_000, vmem=40 << 20,
-    )
-    own_got = lax.ppermute(own_send, "ctx", swap_core)
-    prev_got = lax.ppermute(prev_send, "ctx", swap_core)
-    prev_sum = (prev.astype(F32) + prev_got.astype(F32)).astype(BF16)
-    prev_home = lax.ppermute(prev_sum, "ctx", down_half)
-
+        flops=10_000_000_000, nbytes=6_000_000, vmem=40 << 20,
+    )
+    f, dq = lax.optimization_barrier((f, dq))
     ghq, gf, back_send = call(
         backward_kernel,
-        [((TOK, CH), BF16), (sweep, F32), ((GROUP, 40, LANES), F32)],
+        [((TOK, CH), BF16), (sweep, F32), ((GROUP, ROWS_BACK, LANES), F32)],
         doc_ids, sums, *shared, f, m, dec, hyena_q, hyena_grad, gain,
         smem=(0,), scratch=[vmem(params, F32), vmem(params, F32)],
         flops=40_000_000, nbytes=6_000_000,
     )
+    back_send, own_send, prev_send = lax.optimization_barrier((back_send, own_send, prev_send))
+    prev_got = lax.ppermute(prev_send, "ctx", swap_core)
+    own_got = lax.ppermute(own_send, "ctx", swap_core)
+    prev_sum = (prev.astype(F32) + prev_got.astype(F32)).astype(BF16)
+    prev_home = lax.ppermute(prev_sum, "ctx", down_half)
     back = exchange(back_send)
     (half_mine,) = call(
         half_adjoint_kernel, [((56, LANES), F32)], got, back, rate_part, other, specs=head_spec,

time: 156 us -> 127 us (0.81)
  blocking collectives: 66.6 us -> 56.2 us
  starting transfers between devices: 34.1 us -> 23.8 us
  local copies, waits for them, and re-layouts: 9.91 us -> 2.46 us
  waiting for transfers between devices: 17.5 us -> 10.2 us
  Pallas kernels: 28 us -> 33 us
    ppermute x1, starting transfers between devices: 14.5 us -> 3.68 us  [body(): half_other = lax.ppermute(half_mine, 'ctx', swap_half)]
    all_to_all x4 -> x3, blocking collectives: 66.6 us -> 56.2 us  [exchange(): lax.all_to_all(x, 'ctx', 0, 0, tiled=True, axis_index_groups=[early, late])]
    ppermute x1, waiting for transfers between devices: 10.1 us -> 0.01 us  [body(): kv_half = lax.ppermute(kv, 'ctx', up_half)]
    unnamed x30 -> x24, local copies, waits for them, and re-layouts: 8.37 us -> 1.61 us
    all_to_all x0 -> x1, waiting for transfers between devices: none -> 5.9 us  [exchange(): lax.all_to_all(x, 'ctx', 0, 0, tiled=True, axis_index_groups=[early, late])]
    all_to_all x0 -> x1, starting transfers between devices: none -> 5.87 us  [exchange(): lax.all_to_all(x, 'ctx', 0, 0, tiled=True, axis_index_groups=[early, late])]
    pallas_call x9, Pallas kernels: 28 us -> 33 us  [call(): pl.pallas_call(kernel, out_shape=shapes, grid=grid, in_specs=ins, out_spe...]
    ppermute x3, waiting for transfers between devices: 3.53 us -> 0.01 us  [body(): lax.ppermute(sums, 'chan', [(i, (i + k) % 4) for i in range(4)])]
  transfers between devices with their start and end apart: 11 -> 12, of which waited for: 5 -> 4; matrix products, arithmetic and copies ran while one was open for 1% -> 1% of each run, Pallas kernels for 7% -> 12%
where the time goes in v2:
time: 127 us
  blocking collectives  56.2 us (44%)
  Pallas kernels  33 us (26%)
  starting transfers between devices  23.8 us (19%)
  waiting for transfers between devices  10.2 us (8%)
  local copies, waits for them, and re-layouts  2.46 us (2%)
    all_to_all x3, blocking collectives, exchange(): lax.all_to_all(x, 'ctx', 0, 0, tiled=True, axis_index_groups=[early, late])  56.2 us
    pallas_call x9, Pallas kernels, call(): pl.pallas_call(kernel, out_shape=shapes, grid=grid, in_specs=ins, out_spe...  33 us
    all_to_all x1, waiting for transfers between devices, exchange(): lax.all_to_all(x, 'ctx', 0, 0, tiled=True, axis_index_groups=[early, late])  5.9 us
    all_to_all x1, starting transfers between devices, exchange(): lax.all_to_all(x, 'ctx', 0, 0, tiled=True, axis_index_groups=[early, late])  5.87 us
    ppermute x1, starting transfers between devices, body(): kv_half = lax.ppermute(kv, 'ctx', up_half)  4.61 us
    ppermute x3, starting transfers between devices, body(): lax.ppermute(sums, 'chan', [(i, (i + k) % 4) for i in range(4)])  4.54 us
    ppermute x1, starting transfers between devices, body(): half_other = lax.ppermute(half_mine, 'ctx', swap_half)  3.68 us
  transfers between devices with their start and end apart: 12, of which 4 were waited for; matrix products, arithmetic and copies ran while one was open for 1% of the time, Pallas kernels for 12%

profile of v2, /device:TPU:1, one launch (start us, length us, event | category | flops | bytes accessed | tf_op | source)
XLA Modules:
  0.0 126.5 jit_solution(8572937580832996126)
XLA Ops:
  0.6 6.0 %shard_map.179 = (bf16[16,304,128]{2,1,0:T(8,128)(2,1)}, f32[2048,128]{1,0:T(8,128)}, f32[256,128]{1,0:T(8,128)}, f32[256,128]{1,0:T(8,128)}, f32[16,128]{1,0:T(8,128)}) custom-call(s32[128]{0:T(128)} %docs.7, s32[1,128]{1,0:T(1,128)} %bitcast.6, f32[16,2048]{1,0:T(8,128)} %rate_hbm.1, f32[16,2048]{1,0:T(8,128)} %res_hbm.1, bf16[128,2048]{1,0:T(8,128)(2,1)} %hk.1, ...), custom_call_target="tpu_custom_call" | custom-call | flops 40000000 | bytes 6000000 | tf_op jit(solution)/shard_map/pallas_call | solution.py:46
  6.6 0.0 copy-start.9
  6.6 24.7 %all_to_all.20.got = bf16[16,304,128]{2,1,0:T(8,128)(2,1)S(1)} all-to-all(bf16[16,304,128]{2,1,0:T(8,128)(2,1)} %get-tuple-element.39), channel_id=1, replica_groups={{0,4,8,12,16,20,24,28,32,36,40,44,48,52,56,60},{96,100,104,108,112,116,..., dimensions={0} | all-to-all | bytes 2490368 | tf_op jit(solution)/shard_map/all_to_all | solution.py:535
  31.4 0.2 shard_map.180.ids_mine
  31.6 0.0 copy-start.2
  31.7 2.0 %collective-permute-start = (f32[32,128]{1,0:T(8,128)S(1)}, f32[32,128]{1,0:T(8,128)S(1)}, u32[]{:S(2)}, u32[]{:S(2)}) collective-permute-start(f32[32,128]{1,0:T(8,128)S(1)} %shard_map.180.ids_mine), channel_id=1, source_target_pairs={{0,96},{4,100},{8,104},{12,108},{16,112},{20,116},{24,120},{28,124... | collective-permute-start | bytes 49160 | tf_op jit(solution)/shard_map/ppermute | solution.py:561
  33.7 0.8 slice.4
  34.5 1.0 collective-permute-done.other.ids_other
  35.6 4.6 %collective-permute-start.1 = (bf16[16,128,128]{2,1,0:T(8,128)(2,1)}, bf16[16,128,128]{2,1,0:T(8,128)(2,1)}, u32[]{:S(2)}, u32[]{:S(2)}) collective-permute-start(bf16[16,128,128]{2,1,0:T(8,128)(2,1)} %slice.4), channel_id=1, source_target_pairs={{0,96},{4,100},{8,104},{12,108},{16,112},{20,116},{24,120},{28,124... | collective-permute-start | bytes 1572872 | tf_op jit(solution)/shard_map/ppermute | solution.py:563
  40.2 0.3 shard_map.181
  40.5 0.6 copy-done.8
  41.1 5.9 %all-to-all-start.1 = ((f32[16,16,128]{2,1,0:T(8,128)}), f32[16,16,128]{2,1,0:T(8,128)}, u32[]{:S(2)}, u32[]{:S(2)}) async-start(f32[16,16,128]{2,1,0:T(8,128)} %copy-done.8), calls=%async_computation.1 | async-start | bytes 262144 | tf_op jit(solution)/shard_map/all_to_all | solution.py:535
  47.0 0.4 collective-permute-start.5
  47.3 5.9 %all-to-all-done.1 = f32[16,16,128]{2,1,0:T(8,128)} async-done(((f32[16,16,128]{2,1,0:T(8,128)}), f32[16,16,128]{2,1,0:T(8,128)}, u32[]{:S(2)}, u32[]{:S(2)}) %all-to-all-start.1) | async-done | bytes 131104 | tf_op jit(solution)/shard_map/all_to_all | solution.py:535
  53.2 0.5 collective-permute-start.6
  53.8 0.9 copy-done.6
  54.7 4.1 %shard_map.182 = (f32[2048,128]{1,0:T(8,128)S(1)}, f32[8,128]{1,0:T(8,128)S(1)}) custom-call(s32[128]{0:T(128)S(1)} %copy-done.11, f32[256,128]{1,0:T(8,128)} %bitcast.1.carry, f32[2048,128]{1,0:T(8,128)S(1)} %copy-done, f32[256,128]{1,0:T(8,128)S(1)} %copy-done.5, f32[256,128]{1,0:T(8,128)S(1)} %copy-done.6, bf16[128,2048]{1,0:T(8,128)(2,1)S(1)} %copy-done.1, ...), custom_call_target="tpu_custom_call" | custom-call | flops 40000000 | bytes 6000000 | tf_op jit(solution)/shard_map/pallas_call | solution.py:46
  58.8 3.8 %collective-permute-start.4 = (f32[8,128]{1,0:T(8,128)S(1)}, f32[8,128]{1,0:T(8,128)S(1)}, u32[]{:S(2)}, u32[]{:S(2)}) collective-permute-start(f32[8,128]{1,0:T(8,128)S(1)} %get-tuple-element.47.after.s0), channel_id=1, source_target_pairs={{0,3},{1,0},{2,1},{3,2},{4,7},{5,4},{6,5},{7,6},{8,11},{9,8},{10,9... | collective-permute-start | bytes 12296 | tf_op jit(solution)/shard_map/ppermute | solution.py:577
  62.6 0.7 collective-permute-start.2
  63.3 10.9 %shard_map.183 = (bf16[16,64,128]{2,1,0:T(8,128)(2,1)S(1)}, bf16[16,128,128]{2,1,0:T(8,128)(2,1)S(1)}, bf16[16,128,128]{2,1,0:T(8,128)(2,1)S(1)}, bf16[16,128,12...) custom-call(bf16[16,304,128]{2,1,0:T(8,128)(2,1)S(1)} %all_to_all.20.got, ...), custom_call_target="tpu_custom_call" | custom-call | flops 10000000000 | bytes 6000000 | tf_op jit(solution)/shard_map/pallas_call | solution.py:46
  74.3 5.7 %shard_map.184 = (bf16[128,2048]{1,0:T(8,128)(2,1)}, f32[2048,128]{1,0:T(8,128)S(1)}, f32[16,40,128]{2,1,0:T(8,128)S(1)}) custom-call(s32[128]{0:T(128)S(1)} %copy-done.11, f32[8,128]{1,0:T(8,128)S(1)} %get-tuple-element.47.after.s0, f32[8,128]{1,0:T(8,128)S(1)} %collective-permute-done.2.s1, f32[8,128]{1,0:T(8,128)S(1)} %collective-permute-done.3.s2, ...), custom_call_target="tpu_custom_call" | custom-call | flops 40000000 | bytes 6000000 | tf_op jit(solution)/shard_map/pallas_call | solution.py:46
  80.0 1.0 collective-permute-start.9
  81.0 1.5 %collective-permute-done.9 = bf16[16,128,128]{2,1,0:T(8,128)(2,1)S(1)} collective-permute-done((bf16[16,128,128]{2,1,0:T(8,128)(2,1)S(1)}, bf16[16,128,128]{2,1,0:T(8,128)(2,1)S(1)}, u32[]{:S(2)}, u32[]{:S(2)}) %collective-permute-start.9) | collective-permute-done | bytes 524320 | tf_op jit(solution)/shard_map/ppermute | solution.py:605
  82.5 0.1 add_convert_fusion
  82.7 1.3 %collective-permute-start.10 = (bf16[16,128,128]{2,1,0:T(8,128)(2,1)S(1)}, bf16[16,128,128]{2,1,0:T(8,128)(2,1)S(1)}, u32[]{:S(2)}, u32[]{:S(2)}) collective-permute-start(bf16[16,128,128]{2,1,0:T(8,128)(2,1)S(1)} %add_convert_fusion), channel_id=1, source_target_pairs={{96,0},{100,4},{104,8},{108,12},{112,16},{116,20},{120,24},{124,28... | collective-permute-start | bytes 1572872 | tf_op jit(solution)/shard_map/ppermute | solution.py:608
  84.0 10.5 %all_to_all.21.back = f32[16,40,128]{2,1,0:T(8,128)S(1)} all-to-all(f32[16,40,128]{2,1,0:T(8,128)S(1)} %get-tuple-element.56), channel_id=1, replica_groups={{0,4,8,12,16,20,24,28,32,36,40,44,48,52,56,60},{96,100,104,108,112,116,..., dimensions={0} | all-to-all | bytes 655360 | tf_op jit(solution)/shard_map/all_to_all | solution.py:535
  94.5 0.3 shard_map.185.mine
  94.7 3.7 %collective-permute-start.7 = (f32[56,128]{1,0:T(8,128)S(1)}, f32[56,128]{1,0:T(8,128)S(1)}, u32[]{:S(2)}, u32[]{:S(2)}) collective-permute-start(f32[56,128]{1,0:T(8,128)S(1)} %shard_map.185.mine), channel_id=1, source_target_pairs={{0,96},{4,100},{8,104},{12,108},{16,112},{20,116},{24,120},{28,124... | collective-permute-start | bytes 86024 | tf_op jit(solution)/shard_map/ppermute | solution.py:614
  98.4 1.7 %collective-permute-done.7.theirs = f32[56,128]{1,0:T(8,128)S(1)} collective-permute-done((f32[56,128]{1,0:T(8,128)S(1)}, f32[56,128]{1,0:T(8,128)S(1)}, u32[]{:S(2)}, u32[]{:S(2)}) %collective-permute-start.7) | collective-permute-done | bytes 28704 | tf_op jit(solution)/shard_map/ppermute | solution.py:614
  100.1 0.4 shard_map.186
  100.5 21.0 %all_to_all.22.got = bf16[16,272,128]{2,1,0:T(8,128)(2,1)S(1)} all-to-all(bf16[16,272,128]{2,1,0:T(8,128)(2,1)S(1)} %shard_map.186), channel_id=1, replica_groups={{0,4,8,12,16,20,24,28,32,36,40,44,48,52,56,60},{96,100,104,108,112,116,..., dimensions={0} | all-to-all | bytes 2228224 | tf_op jit(solution)/shard_map/all_to_all | solution.py:535
  121.5 5.0 %shard_map.187 = (bf16[128,2048]{1,0:T(8,128)(2,1)}, bf16[128,2048]{1,0:T(8,128)(2,1)}, f32[16,2048]{1,0:T(8,128)}, f32[1,2048]{1,0:T(1,128)}, bf16[128,1024]{1,...) custom-call(s32[128]{0:T(128)S(1)} %copy-done.11, bf16[16,272,128]{2,1,0:T(8,128)(2,1)S(1)} %all_to_all.22.got, ...), custom_call_target="tpu_custom_call" | custom-call | flops 40000000 | bytes 6000000 | tf_op jit(solution)/shard_map/pallas_call | solution.py:46
  (30 shorter events, 0.1 us)
Async XLA Ops:
  6.6 24.7 %copy-start.9 = (f32[16,128]{1,0:T(8,128)S(1)}, f32[16,128]{1,0:T(8,128)}, u32[]{:S(2)}) copy-start(f32[16,128]{1,0:T(8,128)} %get-tuple-element.40.rate) | copy-start | bytes 24580
  31.6 22.1 %copy-start = (f32[2048,128]{1,0:T(8,128)S(1)}, f32[2048,128]{1,0:T(8,128)}, u32[]{:S(2)}) copy-start(f32[2048,128]{1,0:T(8,128)} %get-tuple-element.44.m) | copy-start | bytes 3145732
  31.6 22.1 %copy-start.1 = (bf16[128,2048]{1,0:T(8,128)(2,1)S(1)}, bf16[128,2048]{1,0:T(8,128)(2,1)}, u32[]{:S(2)}) copy-start(bf16[128,2048]{1,0:T(8,128)(2,1)} %hq.3) | copy-start | bytes 1572868
  31.6 22.1 %copy-start.2 = (bf16[128,2048]{1,0:T(8,128)(2,1)S(1)}, bf16[128,2048]{1,0:T(8,128)(2,1)}, u32[]{:S(2)}) copy-start(bf16[128,2048]{1,0:T(8,128)(2,1)} %hg.3) | copy-start | bytes 1572868
  31.6 22.1 %copy-start.5 = (f32[256,128]{1,0:T(8,128)S(1)}, f32[256,128]{1,0:T(8,128)}, u32[]{:S(2)}) copy-start(f32[256,128]{1,0:T(8,128)} %get-tuple-element.45.dec) | copy-start | bytes 393220
  31.7 22.1 %copy-start.10 = (f32[2048]{0:T(1024)S(1)}, f32[2048]{0:T(1024)}, u32[]{:S(2)}) copy-start(f32[2048]{0:T(1024)} %param.18) | copy-start | bytes 24580
  31.7 22.1 %copy-start.11 = (s32[128]{0:T(128)S(1)}, s32[128]{0:T(128)}, u32[]{:S(2)}) copy-start(s32[128]{0:T(128)} %docs.7) | copy-start | bytes 1540
  31.7 3.9 %collective-permute-start = (f32[32,128]{1,0:T(8,128)S(1)}, f32[32,128]{1,0:T(8,128)S(1)}, u32[]{:S(2)}, u32[]{:S(2)}) collective-permute-start(f32[32,128]{1,0:T(8,128)S(1)} %shard_map.180.ids_mine), channel_id=1, source_target_pairs={{0,96},{4,100},{8,104},{12,108},{16,112},{20,116},{24,120},{28,124... | collective-permute-start | bytes 49160 | tf_op jit(solution)/shard_map/ppermute | solution.py:561
  35.6 17.7 %collective-permute-start.1 = (bf16[16,128,128]{2,1,0:T(8,128)(2,1)}, bf16[16,128,128]{2,1,0:T(8,128)(2,1)}, u32[]{:S(2)}, u32[]{:S(2)}) collective-permute-start(bf16[16,128,128]{2,1,0:T(8,128)(2,1)} %slice.4), channel_id=1, source_target_pairs={{0,96},{4,100},{8,104},{12,108},{16,112},{20,116},{24,120},{28,124... | collective-permute-start | bytes 1572872 | tf_op jit(solution)/shard_map/ppermute | solution.py:563
  40.5 0.7 copy-start.8
  41.1 12.1 %all-to-all-start.1 = ((f32[16,16,128]{2,1,0:T(8,128)}), f32[16,16,128]{2,1,0:T(8,128)}, u32[]{:S(2)}, u32[]{:S(2)}) async-start(f32[16,16,128]{2,1,0:T(8,128)} %copy-done.8), calls=%async_computation.1 | async-start | bytes 262144 | tf_op jit(solution)/shard_map/all_to_all | solution.py:535
  47.0 16.4 %collective-permute-start.5 = (bf16[16,128,128]{2,1,0:T(8,128)(2,1)}, bf16[16,128,128]{2,1,0:T(8,128)(2,1)}, u32[]{:S(2)}, u32[]{:S(2)}) collective-permute-start(bf16[16,128,128]{2,1,0:T(8,128)(2,1)} %slice.4), channel_id=1, source_target_pairs={{0,4},{4,0},{8,12},{12,8},{16,20},{20,16},{24,28},{28,24},{32,36},... | collective-permute-start | bytes 1572872 | tf_op jit(solution)/shard_map/ppermute | solution.py:560
  53.2 10.1 %collective-permute-start.6 = (bf16[16,128,128]{2,1,0:T(8,128)(2,1)}, bf16[16,128,128]{2,1,0:T(8,128)(2,1)S(1)}, u32[]{:S(2)}, u32[]{:S(2)}) collective-permute-start(bf16[16,128,128]{2,1,0:T(8,128)(2,1)} %collective-permute-done.1.kv_half), channel_id=1, source_target_pairs={{0,4},{4,0},{8,12},{12,8},{16,20},{20,16},{24,28},{28,24},{32,36},... | collective-permute-start | bytes 1572872 | tf_op jit(solution)/shard_map/ppermute | solution.py:570
  53.8 0.9 copy-start.6
  58.8 15.5 %collective-permute-start.4 = (f32[8,128]{1,0:T(8,128)S(1)}, f32[8,128]{1,0:T(8,128)S(1)}, u32[]{:S(2)}, u32[]{:S(2)}) collective-permute-start(f32[8,128]{1,0:T(8,128)S(1)} %get-tuple-element.47.after.s0), channel_id=1, source_target_pairs={{0,3},{1,0},{2,1},{3,2},{4,7},{5,4},{6,5},{7,6},{8,11},{9,8},{10,9... | collective-permute-start | bytes 12296 | tf_op jit(solution)/shard_map/ppermute | solution.py:577
  62.6 11.7 %collective-permute-start.3 = (f32[8,128]{1,0:T(8,128)S(1)}, f32[8,128]{1,0:T(8,128)S(1)}, u32[]{:S(2)}, u32[]{:S(2)}) collective-permute-start(f32[8,128]{1,0:T(8,128)S(1)} %get-tuple-element.47.after.s0), channel_id=1, source_target_pairs={{0,2},{1,3},{2,0},{3,1},{4,6},{5,7},{6,4},{7,5},{8,10},{9,11},{10,... | collective-permute-start | bytes 12296 | tf_op jit(solution)/shard_map/ppermute | solution.py:577
  62.6 11.7 %collective-permute-start.2 = (f32[8,128]{1,0:T(8,128)S(1)}, f32[8,128]{1,0:T(8,128)S(1)}, u32[]{:S(2)}, u32[]{:S(2)}) collective-permute-start(f32[8,128]{1,0:T(8,128)S(1)} %get-tuple-element.47.after.s0), channel_id=1, source_target_pairs={{0,1},{1,2},{2,3},{3,0},{4,5},{5,6},{6,7},{7,4},{8,9},{9,10},{10,1... | collective-permute-start | bytes 12296 | tf_op jit(solution)/shard_map/ppermute | solution.py:577
  80.0 2.5 %collective-permute-start.9 = (bf16[16,128,128]{2,1,0:T(8,128)(2,1)S(1)}, bf16[16,128,128]{2,1,0:T(8,128)(2,1)S(1)}, u32[]{:S(2)}, u32[]{:S(2)}) collective-permute-start(bf16[16,128,128]{2,1,0:T(8,128)(2,1)S(1)} %get-tuple-element.61), channel_id=1, source_target_pairs={{0,4},{4,0},{8,12},{12,8},{16,20},{20,16},{24,28},{28,24},{32,36},... | collective-permute-start | bytes 1572872 | tf_op jit(solution)/shard_map/ppermute | solution.py:605
  81.0 19.1 %collective-permute-start.8 = (bf16[16,128,128]{2,1,0:T(8,128)(2,1)S(1)}, bf16[16,128,128]{2,1,0:T(8,128)(2,1)S(1)}, u32[]{:S(2)}, u32[]{:S(2)}) collective-permute-start(bf16[16,128,128]{2,1,0:T(8,128)(2,1)S(1)} %get-tuple-element.59), channel_id=1, source_target_pairs={{0,4},{4,0},{8,12},{12,8},{16,20},{20,16},{24,28},{28,24},{32,36},... | collective-permute-start | bytes 1572872 | tf_op jit(solution)/shard_map/ppermute | solution.py:606
  82.7 17.4 %collective-permute-start.10 = (bf16[16,128,128]{2,1,0:T(8,128)(2,1)S(1)}, bf16[16,128,128]{2,1,0:T(8,128)(2,1)S(1)}, u32[]{:S(2)}, u32[]{:S(2)}) collective-permute-start(bf16[16,128,128]{2,1,0:T(8,128)(2,1)S(1)} %add_convert_fusion), channel_id=1, source_target_pairs={{96,0},{100,4},{104,8},{108,12},{112,16},{116,20},{120,24},{124,28... | collective-permute-start | bytes 1572872 | tf_op jit(solution)/shard_map/ppermute | solution.py:608
  94.7 5.3 %collective-permute-start.7 = (f32[56,128]{1,0:T(8,128)S(1)}, f32[56,128]{1,0:T(8,128)S(1)}, u32[]{:S(2)}, u32[]{:S(2)}) collective-permute-start(f32[56,128]{1,0:T(8,128)S(1)} %shard_map.185.mine), channel_id=1, source_target_pairs={{0,96},{4,100},{8,104},{12,108},{16,112},{20,116},{24,120},{28,124... | collective-permute-start | bytes 86024 | tf_op jit(solution)/shard_map/ppermute | solution.py:614
  100.5 21.0 %copy-start.3 = (bf16[128,2048]{1,0:T(8,128)(2,1)S(1)}, bf16[128,2048]{1,0:T(8,128)(2,1)}, u32[]{:S(2)}) copy-start(bf16[128,2048]{1,0:T(8,128)(2,1)} %hk.1) | copy-start | bytes 1572868
  100.5 21.0 %copy-start.4 = (bf16[128,2048]{1,0:T(8,128)(2,1)S(1)}, bf16[128,2048]{1,0:T(8,128)(2,1)}, u32[]{:S(2)}) copy-start(bf16[128,2048]{1,0:T(8,128)(2,1)} %hv.1) | copy-start | bytes 1572868
  100.5 21.0 %copy-start.7 = (f32[256,128]{1,0:T(8,128)S(1)}, f32[256,128]{1,0:T(8,128)}, u32[]{:S(2)}) copy-start(f32[256,128]{1,0:T(8,128)} %get-tuple-element.46.wgt) | copy-start | bytes 393220

commit v3 on v2

--- a/solution.py
+++ b/solution.py
@@ -1,3 +1,5 @@
+import functools
+
 import jax
 import jax.numpy as jnp
 from jax import lax
@@ -21,13 +23,16 @@
 SCALE = HEAD_DIM ** (-0.5)
 LOG2E = 1.4426950408889634
 
-ROW_LO, ROW_DOC, ROW_K, ROW_V, ROW_Q, ROW_G, ROWS_IN = 16, 32, 48, 112, 176, 240, 304
-OUT_RES, OUT_GAIN, OUT_Q, OUT_KV, ROWS_OUT = 32, 64, 80, 144, 272
-ROWS_BACK = 40
+HALF_ROWS = POLES * 8
+half_shape = (HALF_ROWS, LANES)
+ROW_DOC, ROW_K, ROW_V, ROW_Q, ROW_G, ROWS_IN = 128, 144, 208, 272, 336, 400
+OUT_RES, OUT_GAIN, OUT_Q, OUT_KV, ROWS_OUT = 16, 48, 64, 128, 256
+BACK_SUM, BACK_GAIN, ROWS_BACK = 16, 48, 64
 
 ROWS_TILE = 256
 KEYS_TILE = 512
 N_TILES = 2 * HALF // KEYS_TILE
+HALF_TILES = N_TILES // 2
 Q_TILES = 4
 
 F32 = jnp.float32
@@ -128,13 +133,18 @@
     return high, (value - high.astype(F32)).astype(BF16)
 
 
+def pair_rows(row):
+    high, low = split(jnp.broadcast_to(row, (8, LANES)))
+    return jnp.concatenate([high.astype(F32), low.astype(F32)], axis=0).astype(BF16)
+
+
 def joined(ref, index, row):
     return ref[index, row : row + 16, :].astype(F32) + ref[index, row + 16 : row + 32, :].astype(F32)
 
 
 def first_kernel(
     docs, doc_row, rate_hbm, res_hbm, hk_hbm, hv_hbm, ak_hbm, av_hbm, aq_hbm, ag_hbm,
-    send, m, dec, wgt, rate_part, ends, rate, res, hk, hv, ak, av, aq, ag, sems,
+    send, m, dec, wgt, through, rate_part, thr_all, rate, res, hk, hv, ak, av, aq, ag, sems,
 ):
     pairs = (
         (rate_hbm, rate), (res_hbm, res), (hk_hbm, hk), (hv_hbm, hv),
@@ -149,15 +159,22 @@
     ids = jnp.broadcast_to(doc_row[...].astype(F32), (16, LANES)).astype(BF16)
     for p in range(GROUP):
         send[p, ROW_DOC:ROW_K, :] = ids
+    core = core_of()
     copies[0].wait()
     copies[1].wait()
     rates = rate[...]
-    rate_part[...] = rate[:, pl.ds(pl.multiple_of(position() * LANES, LANES), LANES)]
+    start = pl.multiple_of(chunk_of(position()) * LANES, LANES)
+    rate_part[...] = rate[:, pl.ds(start, LANES)]
     decay = jnp.exp(-rates)
     weight = res[...] * scaling_of(rates)
+    block = jnp.exp(-float(TOK) * rates)
     for j in range(CHUNKS):
         dec[every(j, POLES), :] = decay[:, lanes(j)]
         wgt[every(j, POLES), :] = weight[:, lanes(j)]
+        thr_all[every(j, POLES), :] = block[:, lanes(j)]
+    for n in range(POLES):
+        at = pl.ds(pl.multiple_of(16 * n + 8 * core, 8), 8)
+        through[8 * n : 8 * n + 8, :] = thr_all[at, :]
     copies[2].wait()
     copies[3].wait()
     for j in range(CHUNKS):
@@ -170,12 +187,10 @@
             return tuple(d * s + x for d, s in zip(kept, state))
 
         state = forward_groups(docs, step, (jnp.zeros((8, LANES), F32),) * POLES)
-        for n in range(POLES):
-            ends[n * 16 + 8 * g : n * 16 + 8 * g + 8, :] = state[n]
-    for p in range(GROUP):
-        high, low = split(ends[every(p, POLES), :])
-        send[p, 0:ROW_LO, :] = high
-        send[p, ROW_LO:ROW_DOC, :] = low
+        pairs = [jnp.concatenate(state[n : n + 2], axis=0).astype(BF16) for n in range(0, POLES, 2)]
+        for p in range(g, GROUP, 2):
+            for i, pair in enumerate(pairs):
+                send[p, 16 * i : 16 * i + 16, :] = pair
     for copy, row, ref in zip(copies[4:], (ROW_K, ROW_V, ROW_Q, ROW_G), (ak, av, aq, ag)):
         copy.wait()
         for p in range(GROUP):
@@ -195,54 +210,89 @@
     return block_at(lax.rem(lax.axis_index("ctx"), GROUP))
 
 
+def core_of():
+    return lax.rem(lax.axis_index("ctx"), 2)
+
+
+def chunk_of(p):
+    return 8 * (p % 2) + p // 2
+
+
+def place_of(j):
+    return 2 * (j % 8) + j // 8
+
+
 def block_docs(got):
-    return jnp.concatenate([got[block_at(b), ROW_DOC:ROW_K, :].astype(F32)[0:1] for b in range(GROUP)], axis=0)
-
-
-def end_state(got, b):
-    return joined(got, block_at(b), 0)
-
-
-def spread(value):
-    return jnp.broadcast_to(value, (POLES, LANES))
-
-
-def flags_of(ids):
+    rows = [got[block_at(b), ROW_DOC:ROW_K, :].astype(F32)[0:1] for b in range(GROUP)]
+    return jnp.concatenate(rows, axis=0)
+
+
+def spread(value, rows=POLES):
+    return jnp.broadcast_to(value, (rows, LANES))
+
+
+def flags_of(ids, rows=POLES):
     first, last = ids[:, 0:1], ids[:, LANES - 1 : LANES]
-    same = [spread((first[b : b + 1] == last[b : b + 1]).astype(F32)) for b in range(GROUP)]
+    same = [spread((first[b : b + 1] == last[b : b + 1]).astype(F32), rows) for b in range(GROUP)]
     join = [
-        spread((last[b : b + 1] == first[b + 1 : b + 2]).astype(F32)) for b in range(GROUP - 1)
+        spread((last[b : b + 1] == first[b + 1 : b + 2]).astype(F32), rows) for b in range(GROUP - 1)
     ]
     return same, join
 
 
-def half_state_kernel(got, rate, out):
+def half_state_kernel(got, through, out, local, ends, inside):
     ids = block_docs(got)
-    same, join = flags_of(ids)
-    through = jnp.exp(-float(TOK) * rate[...])
-    carry = jnp.zeros((POLES, LANES), F32)
+    same, join = flags_of(ids, HALF_ROWS)
+    thr = through[...]
+    state = jnp.zeros(half_shape, F32)
+    reach = jnp.ones(half_shape, F32)
+    turn = lax.rem(lax.axis_index("ctx"), GROUP)
+    column = position() // 2
     for b in range(GROUP):
-        carry = end_state(got, b) + same[b] * through * carry
+        inside[b, 0] = state
+        inside[b, 1] = reach
+        end = got[block_at(b), 0:HALF_ROWS, :].astype(F32)
+        inside[b, 2] = end
+        hold = same[b] * thr
+        state = end + hold * state
+        reach = hold * reach
         if b < GROUP - 1:
-            carry = join[b] * carry
-    out[0:16, :] = carry
-    out[16:32, :] = ids
-
-
-def carry_kernel(got, rate, other, out):
-    ids = block_docs(got)
-    same, join = flags_of(ids)
-    through = jnp.exp(-float(TOK) * rate[...])
+            state, reach = join[b] * state, join[b] * reach
+    out[0:HALF_ROWS, :] = state
+    out[HALF_ROWS:ROW_K, :] = ids
+    partner = turn + 1 - 2 * core_of()
+    local[0] = inside[turn, 0]
+    local[1] = inside[turn, 1]
+    local[2] = inside[partner, 0]
+    local[3] = inside[partner, 1]
+    for s in range(8):
+
+        @pl.when(column == s)
+        def _():
+            for b in range(GROUP):
+                ends[b] = inside[b, 2, pl.ds(s, POLES, stride=8), :]
+
+
+def entry_kernel(local, mine, other, keep, send):
     late = jnp.where(is_late(), 1.0, 0.0)
-    met = spread((other[31:32, LANES - 1 : LANES] == ids[0:1, 0:1]).astype(F32))
-    carry = other[0:16, :] * met * late
-    for b in range(GROUP):
-        out[block_at(b)] = carry
-        if b < GROUP - 1:
-            carry = join[b] * (end_state(got, b) + same[b] * through * carry)
-
-
-def forward_kernel(docs, carry, m, dec, wgt, hq, hg, gain, f, sums):
+    met = (other[ROW_K - 1 : ROW_K, LANES - 1 : LANES] == mine[HALF_ROWS : HALF_ROWS + 1, 0:1])
+    carry = other[0:HALF_ROWS, :] * spread(met.astype(F32), HALF_ROWS) * late
+    keep[...] = local[0] + local[1] * carry
+    send[...] = local[2] + local[3] * carry
+
+
+def keys_kernel(got, kv):
+    kv[...] = got[:, ROW_K:ROW_Q, :]
+
+
+def entry_states(keep, got, g):
+    mine = core_of() == g
+    return tuple(
+        jnp.where(mine, keep[8 * n : 8 * n + 8, :], got[8 * n : 8 * n + 8, :]) for n in range(POLES)
+    )
+
+
+def forward_kernel(docs, keep, got, m, dec, wgt, hq, hg, gain, f, sums):
     for g in range(2):
         kept = [dec[n * 16 + 8 * g : n * 16 + 8 * g + 8, :] for n in range(POLES)]
         weights = [wgt[n * 16 + 8 * g : n * 16 + 8 * g + 8, :] for n in range(POLES)]
@@ -257,7 +307,7 @@
             f[at, :] = terms[0]
             return state
 
-        forward_groups(docs, step, tuple(carry[every(8 * g * 16 + n, 8), :] for n in range(POLES)))
+        forward_groups(docs, step, entry_states(keep, got, g))
     squares = jnp.zeros((TOK, LANES), F32)
     along = jnp.zeros((TOK, LANES), F32)
     for j in range(CHUNKS):
@@ -283,9 +333,8 @@
         grad_y = inv * (back * gain[:, lanes(j)]) - out_y * slope
         ghq[:, lanes(j)] = (grad_y * row).astype(BF16)
         gf[every(j, TOK), :] = grad_y * q
-        send[j, 32:40, :] = jnp.broadcast_to(
-            jnp.sum(back * out_y * inv, axis=0, keepdims=True), (8, LANES)
-        )
+        gain_part = jnp.sum(back * out_y * inv, axis=0, keepdims=True)
+        send[place_of(j), BACK_GAIN:ROWS_BACK, :] = pair_rows(gain_part)
     for g in range(2):
         kept = [dec[n * 16 + 8 * g : n * 16 + 8 * g + 8, :] for n in range(POLES)]
 
@@ -301,29 +350,32 @@
             starts[n * 16 + 8 * g : n * 16 + 8 * g + 8, :] = carry[n]
             totals[n * 16 + 8 * g : n * 16 + 8 * g + 8, :] = carry[POLES + n]
     for p in range(GROUP):
-        send[p, 0:16, :] = starts[every(p, POLES), :]
-        send[p, 16:32, :] = totals[every(p, POLES), :]
-
-
-def half_adjoint_kernel(got, back, rate, other, out):
-    ids = block_docs(got)
+        send[p, 0:16, :] = starts[every(chunk_of(p), POLES), :].astype(BF16)
+        high, low = split(totals[every(chunk_of(p), POLES), :])
+        send[p, BACK_SUM : BACK_SUM + 16, :] = high
+        send[p, BACK_SUM + 16 : BACK_GAIN, :] = low
+
+
+def half_adjoint_kernel(docs_mine, ends, back, rate, docs_other, out):
+    ids, other = docs_mine[HALF_ROWS:ROW_K, :], docs_other[HALF_ROWS:ROW_K, :]
     same, join = flags_of(ids)
     rates = rate[...]
     through = jnp.exp(-float(TOK) * rates)
     decay = jnp.exp(-rates)
     early = jnp.where(is_late(), 0.0, 1.0)
-    met = spread((other[16:17, 0:1] == ids[15:16, LANES - 1 : LANES]).astype(F32)) * early
+    met = spread((other[0:1, 0:1] == ids[15:16, LANES - 1 : LANES]).astype(F32)) * early
     total = jnp.zeros((POLES, LANES), F32)
     reach = jnp.zeros((POLES, LANES), F32)
     gains = jnp.zeros((8, LANES), F32)
     carry = jnp.zeros((POLES, LANES), F32)
     unit = met
     for b in reversed(range(GROUP)):
-        end = decay * end_state(got, b)
-        total = total + back[block_at(b), 16:32, :] + end * carry
+        end = decay * ends[b]
+        total = total + joined(back, block_at(b), BACK_SUM) + end * carry
         reach = reach + end * unit
-        gains = gains + back[block_at(b), 32:40, :]
-        carry = back[block_at(b), 0:16, :] + same[b] * through * carry
+        pair = back[block_at(b), BACK_GAIN:ROWS_BACK, :].astype(F32)
+        gains = gains + pair[0:8] + pair[8:16]
+        carry = back[block_at(b), 0:16, :].astype(F32) + same[b] * through * carry
         unit = same[b] * through * unit
         if b > 0:
             carry = join[b - 1] * carry
@@ -334,25 +386,24 @@
     out[48:56, :] = gains
 
 
-def last_pack_kernel(got, back, rate, other, mine, theirs, dq, own, own_got, prev_got, send):
-    ids = block_docs(got)
+def last_pack_kernel(
+    docs_mine, back, rate, docs_other, mine, theirs, dq, own, own_got, prev_got, send
+):
+    ids, other = docs_mine[HALF_ROWS:ROW_K, :], docs_other[HALF_ROWS:ROW_K, :]
     same, join = flags_of(ids)
     rates = rate[...]
     through = jnp.exp(-float(TOK) * rates)
     early = jnp.where(is_late(), 0.0, 1.0)
-    met = spread((other[16:17, 0:1] == ids[15:16, LANES - 1 : LANES]).astype(F32)) * early
+    met = spread((other[0:1, 0:1] == ids[15:16, LANES - 1 : LANES]).astype(F32)) * early
     late_start = mine[0:16, :] * (1.0 - early) + theirs[0:16, :] * early
     early_reach = mine[32:48, :] * early + theirs[32:48, :] * (1.0 - early)
     residue = mine[16:32, :] + theirs[16:32, :] + late_start * early_reach
     res_high, res_low = split(scaling_of(rates) * residue)
-    gain_high, gain_low = split(mine[48:56, :] + theirs[48:56, :])
-    pair = jnp.concatenate([gain_high.astype(F32), gain_low.astype(F32)], axis=0).astype(BF16)
+    pair = pair_rows((mine[48:56, :] + theirs[48:56, :])[0:1])
     carry = theirs[0:16, :] * met
     for b in reversed(range(GROUP)):
         at = block_at(b)
-        high, low = split(carry)
-        send[at, 0:16, :] = high
-        send[at, 16:OUT_RES, :] = low
+        send[at, 0:OUT_RES, :] = carry.astype(BF16)
         send[at, OUT_RES : OUT_RES + 16, :] = res_high
         send[at, OUT_RES + 16 : OUT_GAIN, :] = res_low
         send[at, OUT_GAIN:OUT_Q, :] = pair
@@ -360,17 +411,18 @@
         kv = own[at].astype(F32) + own_got[at].astype(F32) + prev_got[at].astype(F32) * early
         send[at, OUT_KV:ROWS_OUT, :] = kv.astype(BF16)
         if b > 0:
-            carry = join[b - 1] * (back[at, 0:16, :] + same[b] * through * carry)
+            carry = join[b - 1] * (back[at, 0:16, :].astype(F32) + same[b] * through * carry)
 
 
 def final_kernel(
     docs, got, gf, dec, wgt, hk, hv, ghk, ghv, gres, ggain, gaq, gak, gav, gm, entry
 ):
     for p in range(GROUP):
-        entry[16 * p : 16 * p + 16, :] = joined(got, p, 0)
-        gres[:, lanes(p)] = joined(got, p, OUT_RES)
+        j = chunk_of(p)
+        entry[16 * j : 16 * j + 16, :] = got[p, 0:OUT_RES, :].astype(F32)
+        gres[:, lanes(j)] = joined(got, p, OUT_RES)
         pair = got[p, OUT_GAIN:OUT_Q, :].astype(F32)
-        ggain[:, lanes(p)] = pair[0:1] + pair[8:9]
+        ggain[:, lanes(j)] = pair[0:1] + pair[8:9]
         rows = slice(64 * (p % 2), 64 * (p % 2) + 64)
         gaq[rows, lanes(p // 2)] = got[p, OUT_Q:OUT_KV, :]
         gak[rows, lanes(p // 2)] = got[p, OUT_KV : OUT_KV + 64, :]
@@ -397,42 +449,60 @@
         ghv[:, lanes(j)] = (row * hk[:, lanes(j)].astype(F32)).astype(BF16)
 
 
-def attention_kernel(
-    got, kv_core, kv_half, kv_half_core, ids_mine, ids_other, after,
-    dq, own, own_send, prev, prev_send,
-    kbuf, vbuf, kturned, scores, products, peaks, dk, dv,
-):
-    core = lax.rem(lax.axis_index("ctx"), 2)
-    late = is_late()
-
-    def place(base, b, at_core, keys, values):
-        at = pl.ds(pl.multiple_of(base + TOK * b + 64 * at_core, 64), 64)
-        kbuf[at, :] = keys
-        vbuf[at, :] = values
-
+def place(keys, values, b, at_core, key_rows, value_rows):
+    at = pl.ds(pl.multiple_of(TOK * b + 64 * at_core, 64), 64)
+    keys[at, :] = key_rows
+    values[at, :] = value_rows
+
+
+def turn_keys(keys, turned):
+    def one(t, _):
+        at = pl.ds(pl.multiple_of(t * KEYS_TILE, KEYS_TILE), KEYS_TILE)
+        turned[t] = keys[at, :].astype(F32).T.astype(BF16)
+        return 0
+
+    lax.fori_loop(0, HALF_TILES, one, 0)
+
+
+def own_keys_kernel(kv, kv_core, keys, values, turned):
+    core = core_of()
     for b in range(GROUP):
         s = block_at(b)
-        place(HALF, b, core, got[s, ROW_K:ROW_V, :], got[s, ROW_V:ROW_Q, :])
-        place(HALF, b, 1 - core, kv_core[s, 0:64, :], kv_core[s, 64:128, :])
+        place(keys, values, b, core, kv[s, 0:64, :], kv[s, 64:128, :])
+        place(keys, values, b, 1 - core, kv_core[s, 0:64, :], kv_core[s, 64:128, :])
+    turn_keys(keys, turned)
+
+
+def send_keys_kernel(kv, after, out):
+    out[...] = kv[...]
+
+
+def attention_kernel(
+    got, own_k, own_v, own_turned, kv_half, kv_half_core, ids_mine, ids_other, after,
+    dq, own, own_send, prev, prev_send,
+    prev_k, prev_v, prev_turned, scores, products, peaks, dk, dv,
+):
+    core = core_of()
+    late = is_late()
 
     @pl.when(late)
     def _():
         for b in range(GROUP):
-            place(0, b, core, kv_half[b, 0:64, :], kv_half[b, 64:128, :])
-            place(0, b, 1 - core, kv_half_core[b, 0:64, :], kv_half_core[b, 64:128, :])
-
-    first_tile = jnp.where(late, 0, N_TILES // 2)
-
-    def prepare(t, _):
+            place(prev_k, prev_v, b, core, kv_half[b, 0:64, :], kv_half[b, 64:128, :])
+            place(
+                prev_k, prev_v, b, 1 - core, kv_half_core[b, 0:64, :], kv_half_core[b, 64:128, :]
+            )
+        turn_keys(prev_k, prev_turned)
+
+    def clear(t, _):
         at = pl.ds(pl.multiple_of(t * KEYS_TILE, KEYS_TILE), KEYS_TILE)
-        kturned[t] = kbuf[at, :].astype(F32).T.astype(BF16)
         dk[at, :] = jnp.zeros((KEYS_TILE, HEAD_DIM), F32)
         dv[at, :] = jnp.zeros((KEYS_TILE, HEAD_DIM), F32)
         return 0
 
-    lax.fori_loop(first_tile, N_TILES, prepare, 0)
-
-    own_ids, other_ids = ids_mine[16:32, :], ids_other[16:32, :]
+    lax.fori_loop(jnp.where(late, 0, HALF_TILES), N_TILES, clear, 0)
+
+    own_ids, other_ids = ids_mine[HALF_ROWS:ROW_K, :], ids_other[HALF_ROWS:ROW_K, :]
     base = jnp.where(late, 0, HALF)
     starts = []
     for d in (1, 2, 3):
@@ -461,11 +531,11 @@
         def fold(value, by):
             return by(value.reshape(KEYS_TILE // 8, 8, ROWS_TILE), axis=0)
 
-        def first_pass(t, carry):
+        def first_pass(keys, values, base, t, carry):
             peak, total, weighted = carry
-            at = pl.ds(pl.multiple_of(t * KEYS_TILE, KEYS_TILE), KEYS_TILE)
-            s = jnp.dot(kbuf[at, :], turned_q, preferred_element_type=F32)
-            gp = jnp.dot(vbuf[at, :], turned_g, preferred_element_type=F32)
+            at = pl.ds(pl.multiple_of((t - base) * KEYS_TILE, KEYS_TILE), KEYS_TILE)
+            s = jnp.dot(keys[at, :], turned_q, preferred_element_type=F32)
+            gp = jnp.dot(values[at, :], turned_g, preferred_element_type=F32)
             first = t * KEYS_TILE
             s = jnp.where((row <= qpos - first) & (row >= qstart - first), s, FLOOR_SCORE)
             top = jnp.maximum(peak, jnp.max(fold(s, jnp.max), axis=0, keepdims=True))
@@ -478,20 +548,27 @@
 
         zero = jnp.zeros((8, ROWS_TILE), F32)
         floor = jnp.full((1, ROWS_TILE), FLOOR_SCORE, F32)
-        peak, total, weighted = lax.fori_loop(low, high, first_pass, (floor, zero, zero))
+        ahead = functools.partial(first_pass, prev_k, prev_v, 0)
+        carry = lax.fori_loop(low, HALF_TILES, ahead, (floor, zero, zero))
+        within = functools.partial(first_pass, own_k, own_v, HALF_TILES)
+        middle = jnp.maximum(low, HALF_TILES)
+        peak, total, weighted = lax.fori_loop(middle, high, within, carry)
         inv = 1.0 / jnp.sum(total, axis=0, keepdims=True)
         centre = jnp.sum(weighted, axis=0, keepdims=True) * inv
 
-        def second_pass(t, turned_dq):
+        def second_pass(turned, base, t, turned_dq):
             at = pl.ds(pl.multiple_of(t * KEYS_TILE, KEYS_TILE), KEYS_TILE)
             p = scores[t] * (jnp.exp2((peaks[t][0:1] - peak) * (SCALE * LOG2E)) * inv)
             ds = (p * (products[t] - centre)).astype(BF16)
             dk[at, :] += jnp.dot(ds, rows_q, preferred_element_type=F32)
             dv[at, :] += jnp.dot(p.astype(BF16), rows_g, preferred_element_type=F32)
-            return turned_dq + jnp.dot(kturned[t], ds, preferred_element_type=F32)
+            return turned_dq + jnp.dot(turned[t - base], ds, preferred_element_type=F32)
 
         zero = jnp.zeros((HEAD_DIM, ROWS_TILE), F32)
-        turned_dq = lax.fori_loop(low, high, second_pass, zero)
+        ahead = functools.partial(second_pass, prev_turned, 0)
+        turned_dq = lax.fori_loop(low, HALF_TILES, ahead, zero)
+        within = functools.partial(second_pass, own_turned, HALF_TILES)
+        turned_dq = lax.fori_loop(middle, high, within, turned_dq)
         rows = (turned_dq * SCALE).T.astype(BF16)
         for u in range(4):
             dq[block_at(4 * i + u)] = rows[64 * u : 64 * u + 64]
@@ -539,10 +616,10 @@
     params = (POLES * CHUNKS, LANES)
     vmem = pltpu.VMEM
     hbm = pl.BlockSpec(memory_space=pltpu.HBM)
-    send, m, dec, wgt, rate_part = call(
+    send, m, dec, wgt, through, rate_part = call(
         first_kernel,
         [((GROUP, ROWS_IN, LANES), BF16), (sweep, F32), (params, F32), (params, F32)]
-        + [((POLES, LANES), F32)],
+        + [(half_shape, F32), ((POLES, LANES), F32)],
         doc_ids, doc_ids.reshape(1, TOK), pole_rate, residue, hyena_k, hyena_v,
         attn_k, attn_v, attn_q, attn_grad,
         smem=(0,), specs={i: hbm for i in range(2, 10)},
@@ -551,52 +628,60 @@
         flops=40_000_000, nbytes=6_000_000, vmem=60 << 20,
     )
     got = exchange(send)
-    head_spec = {0: pl.BlockSpec((GROUP, ROW_K, LANES), lambda i: (0, 0, 0))}
-    (mine,) = call(
-        half_state_kernel, [((32, LANES), F32)], got, rate_part, specs=head_spec,
+    mine, local, ends = call(
+        half_state_kernel,
+        [((ROW_K, LANES), F32), ((4,) + half_shape, F32), ((GROUP, POLES, LANES), F32)],
+        got, through, scratch=[vmem((GROUP, 3) + half_shape, F32)],
         flops=1_000_000, nbytes=300_000,
     )
-    kv = got[:, ROW_K:ROW_Q, :]
+    other = lax.ppermute(mine, "ctx", swap_half)
+    part = (GROUP, TOK, HEAD_DIM)
+    (kv,) = call(keys_kernel, [(part, BF16)], got, flops=1000, nbytes=1_000_000)
     kv_core = lax.ppermute(kv, "ctx", swap_core)
-    other = lax.ppermute(mine, "ctx", swap_half)
-    other, kv = lax.optimization_barrier((other, kv))
-    kv_half = lax.ppermute(kv, "ctx", up_half)
-    (carry,) = call(
-        carry_kernel, [((GROUP, POLES, LANES), F32)], got, rate_part, other, specs=head_spec,
-        flops=1_000_000, nbytes=300_000,
-    )
-    carry = exchange(carry).reshape(params)
-    carry, kv_half = lax.optimization_barrier((carry, kv_half))
-    kv_half_core = lax.ppermute(kv_half, "ctx", swap_core)
+    (kv_later,) = call(
+        send_keys_kernel, [(part, BF16)], kv, other, flops=1000, nbytes=1_000_000
+    )
+    kv_half = lax.ppermute(kv_later, "ctx", up_half)
+    flat = (HALF, HEAD_DIM)
+    turned = (HALF_TILES, HEAD_DIM, KEYS_TILE)
+    own_k, own_v, own_turned = call(
+        own_keys_kernel, [(flat, BF16), (flat, BF16), (turned, BF16)], kv, kv_core,
+        flops=1_000_000, nbytes=4_000_000,
+    )
+    carry, carry_send = call(
+        entry_kernel, [(half_shape, F32)] * 2, local, mine, other, flops=100_000, nbytes=300_000
+    )
+    carry_got = lax.ppermute(carry_send, "ctx", swap_core)
     f, sums = call(
         forward_kernel, [(sweep, F32), ((8, LANES), F32)],
-        doc_ids, carry, m, dec, wgt, hyena_q, hyena_grad, gain,
+        doc_ids, carry, carry_got, m, dec, wgt, hyena_q, hyena_grad, gain,
         smem=(0,), flops=40_000_000, nbytes=6_000_000,
     )
     shared = [
         lax.ppermute(sums, "chan", [(i, (i + k) % 4) for i in range(4)]) for k in (1, 2, 3)
     ]
-    part = (GROUP, TOK, HEAD_DIM)
+    shared[0], kv_half = lax.optimization_barrier((shared[0], kv_half))
+    kv_half_core = lax.ppermute(kv_half, "ctx", swap_core)
     dq, own, own_send, prev, prev_send = call(
         attention_kernel,
         [((GROUP, 64, HEAD_DIM), BF16)] + [(part, BF16)] * 4,
-        got, kv_core, kv_half, kv_half_core, mine, other, sums,
+        got, own_k, own_v, own_turned, kv_half, kv_half_core, mine, other, sums,
         scratch=[
-            vmem((2 * HALF, HEAD_DIM), BF16),
-            vmem((2 * HALF, HEAD_DIM), BF16),
-            vmem((N_TILES, HEAD_DIM, KEYS_TILE), BF16),
+            vmem(flat, BF16),
+            vmem(flat, BF16),
+            vmem(turned, BF16),
             vmem((N_TILES, KEYS_TILE, ROWS_TILE), F32),
             vmem((N_TILES, KEYS_TILE, ROWS_TILE), F32),
             vmem((N_TILES, 8, ROWS_TILE), F32),
             vmem((2 * HALF, HEAD_DIM), F32),
             vmem((2 * HALF, HEAD_DIM), F32),
         ],
-        flops=10_000_000_000, nbytes=6_000_000, vmem=40 << 20,
+        flops=10_000_000_000, nbytes=6_000_000, vmem=28 << 20,
     )
     f, dq = lax.optimization_barrier((f, dq))
     ghq, gf, back_send = call(
         backward_kernel,
-        [((TOK, CH), BF16), (sweep, F32), ((GROUP, ROWS_BACK, LANES), F32)],
+        [((TOK, CH), BF16), (sweep, F32), ((GROUP, ROWS_BACK, LANES), BF16)],
         doc_ids, sums, *shared, f, m, dec, hyena_q, hyena_grad, gain,
         smem=(0,), scratch=[vmem(params, F32), vmem(params, F32)],
         flops=40_000_000, nbytes=6_000_000,
@@ -608,14 +693,14 @@
     prev_home = lax.ppermute(prev_sum, "ctx", down_half)
     back = exchange(back_send)
     (half_mine,) = call(
-        half_adjoint_kernel, [((56, LANES), F32)], got, back, rate_part, other, specs=head_spec,
+        half_adjoint_kernel, [((56, LANES), F32)], mine, ends, back, rate_part, other,
         flops=1_000_000, nbytes=300_000,
     )
     half_other = lax.ppermute(half_mine, "ctx", swap_half)
     (last_send,) = call(
         last_pack_kernel, [((GROUP, ROWS_OUT, LANES), BF16)],
-        got, back, rate_part, other, half_mine, half_other, dq, own, own_got, prev_home,
-        specs=head_spec, flops=1_000_000, nbytes=3_000_000,
+        mine, back, rate_part, other, half_mine, half_other, dq, own, own_got, prev_home,
+        flops=1_000_000, nbytes=3_000_000,
     )
     last = exchange(last_send)
     ghk, ghv, gres, ggain, gaq, gak, gav = call(

time: 127 us -> 122 us (0.961)
  Pallas kernels: 33 us -> 29.7 us
  local copies, waits for them, and re-layouts: 2.46 us -> 0.06 us
  blocking collectives: 56.2 us -> 58.5 us
    all_to_all x1 -> x0, waiting for transfers between devices: 5.9 us -> none  [exchange(): lax.all_to_all(x, 'ctx', 0, 0, tiled=True, axis_index_groups=[early, late])]
    all_to_all x1 -> x0, starting transfers between devices: 5.87 us -> none  [exchange(): lax.all_to_all(x, 'ctx', 0, 0, tiled=True, axis_index_groups=[early, late])]
    pallas_call x9 -> x12, Pallas kernels: 33 us -> 29.7 us  [call(): pl.pallas_call(kernel, out_shape=shapes, grid=grid, in_specs=ins, out_spe...]
    ppermute x1, starting transfers between devices: 3.68 us -> 6.5 us  [body(): half_other = lax.ppermute(half_mine, 'ctx', swap_half)]
    ppermute x3, waiting for transfers between devices: 0.01 us -> 2.48 us  [body(): lax.ppermute(sums, 'chan', [(i, (i + k) % 4) for i in range(4)])]
    all_to_all x3, blocking collectives: 56.2 us -> 58.5 us  [exchange(): lax.all_to_all(x, 'ctx', 0, 0, tiled=True, axis_index_groups=[early, late])]
    unnamed x24 -> x22, local copies, waits for them, and re-layouts: 1.61 us -> 0.06 us
    ppermute x1, waiting for transfers between devices: 1.05 us -> 2.47 us  [body(): other = lax.ppermute(mine, 'ctx', swap_half)]
  transfers between devices with their start and end apart: 12 -> 12, of which waited for: 4 -> 5; matrix products, arithmetic and copies ran while one was open for 1% -> 0% of each run, Pallas kernels for 12% -> 10%
where the time goes in v3:
time: 122 us
  blocking collectives  58.5 us (48%)
  Pallas kernels  29.7 us (24%)
  starting transfers between devices  22.9 us (19%)
  waiting for transfers between devices  9.6 us (8%)
    all_to_all x3, blocking collectives, exchange(): lax.all_to_all(x, 'ctx', 0, 0, tiled=True, axis_index_groups=[early, late])  58.5 us
    pallas_call x12, Pallas kernels, call(): pl.pallas_call(kernel, out_shape=shapes, grid=grid, in_specs=ins, out_spe...  29.7 us
    ppermute x1, starting transfers between devices, body(): half_other = lax.ppermute(half_mine, 'ctx', swap_half)  6.5 us
    ppermute x3, starting transfers between devices, body(): lax.ppermute(sums, 'chan', [(i, (i + k) % 4) for i in range(4)])  4.97 us
    ppermute x1, starting transfers between devices, body(): kv_half = lax.ppermute(kv_later, 'ctx', up_half)  3.84 us
    ppermute x3, waiting for transfers between devices, body(): lax.ppermute(sums, 'chan', [(i, (i + k) % 4) for i in range(4)])  2.48 us
    ppermute x1, waiting for transfers between devices, body(): other = lax.ppermute(mine, 'ctx', swap_half)  2.47 us
  transfers between devices with their start and end apart: 12, of which 5 were waited for; matrix products, arithmetic and copies ran while one was open for 0% of the time, Pallas kernels for 10%

profile of v3, /device:TPU:1, one launch (start us, length us, event | category | flops | bytes accessed | tf_op | source)
XLA Modules:
  0.0 121.8 jit_solution(14273970978647622589)
XLA Ops:
  0.6 6.1 %shard_map.179 = (bf16[16,400,128]{2,1,0:T(8,128)(2,1)}, f32[2048,128]{1,0:T(8,128)}, f32[256,128]{1,0:T(8,128)}, f32[256,128]{1,0:T(8,128)}, f32[128,128]{1,0:T(8,128)}, /*index=5*/f32[16,128]{1,0:T(8,128)}) custom-call(s32[128]{0:T(128)} %docs.7, s32[1,128]{1,0:T(1,128)} %bitcast.5, f32[16,2048]{1,0:T(8,128)} %rate_hbm.1, f32[16,2048]{1,0:T(8,128)} %res_hbm.1, ...), custom_call_target="tpu_custom_call" | custom-call | flops 40000000 | bytes 6000000 | tf_op jit(solution)/shard_map/pallas_call | solution.py:51
  6.8 0.0 copy-start.7
  6.8 29.5 %all_to_all.15.got = bf16[16,400,128]{2,1,0:T(8,128)(2,1)S(1)} all-to-all(bf16[16,400,128]{2,1,0:T(8,128)(2,1)} %get-tuple-element.46), channel_id=1, replica_groups={{0,4,8,12,16,20,24,28,32,36,40,44,48,52,56,60},{96,100,104,108,112,116,..., dimensions={0} | all-to-all | bytes 3276800 | tf_op jit(solution)/shard_map/all_to_all | solution.py:612
  36.3 0.6 shard_map.180
  36.8 0.0 copy-start.1
  36.9 2.0 %collective-permute-start = (f32[144,128]{1,0:T(8,128)S(1)}, f32[144,128]{1,0:T(8,128)S(1)}, u32[]{:S(2)}, u32[]{:S(2)}) collective-permute-start(f32[144,128]{1,0:T(8,128)S(1)} %get-tuple-element.49.mine.ids_mine.docs_mine), channel_id=1, source_target_pairs={{0,96},{4,100},{8,104},{12,108},{16,112},{20,116},{24,120},{28,124... | collective-permute-start | bytes 221192 | tf_op jit(solution)/shard_map/ppermute | solution.py:637
  38.9 2.5 %collective-permute-done.other.after.ids_other.docs_other = f32[144,128]{1,0:T(8,128)S(1)} collective-permute-done((f32[144,128]{1,0:T(8,128)S(1)}, f32[144,128]{1,0:T(8,128)S(1)}, u32[]{:S(2)}, u32[]{:S(2)}) %collective-permute-start) | collective-permute-done | bytes 73760 | tf_op jit(solution)/shard_map/ppermute | solution.py:637
  41.4 3.8 %collective-permute-start.3 = (bf16[16,128,128]{2,1,0:T(8,128)(2,1)S(1)}, bf16[16,128,128]{2,1,0:T(8,128)(2,1)S(1)}, u32[]{:S(2)}, u32[]{:S(2)}) collective-permute-start(bf16[16,128,128]{2,1,0:T(8,128)(2,1)S(1)} %shard_map.184), channel_id=1, source_target_pairs={{0,96},{4,100},{8,104},{12,108},{16,112},{20,116},{24,120},{28,124... | collective-permute-start | bytes 1572872 | tf_op jit(solution)/shard_map/ppermute | solution.py:644
  45.3 0.2 shard_map.181
  45.5 1.9 %collective-permute-start.1 = (f32[128,128]{1,0:T(8,128)S(1)}, f32[128,128]{1,0:T(8,128)S(1)}, u32[]{:S(2)}, u32[]{:S(2)}) collective-permute-start(f32[128,128]{1,0:T(8,128)S(1)} %get-tuple-element.51), channel_id=1, source_target_pairs={{0,4},{4,0},{8,12},{12,8},{16,20},{20,16},{24,28},{28,24},{32,36},... | collective-permute-start | bytes 196616 | tf_op jit(solution)/shard_map/ppermute | solution.py:654
  47.4 0.9 collective-permute-done.1.got
  48.3 3.7 %shard_map.182 = (f32[2048,128]{1,0:T(8,128)S(1)}, f32[8,128]{1,0:T(8,128)S(1)}) custom-call(s32[128]{0:T(128)S(1)} %copy-done.10, f32[128,128]{1,0:T(8,128)S(1)} %get-tuple-element.50.keep, f32[128,128]{1,0:T(8,128)S(1)} %collective-permute-done.1.got, f32[2048,128]{1,0:T(8,128)S(1)} %copy-done, f32[256,128]{1,0:T(8,128)S(1)} %copy-done.5, ...), custom_call_target="tpu_custom_call" | custom-call | flops 40000000 | bytes 6000000 | tf_op jit(solution)/shard_map/pallas_call | solution.py:51
  52.1 1.7 %collective-permute-start.2 = (f32[8,128]{1,0:T(8,128)S(1)}, f32[8,128]{1,0:T(8,128)S(1)}, u32[]{:S(2)}, u32[]{:S(2)}) collective-permute-start(f32[8,128]{1,0:T(8,128)S(1)} %get-tuple-element.55.after.s0), channel_id=1, source_target_pairs={{0,1},{1,2},{2,3},{3,0},{4,5},{5,6},{6,7},{7,4},{8,9},{9,10},{10,1... | collective-permute-start | bytes 12296 | tf_op jit(solution)/shard_map/ppermute | solution.py:661
  53.8 0.6 collective-permute-start.6
  54.4 2.5 %collective-permute-done.2.s1 = f32[8,128]{1,0:T(8,128)S(1)} collective-permute-done((f32[8,128]{1,0:T(8,128)S(1)}, f32[8,128]{1,0:T(8,128)S(1)}, u32[]{:S(2)}, u32[]{:S(2)}) %collective-permute-start.2) | collective-permute-done | bytes 4128 | tf_op jit(solution)/shard_map/ppermute | solution.py:661
  56.9 1.2 %collective-permute-start.7 = (bf16[16,128,128]{2,1,0:T(8,128)(2,1)S(1)}, bf16[16,128,128]{2,1,0:T(8,128)(2,1)S(1)}, u32[]{:S(2)}, u32[]{:S(2)}) collective-permute-start(bf16[16,128,128]{2,1,0:T(8,128)(2,1)S(1)} %collective-permute-done.3.kv_half), channel_id=1, source_target_pairs={{0,4},{4,0},{8,12},{12,8},{16,20},{20,16},{24,28},{28,24},{32,36},... | collective-permute-start | bytes 1572872 | tf_op jit(solution)/shard_map/ppermute | solution.py:664
  58.1 2.8 %collective-permute-start.4 = (f32[8,128]{1,0:T(8,128)S(1)}, f32[8,128]{1,0:T(8,128)S(1)}, u32[]{:S(2)}, u32[]{:S(2)}) collective-permute-start(f32[8,128]{1,0:T(8,128)S(1)} %get-tuple-element.55.after.s0), channel_id=1, source_target_pairs={{0,2},{1,3},{2,0},{3,1},{4,6},{5,7},{6,4},{7,5},{8,10},{9,11},{10,... | collective-permute-start | bytes 12296 | tf_op jit(solution)/shard_map/ppermute | solution.py:661
  61.0 0.4 collective-permute-start.5
  61.4 0.5 shard_map.185
  61.9 7.0 %shard_map.186 = (bf16[16,64,128]{2,1,0:T(8,128)(2,1)S(1)}, bf16[16,128,128]{2,1,0:T(8,128)(2,1)S(1)}, bf16[16,128,128]{2,1,0:T(8,128)(2,1)S(1)}, bf16[16,128,12...) custom-call(bf16[16,400,128]{2,1,0:T(8,128)(2,1)S(1)} %all_to_all.15.got, bf16[2048,128]{1,0:T(8,128)(2,1)S(1)} %get-tuple-element.58.own_k, ...), custom_call_target="tpu_custom_call" | custom-call | flops 10000000000 | bytes 6000000 | tf_op jit(solution)/shard_map/pallas_call | solution.py:51
  69.0 5.8 %shard_map.187 = (bf16[128,2048]{1,0:T(8,128)(2,1)}, f32[2048,128]{1,0:T(8,128)S(1)}, bf16[16,64,128]{2,1,0:T(8,128)(2,1)S(1)}) custom-call(s32[128]{0:T(128)S(1)} %copy-done.10, f32[8,128]{1,0:T(8,128)S(1)} %get-tuple-element.55.after.s0, f32[8,128]{1,0:T(8,128)S(1)} %collective-permute-done.2.s1, f32[8,128]{1,0:T(8,128)S(1)} %collective-permute-done.4.s2, ...), custom_call_target="tpu_custom_call" | custom-call | flops 40000000 | bytes 6000000 | tf_op jit(solution)/shard_map/pallas_call | solution.py:51
  74.7 0.6 collective-permute-start.10
  75.3 1.5 %collective-permute-done.10 = bf16[16,128,128]{2,1,0:T(8,128)(2,1)S(1)} collective-permute-done((bf16[16,128,128]{2,1,0:T(8,128)(2,1)S(1)}, bf16[16,128,128]{2,1,0:T(8,128)(2,1)S(1)}, u32[]{:S(2)}, u32[]{:S(2)}) %collective-permute-start.10) | collective-permute-done | bytes 524320 | tf_op jit(solution)/shard_map/ppermute | solution.py:690
  76.8 0.1 add_convert_fusion
  77.0 1.3 %collective-permute-start.11 = (bf16[16,128,128]{2,1,0:T(8,128)(2,1)S(1)}, bf16[16,128,128]{2,1,0:T(8,128)(2,1)S(1)}, u32[]{:S(2)}, u32[]{:S(2)}) collective-permute-start(bf16[16,128,128]{2,1,0:T(8,128)(2,1)S(1)} %add_convert_fusion), channel_id=1, source_target_pairs={{96,0},{100,4},{104,8},{108,12},{112,16},{116,20},{120,24},{124,28... | collective-permute-start | bytes 1572872 | tf_op jit(solution)/shard_map/ppermute | solution.py:693
  78.3 10.0 %all_to_all.16.back = bf16[16,64,128]{2,1,0:T(8,128)(2,1)S(1)} all-to-all(bf16[16,64,128]{2,1,0:T(8,128)(2,1)S(1)} %get-tuple-element.68), channel_id=1, replica_groups={{0,4,8,12,16,20,24,28,32,36,40,44,48,52,56,60},{96,100,104,108,112,116,..., dimensions={0} | all-to-all | bytes 524288 | tf_op jit(solution)/shard_map/all_to_all | solution.py:612
  88.3 0.2 shard_map.188.mine
  88.6 6.5 %collective-permute-start.8 = (f32[56,128]{1,0:T(8,128)S(1)}, f32[56,128]{1,0:T(8,128)S(1)}, u32[]{:S(2)}, u32[]{:S(2)}) collective-permute-start(f32[56,128]{1,0:T(8,128)S(1)} %shard_map.188.mine), channel_id=1, source_target_pairs={{0,96},{4,100},{8,104},{12,108},{16,112},{20,116},{24,120},{28,124... | collective-permute-start | bytes 86024 | tf_op jit(solution)/shard_map/ppermute | solution.py:699
  95.1 2.2 %collective-permute-done.8.theirs = f32[56,128]{1,0:T(8,128)S(1)} collective-permute-done((f32[56,128]{1,0:T(8,128)S(1)}, f32[56,128]{1,0:T(8,128)S(1)}, u32[]{:S(2)}, u32[]{:S(2)}) %collective-permute-start.8) | collective-permute-done | bytes 28704 | tf_op jit(solution)/shard_map/ppermute | solution.py:699
  97.3 0.4 shard_map.189
  97.7 19.1 %all_to_all.17.got = bf16[16,256,128]{2,1,0:T(8,128)(2,1)S(1)} all-to-all(bf16[16,256,128]{2,1,0:T(8,128)(2,1)S(1)} %shard_map.189), channel_id=1, replica_groups={{0,4,8,12,16,20,24,28,32,36,40,44,48,52,56,60},{96,100,104,108,112,116,..., dimensions={0} | all-to-all | bytes 2097152 | tf_op jit(solution)/shard_map/all_to_all | solution.py:612
  116.7 5.1 %shard_map.190 = (bf16[128,2048]{1,0:T(8,128)(2,1)}, bf16[128,2048]{1,0:T(8,128)(2,1)}, f32[16,2048]{1,0:T(8,128)}, f32[1,2048]{1,0:T(1,128)}, bf16[128,1024]{1,...) custom-call(s32[128]{0:T(128)S(1)} %copy-done.10, bf16[16,256,128]{2,1,0:T(8,128)(2,1)S(1)} %all_to_all.17.got, ...), custom_call_target="tpu_custom_call" | custom-call | flops 40000000 | bytes 6000000 | tf_op jit(solution)/shard_map/pallas_call | solution.py:51
  (30 shorter events, 0.1 us)
Async XLA Ops:
  6.8 29.5 %copy-start.7 = (f32[128,128]{1,0:T(8,128)S(1)}, f32[128,128]{1,0:T(8,128)}, u32[]{:S(2)}) copy-start(f32[128,128]{1,0:T(8,128)} %get-tuple-element.47.through) | copy-start | bytes 196612
  36.8 11.5 %copy-start = (f32[2048,128]{1,0:T(8,128)S(1)}, f32[2048,128]{1,0:T(8,128)}, u32[]{:S(2)}) copy-start(f32[2048,128]{1,0:T(8,128)} %get-tuple-element.52.m) | copy-start | bytes 3145732
  36.8 11.5 %copy-start.1 = (bf16[128,2048]{1,0:T(8,128)(2,1)S(1)}, bf16[128,2048]{1,0:T(8,128)(2,1)}, u32[]{:S(2)}) copy-start(bf16[128,2048]{1,0:T(8,128)(2,1)} %hq.3) | copy-start | bytes 1572868
  36.8 11.5 %copy-start.2 = (bf16[128,2048]{1,0:T(8,128)(2,1)S(1)}, bf16[128,2048]{1,0:T(8,128)(2,1)}, u32[]{:S(2)}) copy-start(bf16[128,2048]{1,0:T(8,128)(2,1)} %hg.3) | copy-start | bytes 1572868
  36.9 11.4 %copy-start.5 = (f32[256,128]{1,0:T(8,128)S(1)}, f32[256,128]{1,0:T(8,128)}, u32[]{:S(2)}) copy-start(f32[256,128]{1,0:T(8,128)} %get-tuple-element.53.dec) | copy-start | bytes 393220
  36.9 11.4 %copy-start.6 = (f32[256,128]{1,0:T(8,128)S(1)}, f32[256,128]{1,0:T(8,128)}, u32[]{:S(2)}) copy-start(f32[256,128]{1,0:T(8,128)} %get-tuple-element.54.wgt) | copy-start | bytes 393220
  36.9 11.4 %copy-start.8 = (f32[2048]{0:T(1024)S(1)}, f32[2048]{0:T(1024)}, u32[]{:S(2)}) copy-start(f32[2048]{0:T(1024)} %param.18) | copy-start | bytes 24580
  36.9 11.4 %copy-start.10 = (s32[128]{0:T(128)S(1)}, s32[128]{0:T(128)}, u32[]{:S(2)}) copy-start(s32[128]{0:T(128)} %docs.7) | copy-start | bytes 1540
  36.9 4.5 %collective-permute-start = (f32[144,128]{1,0:T(8,128)S(1)}, f32[144,128]{1,0:T(8,128)S(1)}, u32[]{:S(2)}, u32[]{:S(2)}) collective-permute-start(f32[144,128]{1,0:T(8,128)S(1)} %get-tuple-element.49.mine.ids_mine.docs_mine), channel_id=1, source_target_pairs={{0,96},{4,100},{8,104},{12,108},{16,112},{20,116},{24,120},{28,124... | collective-permute-start | bytes 221192 | tf_op jit(solution)/shard_map/ppermute | solution.py:637
  41.4 15.5 %collective-permute-start.3 = (bf16[16,128,128]{2,1,0:T(8,128)(2,1)S(1)}, bf16[16,128,128]{2,1,0:T(8,128)(2,1)S(1)}, u32[]{:S(2)}, u32[]{:S(2)}) collective-permute-start(bf16[16,128,128]{2,1,0:T(8,128)(2,1)S(1)} %shard_map.184), channel_id=1, source_target_pairs={{0,96},{4,100},{8,104},{12,108},{16,112},{20,116},{24,120},{28,124... | collective-permute-start | bytes 1572872 | tf_op jit(solution)/shard_map/ppermute | solution.py:644
  45.5 2.8 %collective-permute-start.1 = (f32[128,128]{1,0:T(8,128)S(1)}, f32[128,128]{1,0:T(8,128)S(1)}, u32[]{:S(2)}, u32[]{:S(2)}) collective-permute-start(f32[128,128]{1,0:T(8,128)S(1)} %get-tuple-element.51), channel_id=1, source_target_pairs={{0,4},{4,0},{8,12},{12,8},{16,20},{20,16},{24,28},{28,24},{32,36},... | collective-permute-start | bytes 196616 | tf_op jit(solution)/shard_map/ppermute | solution.py:654
  52.1 4.8 %collective-permute-start.2 = (f32[8,128]{1,0:T(8,128)S(1)}, f32[8,128]{1,0:T(8,128)S(1)}, u32[]{:S(2)}, u32[]{:S(2)}) collective-permute-start(f32[8,128]{1,0:T(8,128)S(1)} %get-tuple-element.55.after.s0), channel_id=1, source_target_pairs={{0,1},{1,2},{2,3},{3,0},{4,5},{5,6},{6,7},{7,4},{8,9},{9,10},{10,1... | collective-permute-start | bytes 12296 | tf_op jit(solution)/shard_map/ppermute | solution.py:661
  53.8 7.6 %collective-permute-start.6 = (bf16[16,128,128]{2,1,0:T(8,128)(2,1)S(1)}, bf16[16,128,128]{2,1,0:T(8,128)(2,1)S(1)}, u32[]{:S(2)}, u32[]{:S(2)}) collective-permute-start(bf16[16,128,128]{2,1,0:T(8,128)(2,1)S(1)} %shard_map.183.kv), channel_id=1, source_target_pairs={{0,4},{4,0},{8,12},{12,8},{16,20},{20,16},{24,28},{28,24},{32,36},... | collective-permute-start | bytes 1572872 | tf_op jit(solution)/shard_map/ppermute | solution.py:640
  56.9 5.0 %collective-permute-start.7 = (bf16[16,128,128]{2,1,0:T(8,128)(2,1)S(1)}, bf16[16,128,128]{2,1,0:T(8,128)(2,1)S(1)}, u32[]{:S(2)}, u32[]{:S(2)}) collective-permute-start(bf16[16,128,128]{2,1,0:T(8,128)(2,1)S(1)} %collective-permute-done.3.kv_half), channel_id=1, source_target_pairs={{0,4},{4,0},{8,12},{12,8},{16,20},{20,16},{24,28},{28,24},{32,36},... | collective-permute-start | bytes 1572872 | tf_op jit(solution)/shard_map/ppermute | solution.py:664
  58.1 10.8 %collective-permute-start.4 = (f32[8,128]{1,0:T(8,128)S(1)}, f32[8,128]{1,0:T(8,128)S(1)}, u32[]{:S(2)}, u32[]{:S(2)}) collective-permute-start(f32[8,128]{1,0:T(8,128)S(1)} %get-tuple-element.55.after.s0), channel_id=1, source_target_pairs={{0,2},{1,3},{2,0},{3,1},{4,6},{5,7},{6,4},{7,5},{8,10},{9,11},{10,... | collective-permute-start | bytes 12296 | tf_op jit(solution)/shard_map/ppermute | solution.py:661
  61.0 8.0 %collective-permute-start.5 = (f32[8,128]{1,0:T(8,128)S(1)}, f32[8,128]{1,0:T(8,128)S(1)}, u32[]{:S(2)}, u32[]{:S(2)}) collective-permute-start(f32[8,128]{1,0:T(8,128)S(1)} %get-tuple-element.55.after.s0), channel_id=1, source_target_pairs={{0,3},{1,0},{2,1},{3,2},{4,7},{5,4},{6,5},{7,6},{8,11},{9,8},{10,9... | collective-permute-start | bytes 12296 | tf_op jit(solution)/shard_map/ppermute | solution.py:661
  74.7 13.6 %copy-start.9 = (f32[16,128]{1,0:T(8,128)S(1)}, f32[16,128]{1,0:T(8,128)}, u32[]{:S(2)}) copy-start(f32[16,128]{1,0:T(8,128)} %get-tuple-element.69.rate) | copy-start | bytes 24580
  74.7 2.1 %collective-permute-start.10 = (bf16[16,128,128]{2,1,0:T(8,128)(2,1)S(1)}, bf16[16,128,128]{2,1,0:T(8,128)(2,1)S(1)}, u32[]{:S(2)}, u32[]{:S(2)}) collective-permute-start(bf16[16,128,128]{2,1,0:T(8,128)(2,1)S(1)} %get-tuple-element.75), channel_id=1, source_target_pairs={{0,4},{4,0},{8,12},{12,8},{16,20},{20,16},{24,28},{28,24},{32,36},... | collective-permute-start | bytes 1572872 | tf_op jit(solution)/shard_map/ppermute | solution.py:690
  75.3 22.0 %collective-permute-start.9 = (bf16[16,128,128]{2,1,0:T(8,128)(2,1)S(1)}, bf16[16,128,128]{2,1,0:T(8,128)(2,1)S(1)}, u32[]{:S(2)}, u32[]{:S(2)}) collective-permute-start(bf16[16,128,128]{2,1,0:T(8,128)(2,1)S(1)} %get-tuple-element.73), channel_id=1, source_target_pairs={{0,4},{4,0},{8,12},{12,8},{16,20},{20,16},{24,28},{28,24},{32,36},... | collective-permute-start | bytes 1572872 | tf_op jit(solution)/shard_map/ppermute | solution.py:691
  77.0 20.3 %collective-permute-start.11 = (bf16[16,128,128]{2,1,0:T(8,128)(2,1)S(1)}, bf16[16,128,128]{2,1,0:T(8,128)(2,1)S(1)}, u32[]{:S(2)}, u32[]{:S(2)}) collective-permute-start(bf16[16,128,128]{2,1,0:T(8,128)(2,1)S(1)} %add_convert_fusion), channel_id=1, source_target_pairs={{96,0},{100,4},{104,8},{108,12},{112,16},{116,20},{120,24},{124,28... | collective-permute-start | bytes 1572872 | tf_op jit(solution)/shard_map/ppermute | solution.py:693
  88.6 8.7 %collective-permute-start.8 = (f32[56,128]{1,0:T(8,128)S(1)}, f32[56,128]{1,0:T(8,128)S(1)}, u32[]{:S(2)}, u32[]{:S(2)}) collective-permute-start(f32[56,128]{1,0:T(8,128)S(1)} %shard_map.188.mine), channel_id=1, source_target_pairs={{0,96},{4,100},{8,104},{12,108},{16,112},{20,116},{24,120},{28,124... | collective-permute-start | bytes 86024 | tf_op jit(solution)/shard_map/ppermute | solution.py:699
  97.7 19.1 %copy-start.3 = (bf16[128,2048]{1,0:T(8,128)(2,1)S(1)}, bf16[128,2048]{1,0:T(8,128)(2,1)}, u32[]{:S(2)}) copy-start(bf16[128,2048]{1,0:T(8,128)(2,1)} %hk.1) | copy-start | bytes 1572868
  97.7 19.1 %copy-start.4 = (bf16[128,2048]{1,0:T(8,128)(2,1)S(1)}, bf16[128,2048]{1,0:T(8,128)(2,1)}, u32[]{:S(2)}) copy-start(bf16[128,2048]{1,0:T(8,128)(2,1)} %hv.1) | copy-start | bytes 1572868

commit v4 on v3

--- a/solution.py
+++ b/solution.py
@@ -19,7 +19,7 @@
 CHUNKS = CH // LANES
 GROUP = 16
 HALF = GROUP * TOK
-SPAN = 8
+SPAN = 32
 SCALE = HEAD_DIM ** (-0.5)
 LOG2E = 1.4426950408889634
 
@@ -33,6 +33,8 @@
 KEYS_TILE = 512
 N_TILES = 2 * HALF // KEYS_TILE
 HALF_TILES = N_TILES // 2
+CHUNK = 256
+STEP = 256
 Q_TILES = 4
 
 F32 = jnp.float32
@@ -144,7 +146,8 @@
 
 def first_kernel(
     docs, doc_row, rate_hbm, res_hbm, hk_hbm, hv_hbm, ak_hbm, av_hbm, aq_hbm, ag_hbm,
-    send, m, dec, wgt, through, rate_part, thr_all, rate, res, hk, hv, ak, av, aq, ag, sems,
+    send, m_out, dec, wgt, through, rate_part,
+    thr_all, rate, res, hk, hv, ak, av, aq, ag, m, sems,
 ):
     pairs = (
         (rate_hbm, rate), (res_hbm, res), (hk_hbm, hk), (hv_hbm, hv),
@@ -179,6 +182,8 @@
     copies[3].wait()
     for j in range(CHUNKS):
         m[every(j, TOK), :] = hk[:, lanes(j)].astype(F32) * hv[:, lanes(j)].astype(F32)
+    leaving = pltpu.make_async_copy(m, m_out, sems.at[8])
+    leaving.start()
     for g in range(2):
         kept = [dec[n * 16 + 8 * g : n * 16 + 8 * g + 8, :] for n in range(POLES)]
 
@@ -196,6 +201,7 @@
         for p in range(GROUP):
             part = slice(64 * (p % 2), 64 * (p % 2) + 64)
             send[p, row : row + 64, :] = ref[part, lanes(p // 2)]
+    leaving.wait()
 
 
 def is_late():
@@ -319,8 +325,8 @@
     sums[2:8, :] = jnp.zeros((6, LANES), F32)
 
 
-def backward_kernel(docs, s0, s1, s2, s3, f, m, dec, hq, hg, gain, ghq, gf, send, starts, totals):
-    total = s0[...] + s1[...] + s2[...] + s3[...]
+def backward_kernel(docs, sums, after, f, m, dec, hq, hg, gain, ghq, gf, send, starts, totals):
+    total = sums[...]
     inv = lax.rsqrt(total[0:1, :] / D + EPSILON)
     slope = inv * inv * inv * total[1:2, :] / D
     inv = jnp.broadcast_to(inv, (TOK, LANES)).T
@@ -464,8 +470,15 @@
     lax.fori_loop(0, HALF_TILES, one, 0)
 
 
-def own_keys_kernel(kv, kv_core, keys, values, turned):
+def own_keys_kernel(got, kv, kv_core, keys, values, turned, rows_q, rows_g, turned_q, turned_g):
     core = core_of()
+    for i in range(Q_TILES):
+        for u in range(4):
+            part = slice(64 * u, 64 * u + 64)
+            rows_q[i, part, :] = got[block_at(4 * i + u), ROW_Q:ROW_G, :]
+            rows_g[i, part, :] = got[block_at(4 * i + u), ROW_G:ROWS_IN, :]
+        turned_q[i] = rows_q[i].astype(F32).T.astype(BF16)
+        turned_g[i] = rows_g[i].astype(F32).T.astype(BF16)
     for b in range(GROUP):
         s = block_at(b)
         place(keys, values, b, core, kv[s, 0:64, :], kv[s, 64:128, :])
@@ -473,17 +486,23 @@
     turn_keys(keys, turned)
 
 
+def sums_kernel(s0, s1, s2, s3, total):
+    total[...] = s0[...] + s1[...] + s2[...] + s3[...]
+
+
 def send_keys_kernel(kv, after, out):
     out[...] = kv[...]
 
 
 def attention_kernel(
-    got, own_k, own_v, own_turned, kv_half, kv_half_core, ids_mine, ids_other, after,
-    dq, own, own_send, prev, prev_send,
+    all_q, all_g, all_turned_q, all_turned_g, own_k, own_v, own_turned, kv_half, kv_half_core,
+    ids_mine, ids_other, after,
+    dq, own, own_send, prev, prev_send, token,
     prev_k, prev_v, prev_turned, scores, products, peaks, dk, dv,
 ):
     core = core_of()
     late = is_late()
+    token[...] = jnp.zeros((8, LANES), F32)
 
     @pl.when(late)
     def _():
@@ -517,34 +536,36 @@
         return result
 
     def query_tile(i, _):
-        rows_q = jnp.concatenate([got[block_at(4 * i + u), ROW_Q:ROW_G, :] for u in range(4)], axis=0)
-        rows_g = jnp.concatenate([got[block_at(4 * i + u), ROW_G:ROWS_IN, :] for u in range(4)], axis=0)
-        turned_q = rows_q.astype(F32).T.astype(BF16)
-        turned_g = rows_g.astype(F32).T.astype(BF16)
+        rows_q, rows_g = all_q[i], all_g[i]
+        turned_q, turned_g = all_turned_q[i], all_turned_g[i]
         lane = lax.broadcasted_iota(jnp.int32, (1, ROWS_TILE), 1)
         qpos = HALF + 512 * i + 128 * (lane // 64) + 64 * core + lax.rem(lane, 64)
         qstart = start_of(qpos)
         low = start_of(HALF + 512 * i + 64 * core) // KEYS_TILE
         high = HALF // KEYS_TILE + i + 1
-        row = lax.broadcasted_iota(jnp.int32, (KEYS_TILE, ROWS_TILE), 0)
+        row = lax.broadcasted_iota(jnp.int32, (CHUNK, ROWS_TILE), 0)
 
         def fold(value, by):
-            return by(value.reshape(KEYS_TILE // 8, 8, ROWS_TILE), axis=0)
+            return by(value.reshape(CHUNK // 8, 8, ROWS_TILE), axis=0)
 
         def first_pass(keys, values, base, t, carry):
             peak, total, weighted = carry
-            at = pl.ds(pl.multiple_of((t - base) * KEYS_TILE, KEYS_TILE), KEYS_TILE)
-            s = jnp.dot(keys[at, :], turned_q, preferred_element_type=F32)
-            gp = jnp.dot(values[at, :], turned_g, preferred_element_type=F32)
-            first = t * KEYS_TILE
-            s = jnp.where((row <= qpos - first) & (row >= qstart - first), s, FLOOR_SCORE)
-            top = jnp.maximum(peak, jnp.max(fold(s, jnp.max), axis=0, keepdims=True))
-            p = jnp.exp2((s - top) * (SCALE * LOG2E))
-            scores[t] = p
-            products[t] = gp
-            peaks[t] = jnp.broadcast_to(top, (8, ROWS_TILE))
-            shrink = jnp.exp2((peak - top) * (SCALE * LOG2E))
-            return top, total * shrink + fold(p, jnp.sum), weighted * shrink + fold(p * gp, jnp.sum)
+            for u in range(KEYS_TILE // CHUNK):
+                first = t * KEYS_TILE + u * CHUNK
+                at = pl.ds(pl.multiple_of(first - base * KEYS_TILE, CHUNK), CHUNK)
+                s = jnp.dot(keys[at, :], turned_q, preferred_element_type=F32)
+                gp = jnp.dot(values[at, :], turned_g, preferred_element_type=F32)
+                s = jnp.where((row <= qpos - first) & (row >= qstart - first), s, FLOOR_SCORE)
+                top = jnp.maximum(peak, jnp.max(fold(s, jnp.max), axis=0, keepdims=True))
+                p = jnp.exp2((s - top) * (SCALE * LOG2E))
+                scores[t, u * CHUNK : u * CHUNK + CHUNK, :] = p
+                products[t, u * CHUNK : u * CHUNK + CHUNK, :] = gp
+                peaks[t, u : u + 1, :] = top
+                shrink = jnp.exp2((peak - top) * (SCALE * LOG2E))
+                total = total * shrink + fold(p, jnp.sum)
+                weighted = weighted * shrink + fold(p * gp, jnp.sum)
+                peak = top
+            return peak, total, weighted
 
         zero = jnp.zeros((8, ROWS_TILE), F32)
         floor = jnp.full((1, ROWS_TILE), FLOOR_SCORE, F32)
@@ -557,12 +578,21 @@
         centre = jnp.sum(weighted, axis=0, keepdims=True) * inv
 
         def second_pass(turned, base, t, turned_dq):
-            at = pl.ds(pl.multiple_of(t * KEYS_TILE, KEYS_TILE), KEYS_TILE)
-            p = scores[t] * (jnp.exp2((peaks[t][0:1] - peak) * (SCALE * LOG2E)) * inv)
-            ds = (p * (products[t] - centre)).astype(BF16)
-            dk[at, :] += jnp.dot(ds, rows_q, preferred_element_type=F32)
-            dv[at, :] += jnp.dot(p.astype(BF16), rows_g, preferred_element_type=F32)
-            return turned_dq + jnp.dot(turned[t - base], ds, preferred_element_type=F32)
+            for v in range(KEYS_TILE // STEP):
+                parts = []
+                for u in range(v * STEP // CHUNK, (v + 1) * STEP // CHUNK):
+                    rows = slice(u * CHUNK, u * CHUNK + CHUNK)
+                    fall = jnp.exp2((peaks[t, u : u + 1, :] - peak) * (SCALE * LOG2E)) * inv
+                    p = scores[t, rows, :] * fall
+                    parts.append((p.astype(BF16), (p * (products[t, rows, :] - centre)).astype(BF16)))
+                p = jnp.concatenate([one for one, _ in parts], axis=0)
+                ds = jnp.concatenate([one for _, one in parts], axis=0)
+                at = pl.ds(pl.multiple_of(t * KEYS_TILE + v * STEP, STEP), STEP)
+                dk[at, :] += jnp.dot(ds, rows_q, preferred_element_type=F32)
+                dv[at, :] += jnp.dot(p, rows_g, preferred_element_type=F32)
+                part = turned[t - base, :, v * STEP : v * STEP + STEP]
+                turned_dq = turned_dq + jnp.dot(part, ds, preferred_element_type=F32)
+            return turned_dq
 
         zero = jnp.zeros((HEAD_DIM, ROWS_TILE), F32)
         ahead = functools.partial(second_pass, prev_turned, 0)
@@ -622,9 +652,9 @@
         + [(half_shape, F32), ((POLES, LANES), F32)],
         doc_ids, doc_ids.reshape(1, TOK), pole_rate, residue, hyena_k, hyena_v,
         attn_k, attn_v, attn_q, attn_grad,
-        smem=(0,), specs={i: hbm for i in range(2, 10)},
+        smem=(0,), specs={i: hbm for i in range(2, 10)}, far=(1,),
         scratch=[vmem(params, F32)] + [vmem((POLES, CH), F32)] * 2 + [vmem((TOK, CH), BF16)] * 2
-        + [vmem((TOK, 1024), BF16)] * 4 + [pltpu.SemaphoreType.DMA((8,))],
+        + [vmem((TOK, 1024), BF16)] * 4 + [vmem(sweep, F32), pltpu.SemaphoreType.DMA((9,))],
         flops=40_000_000, nbytes=6_000_000, vmem=60 << 20,
     )
     got = exchange(send)
@@ -644,8 +674,11 @@
     kv_half = lax.ppermute(kv_later, "ctx", up_half)
     flat = (HALF, HEAD_DIM)
     turned = (HALF_TILES, HEAD_DIM, KEYS_TILE)
-    own_k, own_v, own_turned = call(
-        own_keys_kernel, [(flat, BF16), (flat, BF16), (turned, BF16)], kv, kv_core,
+    tall, wide = (Q_TILES, ROWS_TILE, HEAD_DIM), (Q_TILES, HEAD_DIM, ROWS_TILE)
+    own_k, own_v, own_turned, *query_parts = call(
+        own_keys_kernel,
+        [(flat, BF16), (flat, BF16), (turned, BF16)] + [(tall, BF16)] * 2 + [(wide, BF16)] * 2,
+        got, kv, kv_core,
         flops=1_000_000, nbytes=4_000_000,
     )
     carry, carry_send = call(
@@ -660,12 +693,17 @@
     shared = [
         lax.ppermute(sums, "chan", [(i, (i + k) % 4) for i in range(4)]) for k in (1, 2, 3)
     ]
-    shared[0], kv_half = lax.optimization_barrier((shared[0], kv_half))
+    (sums,) = call(
+        sums_kernel, [((8, LANES), F32)], sums, *shared, flops=1000, nbytes=10_000
+    )
+    (kv_half,) = call(
+        send_keys_kernel, [(part, BF16)], kv_half, sums, flops=1000, nbytes=1_000_000
+    )
     kv_half_core = lax.ppermute(kv_half, "ctx", swap_core)
-    dq, own, own_send, prev, prev_send = call(
+    dq, own, own_send, prev, prev_send, after = call(
         attention_kernel,
-        [((GROUP, 64, HEAD_DIM), BF16)] + [(part, BF16)] * 4,
-        got, own_k, own_v, own_turned, kv_half, kv_half_core, mine, other, sums,
+        [((GROUP, 64, HEAD_DIM), BF16)] + [(part, BF16)] * 4 + [((8, LANES), F32)],
+        *query_parts, own_k, own_v, own_turned, kv_half, kv_half_core, mine, other, sums,
         scratch=[
             vmem(flat, BF16),
             vmem(flat, BF16),
@@ -678,17 +716,16 @@
         ],
         flops=10_000_000_000, nbytes=6_000_000, vmem=28 << 20,
     )
-    f, dq = lax.optimization_barrier((f, dq))
     ghq, gf, back_send = call(
         backward_kernel,
         [((TOK, CH), BF16), (sweep, F32), ((GROUP, ROWS_BACK, LANES), BF16)],
-        doc_ids, sums, *shared, f, m, dec, hyena_q, hyena_grad, gain,
+        doc_ids, sums, after, f, m, dec, hyena_q, hyena_grad, gain,
         smem=(0,), scratch=[vmem(params, F32), vmem(params, F32)],
         flops=40_000_000, nbytes=6_000_000,
     )
-    back_send, own_send, prev_send = lax.optimization_barrier((back_send, own_send, prev_send))
     prev_got = lax.ppermute(prev_send, "ctx", swap_core)
     own_got = lax.ppermute(own_send, "ctx", swap_core)
+    back_send, prev_got = lax.optimization_barrier((back_send, prev_got))
     prev_sum = (prev.astype(F32) + prev_got.astype(F32)).astype(BF16)
     prev_home = lax.ppermute(prev_sum, "ctx", down_half)
     back = exchange(back_send)

time: 122 us -> 119 us (0.975)
  starting transfers between devices: 22.9 us -> 21 us
  waiting for transfers between devices: 9.6 us -> 8.18 us
    ppermute x1, starting transfers between devices: 6.5 us -> 3.68 us  [body(): half_other = lax.ppermute(half_mine, 'ctx', swap_half)]
    ppermute x1, waiting for transfers between devices: 1.53 us -> 0.01 us  [body(): prev_got = lax.ppermute(prev_send, 'ctx', swap_core)]
    pallas_call x12 -> x14, Pallas kernels: 29.7 us -> 29.7 us  [call(): pl.pallas_call(kernel, out_shape=shapes, grid=grid, in_specs=ins, out_spe...]
  transfers between devices with their start and end apart: 12 -> 12, of which waited for: 5 -> 5; matrix products, arithmetic and copies ran while one was open for 0% -> 0% of each run, Pallas kernels for 10% -> 8%
where the time goes in v4:
time: 119 us
  blocking collectives  58.6 us (49%)
  Pallas kernels  29.7 us (25%)
  starting transfers between devices  21 us (18%)
  waiting for transfers between devices  8.18 us (7%)
    all_to_all x3, blocking collectives, exchange(): lax.all_to_all(x, 'ctx', 0, 0, tiled=True, axis_index_groups=[early, late])  58.6 us
    pallas_call x14, Pallas kernels, call(): pl.pallas_call(kernel, out_shape=shapes, grid=grid, in_specs=ins, out_spe...  29.7 us
    ppermute x3, starting transfers between devices, body(): lax.ppermute(sums, 'chan', [(i, (i + k) % 4) for i in range(4)])  4.53 us
    ppermute x1, starting transfers between devices, body(): kv_half = lax.ppermute(kv_later, 'ctx', up_half)  3.84 us
    ppermute x1, starting transfers between devices, body(): half_other = lax.ppermute(half_mine, 'ctx', swap_half)  3.68 us
    ppermute x1, waiting for transfers between devices, body(): other = lax.ppermute(mine, 'ctx', swap_half)  2.47 us
  transfers between devices with their start and end apart: 12, of which 5 were waited for; matrix products, arithmetic and copies ran while one was open for 0% of the time, Pallas kernels for 8%

profile of v4, /device:TPU:1, one launch (start us, length us, event | category | flops | bytes accessed | tf_op | source)
XLA Modules:
  0.0 118.5 jit_solution(9102973666409955197)
XLA Ops:
  0.6 5.4 %shard_map.179 = (bf16[16,400,128]{2,1,0:T(8,128)(2,1)}, f32[2048,128]{1,0:T(8,128)}, f32[256,128]{1,0:T(8,128)}, f32[256,128]{1,0:T(8,128)}, f32[128,128]{1,0:T(8,128)}, /*index=5*/f32[16,128]{1,0:T(8,128)}) custom-call(s32[128]{0:T(128)} %docs.7, s32[1,128]{1,0:T(1,128)} %bitcast.5, f32[16,2048]{1,0:T(8,128)} %rate_hbm.1, f32[16,2048]{1,0:T(8,128)} %res_hbm.1, ...), custom_call_target="tpu_custom_call" | custom-call | flops 40000000 | bytes 6000000 | tf_op jit(solution)/shard_map/pallas_call | solution.py:53
  6.0 0.0 copy-start.7
  6.0 29.5 %all_to_all.15.got = bf16[16,400,128]{2,1,0:T(8,128)(2,1)S(1)} all-to-all(bf16[16,400,128]{2,1,0:T(8,128)(2,1)} %get-tuple-element.46), channel_id=1, replica_groups={{0,4,8,12,16,20,24,28,32,36,40,44,48,52,56,60},{96,100,104,108,112,116,..., dimensions={0} | all-to-all | bytes 3276800 | tf_op jit(solution)/shard_map/all_to_all | solution.py:642
  35.5 0.6 shard_map.180
  36.1 0.0 copy-start.1
  36.1 2.0 %collective-permute-start = (f32[144,128]{1,0:T(8,128)S(1)}, f32[144,128]{1,0:T(8,128)S(1)}, u32[]{:S(2)}, u32[]{:S(2)}) collective-permute-start(f32[144,128]{1,0:T(8,128)S(1)} %get-tuple-element.49.mine.ids_mine.docs_mine), channel_id=1, source_target_pairs={{0,96},{4,100},{8,104},{12,108},{16,112},{20,116},{24,120},{28,124... | collective-permute-start | bytes 221192 | tf_op jit(solution)/shard_map/ppermute | solution.py:667
  38.2 2.5 %collective-permute-done.other.after.ids_other.docs_other = f32[144,128]{1,0:T(8,128)S(1)} collective-permute-done((f32[144,128]{1,0:T(8,128)S(1)}, f32[144,128]{1,0:T(8,128)S(1)}, u32[]{:S(2)}, u32[]{:S(2)}) %collective-permute-start) | collective-permute-done | bytes 73760 | tf_op jit(solution)/shard_map/ppermute | solution.py:667
  40.7 3.8 %collective-permute-start.6 = (bf16[16,128,128]{2,1,0:T(8,128)(2,1)S(1)}, bf16[16,128,128]{2,1,0:T(8,128)(2,1)S(1)}, u32[]{:S(2)}, u32[]{:S(2)}) collective-permute-start(bf16[16,128,128]{2,1,0:T(8,128)(2,1)S(1)} %shard_map.186), channel_id=1, source_target_pairs={{0,96},{4,100},{8,104},{12,108},{16,112},{20,116},{24,120},{28,124... | collective-permute-start | bytes 1572872 | tf_op jit(solution)/shard_map/ppermute | solution.py:674
  44.5 0.2 shard_map.181
  44.7 1.9 %collective-permute-start.1 = (f32[128,128]{1,0:T(8,128)S(1)}, f32[128,128]{1,0:T(8,128)S(1)}, u32[]{:S(2)}, u32[]{:S(2)}) collective-permute-start(f32[128,128]{1,0:T(8,128)S(1)} %get-tuple-element.51), channel_id=1, source_target_pairs={{0,4},{4,0},{8,12},{12,8},{16,20},{20,16},{24,28},{28,24},{32,36},... | collective-permute-start | bytes 196616 | tf_op jit(solution)/shard_map/ppermute | solution.py:687
  46.6 0.9 collective-permute-done.1.got
  47.6 3.3 %shard_map.182 = (f32[2048,128]{1,0:T(8,128)S(1)}, f32[8,128]{1,0:T(8,128)S(1)}) custom-call(s32[128]{0:T(128)S(1)} %copy-done.10, f32[128,128]{1,0:T(8,128)S(1)} %get-tuple-element.50.keep, f32[128,128]{1,0:T(8,128)S(1)} %collective-permute-done.1.got, f32[2048,128]{1,0:T(8,128)S(1)} %copy-done, f32[256,128]{1,0:T(8,128)S(1)} %copy-done.5, ...), custom_call_target="tpu_custom_call" | custom-call | flops 40000000 | bytes 6000000 | tf_op jit(solution)/shard_map/pallas_call | solution.py:53
  50.9 3.8 %collective-permute-start.4 = (f32[8,128]{1,0:T(8,128)S(1)}, f32[8,128]{1,0:T(8,128)S(1)}, u32[]{:S(2)}, u32[]{:S(2)}) collective-permute-start(f32[8,128]{1,0:T(8,128)S(1)} %get-tuple-element.55.s0), channel_id=1, source_target_pairs={{0,3},{1,0},{2,1},{3,2},{4,7},{5,4},{6,5},{7,6},{8,11},{9,8},{10,9... | collective-permute-start | bytes 12296 | tf_op jit(solution)/shard_map/ppermute | solution.py:694
  54.7 0.7 collective-permute-start.2
  55.4 1.2 %collective-permute-start.5 = (bf16[16,128,128]{2,1,0:T(8,128)(2,1)S(1)}, bf16[16,128,128]{2,1,0:T(8,128)(2,1)S(1)}, u32[]{:S(2)}, u32[]{:S(2)}) collective-permute-start(bf16[16,128,128]{2,1,0:T(8,128)(2,1)S(1)} %shard_map.184.kv), channel_id=1, source_target_pairs={{0,4},{4,0},{8,12},{12,8},{16,20},{20,16},{24,28},{28,24},{32,36},... | collective-permute-start | bytes 1572872 | tf_op jit(solution)/shard_map/ppermute | solution.py:670
  56.6 2.1 %collective-permute-done.3.s2 = f32[8,128]{1,0:T(8,128)S(1)} collective-permute-done((f32[8,128]{1,0:T(8,128)S(1)}, f32[8,128]{1,0:T(8,128)S(1)}, u32[]{:S(2)}, u32[]{:S(2)}) %collective-permute-start.3) | collective-permute-done | bytes 4128 | tf_op jit(solution)/shard_map/ppermute | solution.py:694
  58.8 1.9 %collective-permute-start.7 = (bf16[16,128,128]{2,1,0:T(8,128)(2,1)S(1)}, bf16[16,128,128]{2,1,0:T(8,128)(2,1)S(1)}, u32[]{:S(2)}, u32[]{:S(2)}) collective-permute-start(bf16[16,128,128]{2,1,0:T(8,128)(2,1)S(1)} %shard_map.187.kv_half), channel_id=1, source_target_pairs={{0,4},{4,0},{8,12},{12,8},{16,20},{20,16},{24,28},{28,24},{32,36},... | collective-permute-start | bytes 1572872 | tf_op jit(solution)/shard_map/ppermute | solution.py:702
  60.6 0.7 shard_map.185
  61.3 0.9 collective-permute-done.7.kv_half_core
  62.2 8.7 %shard_map.188 = (bf16[16,64,128]{2,1,0:T(8,128)(2,1)S(1)}, bf16[16,128,128]{2,1,0:T(8,128)(2,1)S(1)}, bf16[16,128,128]{2,1,0:T(8,128)(2,1)S(1)}, bf16[16,128,12...) custom-call(bf16[4,256,128]{2,1,0:T(8,128)(2,1)S(1)} %get-tuple-element.56.all_q, ...), custom_call_target="tpu_custom_call" | custom-call | flops 10000000000 | bytes 6000000 | tf_op jit(solution)/shard_map/pallas_call | solution.py:53
  70.8 0.4 collective-permute-start.8
  71.3 0.3 collective-permute-start.10
  71.5 5.3 %shard_map.189 = (bf16[128,2048]{1,0:T(8,128)(2,1)}, f32[2048,128]{1,0:T(8,128)S(1)}, bf16[16,64,128]{2,1,0:T(8,128)(2,1)S(1)}) custom-call(s32[128]{0:T(128)S(1)} %copy-done.10, f32[8,128]{1,0:T(8,128)S(1)} %shard_map.183.after.sums, f32[8,128]{1,0:T(8,128)S(1)} %get-tuple-element.63.after, f32[2048,128]{1,0:T(8,128)S(1)} %get-tuple-element.64.f, ...), custom_call_target="tpu_custom_call" | custom-call | flops 40000000 | bytes 6000000 | tf_op jit(solution)/shard_map/pallas_call | solution.py:53
  76.8 0.1 add_convert_fusion
  77.0 1.3 %collective-permute-start.11 = (bf16[16,128,128]{2,1,0:T(8,128)(2,1)S(1)}, bf16[16,128,128]{2,1,0:T(8,128)(2,1)S(1)}, u32[]{:S(2)}, u32[]{:S(2)}) collective-permute-start(bf16[16,128,128]{2,1,0:T(8,128)(2,1)S(1)} %add_convert_fusion), channel_id=1, source_target_pairs={{96,0},{100,4},{104,8},{108,12},{112,16},{116,20},{120,24},{124,28... | collective-permute-start | bytes 1572872 | tf_op jit(solution)/shard_map/ppermute | solution.py:730
  78.3 9.9 %all_to_all.16.back = bf16[16,64,128]{2,1,0:T(8,128)(2,1)S(1)} all-to-all(bf16[16,64,128]{2,1,0:T(8,128)(2,1)S(1)} %get-tuple-element.68), channel_id=1, replica_groups={{0,4,8,12,16,20,24,28,32,36,40,44,48,52,56,60},{96,100,104,108,112,116,..., dimensions={0} | all-to-all | bytes 524288 | tf_op jit(solution)/shard_map/all_to_all | solution.py:642
  88.2 0.2 shard_map.190.mine
  88.4 3.7 %collective-permute-start.9 = (f32[56,128]{1,0:T(8,128)S(1)}, f32[56,128]{1,0:T(8,128)S(1)}, u32[]{:S(2)}, u32[]{:S(2)}) collective-permute-start(f32[56,128]{1,0:T(8,128)S(1)} %shard_map.190.mine), channel_id=1, source_target_pairs={{0,96},{4,100},{8,104},{12,108},{16,112},{20,116},{24,120},{28,124... | collective-permute-start | bytes 86024 | tf_op jit(solution)/shard_map/ppermute | solution.py:736
  92.1 1.9 %collective-permute-done.9.theirs = f32[56,128]{1,0:T(8,128)S(1)} collective-permute-done((f32[56,128]{1,0:T(8,128)S(1)}, f32[56,128]{1,0:T(8,128)S(1)}, u32[]{:S(2)}, u32[]{:S(2)}) %collective-permute-start.9) | collective-permute-done | bytes 28704 | tf_op jit(solution)/shard_map/ppermute | solution.py:736
  94.0 0.4 shard_map.191
  94.4 19.2 %all_to_all.17.got = bf16[16,256,128]{2,1,0:T(8,128)(2,1)S(1)} all-to-all(bf16[16,256,128]{2,1,0:T(8,128)(2,1)S(1)} %shard_map.191), channel_id=1, replica_groups={{0,4,8,12,16,20,24,28,32,36,40,44,48,52,56,60},{96,100,104,108,112,116,..., dimensions={0} | all-to-all | bytes 2097152 | tf_op jit(solution)/shard_map/all_to_all | solution.py:642
  113.6 4.9 %shard_map.192 = (bf16[128,2048]{1,0:T(8,128)(2,1)}, bf16[128,2048]{1,0:T(8,128)(2,1)}, f32[16,2048]{1,0:T(8,128)}, f32[1,2048]{1,0:T(1,128)}, bf16[128,1024]{1,...) custom-call(s32[128]{0:T(128)S(1)} %copy-done.10, bf16[16,256,128]{2,1,0:T(8,128)(2,1)S(1)} %all_to_all.17.got, ...), custom_call_target="tpu_custom_call" | custom-call | flops 40000000 | bytes 6000000 | tf_op jit(solution)/shard_map/pallas_call | solution.py:53
  (32 shorter events, 0.2 us)
Async XLA Ops:
  6.0 29.5 %copy-start.7 = (f32[128,128]{1,0:T(8,128)S(1)}, f32[128,128]{1,0:T(8,128)}, u32[]{:S(2)}) copy-start(f32[128,128]{1,0:T(8,128)} %get-tuple-element.47.through) | copy-start | bytes 196612
  36.1 11.5 %copy-start = (f32[2048,128]{1,0:T(8,128)S(1)}, f32[2048,128]{1,0:T(8,128)}, u32[]{:S(2)}) copy-start(f32[2048,128]{1,0:T(8,128)} %get-tuple-element.52.m) | copy-start | bytes 3145732
  36.1 11.5 %copy-start.1 = (bf16[128,2048]{1,0:T(8,128)(2,1)S(1)}, bf16[128,2048]{1,0:T(8,128)(2,1)}, u32[]{:S(2)}) copy-start(bf16[128,2048]{1,0:T(8,128)(2,1)} %hq.3) | copy-start | bytes 1572868
  36.1 11.5 %copy-start.2 = (bf16[128,2048]{1,0:T(8,128)(2,1)S(1)}, bf16[128,2048]{1,0:T(8,128)(2,1)}, u32[]{:S(2)}) copy-start(bf16[128,2048]{1,0:T(8,128)(2,1)} %hg.3) | copy-start | bytes 1572868
  36.1 11.4 %copy-start.5 = (f32[256,128]{1,0:T(8,128)S(1)}, f32[256,128]{1,0:T(8,128)}, u32[]{:S(2)}) copy-start(f32[256,128]{1,0:T(8,128)} %get-tuple-element.53.dec) | copy-start | bytes 393220
  36.1 11.4 %copy-start.6 = (f32[256,128]{1,0:T(8,128)S(1)}, f32[256,128]{1,0:T(8,128)}, u32[]{:S(2)}) copy-start(f32[256,128]{1,0:T(8,128)} %get-tuple-element.54.wgt) | copy-start | bytes 393220
  36.1 11.4 %copy-start.8 = (f32[2048]{0:T(1024)S(1)}, f32[2048]{0:T(1024)}, u32[]{:S(2)}) copy-start(f32[2048]{0:T(1024)} %param.18) | copy-start | bytes 24580
  36.1 11.4 %copy-start.10 = (s32[128]{0:T(128)S(1)}, s32[128]{0:T(128)}, u32[]{:S(2)}) copy-start(s32[128]{0:T(128)} %docs.7) | copy-start | bytes 1540
  36.1 4.5 %collective-permute-start = (f32[144,128]{1,0:T(8,128)S(1)}, f32[144,128]{1,0:T(8,128)S(1)}, u32[]{:S(2)}, u32[]{:S(2)}) collective-permute-start(f32[144,128]{1,0:T(8,128)S(1)} %get-tuple-element.49.mine.ids_mine.docs_mine), channel_id=1, source_target_pairs={{0,96},{4,100},{8,104},{12,108},{16,112},{20,116},{24,120},{28,124... | collective-permute-start | bytes 221192 | tf_op jit(solution)/shard_map/ppermute | solution.py:667
  40.7 18.0 %collective-permute-start.6 = (bf16[16,128,128]{2,1,0:T(8,128)(2,1)S(1)}, bf16[16,128,128]{2,1,0:T(8,128)(2,1)S(1)}, u32[]{:S(2)}, u32[]{:S(2)}) collective-permute-start(bf16[16,128,128]{2,1,0:T(8,128)(2,1)S(1)} %shard_map.186), channel_id=1, source_target_pairs={{0,96},{4,100},{8,104},{12,108},{16,112},{20,116},{24,120},{28,124... | collective-permute-start | bytes 1572872 | tf_op jit(solution)/shard_map/ppermute | solution.py:674
  44.7 2.8 %collective-permute-start.1 = (f32[128,128]{1,0:T(8,128)S(1)}, f32[128,128]{1,0:T(8,128)S(1)}, u32[]{:S(2)}, u32[]{:S(2)}) collective-permute-start(f32[128,128]{1,0:T(8,128)S(1)} %get-tuple-element.51), channel_id=1, source_target_pairs={{0,4},{4,0},{8,12},{12,8},{16,20},{20,16},{24,28},{28,24},{32,36},... | collective-permute-start | bytes 196616 | tf_op jit(solution)/shard_map/ppermute | solution.py:687
  50.9 5.7 %collective-permute-start.4 = (f32[8,128]{1,0:T(8,128)S(1)}, f32[8,128]{1,0:T(8,128)S(1)}, u32[]{:S(2)}, u32[]{:S(2)}) collective-permute-start(f32[8,128]{1,0:T(8,128)S(1)} %get-tuple-element.55.s0), channel_id=1, source_target_pairs={{0,3},{1,0},{2,1},{3,2},{4,7},{5,4},{6,5},{7,6},{8,11},{9,8},{10,9... | collective-permute-start | bytes 12296 | tf_op jit(solution)/shard_map/ppermute | solution.py:694
  54.7 4.0 %collective-permute-start.3 = (f32[8,128]{1,0:T(8,128)S(1)}, f32[8,128]{1,0:T(8,128)S(1)}, u32[]{:S(2)}, u32[]{:S(2)}) collective-permute-start(f32[8,128]{1,0:T(8,128)S(1)} %get-tuple-element.55.s0), channel_id=1, source_target_pairs={{0,2},{1,3},{2,0},{3,1},{4,6},{5,7},{6,4},{7,5},{8,10},{9,11},{10,... | collective-permute-start | bytes 12296 | tf_op jit(solution)/shard_map/ppermute | solution.py:694
  54.7 4.0 %collective-permute-start.2 = (f32[8,128]{1,0:T(8,128)S(1)}, f32[8,128]{1,0:T(8,128)S(1)}, u32[]{:S(2)}, u32[]{:S(2)}) collective-permute-start(f32[8,128]{1,0:T(8,128)S(1)} %get-tuple-element.55.s0), channel_id=1, source_target_pairs={{0,1},{1,2},{2,3},{3,0},{4,5},{5,6},{6,7},{7,4},{8,9},{9,10},{10,1... | collective-permute-start | bytes 12296 | tf_op jit(solution)/shard_map/ppermute | solution.py:694
  55.4 5.2 %collective-permute-start.5 = (bf16[16,128,128]{2,1,0:T(8,128)(2,1)S(1)}, bf16[16,128,128]{2,1,0:T(8,128)(2,1)S(1)}, u32[]{:S(2)}, u32[]{:S(2)}) collective-permute-start(bf16[16,128,128]{2,1,0:T(8,128)(2,1)S(1)} %shard_map.184.kv), channel_id=1, source_target_pairs={{0,4},{4,0},{8,12},{12,8},{16,20},{20,16},{24,28},{28,24},{32,36},... | collective-permute-start | bytes 1572872 | tf_op jit(solution)/shard_map/ppermute | solution.py:670
  58.8 3.4 %collective-permute-start.7 = (bf16[16,128,128]{2,1,0:T(8,128)(2,1)S(1)}, bf16[16,128,128]{2,1,0:T(8,128)(2,1)S(1)}, u32[]{:S(2)}, u32[]{:S(2)}) collective-permute-start(bf16[16,128,128]{2,1,0:T(8,128)(2,1)S(1)} %shard_map.187.kv_half), channel_id=1, source_target_pairs={{0,4},{4,0},{8,12},{12,8},{16,20},{20,16},{24,28},{28,24},{32,36},... | collective-permute-start | bytes 1572872 | tf_op jit(solution)/shard_map/ppermute | solution.py:702
  70.8 6.0 %collective-permute-start.8 = (bf16[16,128,128]{2,1,0:T(8,128)(2,1)S(1)}, bf16[16,128,128]{2,1,0:T(8,128)(2,1)S(1)}, u32[]{:S(2)}, u32[]{:S(2)}) collective-permute-start(bf16[16,128,128]{2,1,0:T(8,128)(2,1)S(1)} %get-tuple-element.67), channel_id=1, source_target_pairs={{0,4},{4,0},{8,12},{12,8},{16,20},{20,16},{24,28},{28,24},{32,36},... | collective-permute-start | bytes 1572872 | tf_op jit(solution)/shard_map/ppermute | solution.py:726
  71.3 20.8 %collective-permute-start.10 = (bf16[16,128,128]{2,1,0:T(8,128)(2,1)S(1)}, bf16[16,128,128]{2,1,0:T(8,128)(2,1)S(1)}, u32[]{:S(2)}, u32[]{:S(2)}) collective-permute-start(bf16[16,128,128]{2,1,0:T(8,128)(2,1)S(1)} %get-tuple-element.73), channel_id=1, source_target_pairs={{0,4},{4,0},{8,12},{12,8},{16,20},{20,16},{24,28},{28,24},{32,36},... | collective-permute-start | bytes 1572872 | tf_op jit(solution)/shard_map/ppermute | solution.py:727
  76.8 11.4 %copy-start.9 = (f32[16,128]{1,0:T(8,128)S(1)}, f32[16,128]{1,0:T(8,128)}, u32[]{:S(2)}) copy-start(f32[16,128]{1,0:T(8,128)} %get-tuple-element.69.rate) | copy-start | bytes 24580
  77.0 17.0 %collective-permute-start.11 = (bf16[16,128,128]{2,1,0:T(8,128)(2,1)S(1)}, bf16[16,128,128]{2,1,0:T(8,128)(2,1)S(1)}, u32[]{:S(2)}, u32[]{:S(2)}) collective-permute-start(bf16[16,128,128]{2,1,0:T(8,128)(2,1)S(1)} %add_convert_fusion), channel_id=1, source_target_pairs={{96,0},{100,4},{104,8},{108,12},{112,16},{116,20},{120,24},{124,28... | collective-permute-start | bytes 1572872 | tf_op jit(solution)/shard_map/ppermute | solution.py:730
  88.4 5.6 %collective-permute-start.9 = (f32[56,128]{1,0:T(8,128)S(1)}, f32[56,128]{1,0:T(8,128)S(1)}, u32[]{:S(2)}, u32[]{:S(2)}) collective-permute-start(f32[56,128]{1,0:T(8,128)S(1)} %shard_map.190.mine), channel_id=1, source_target_pairs={{0,96},{4,100},{8,104},{12,108},{16,112},{20,116},{24,120},{28,124... | collective-permute-start | bytes 86024 | tf_op jit(solution)/shard_map/ppermute | solution.py:736
  94.4 19.3 %copy-start.3 = (bf16[128,2048]{1,0:T(8,128)(2,1)S(1)}, bf16[128,2048]{1,0:T(8,128)(2,1)}, u32[]{:S(2)}) copy-start(bf16[128,2048]{1,0:T(8,128)(2,1)} %hk.1) | copy-start | bytes 1572868
  94.4 19.3 %copy-start.4 = (bf16[128,2048]{1,0:T(8,128)(2,1)S(1)}, bf16[128,2048]{1,0:T(8,128)(2,1)}, u32[]{:S(2)}) copy-start(bf16[128,2048]{1,0:T(8,128)(2,1)} %hv.1) | copy-start | bytes 1572868

commit v5 on v4

--- a/solution.py
+++ b/solution.py
@@ -19,15 +19,15 @@
 CHUNKS = CH // LANES
 GROUP = 16
 HALF = GROUP * TOK
-SPAN = 32
+SPAN = 64
 SCALE = HEAD_DIM ** (-0.5)
 LOG2E = 1.4426950408889634
 
 HALF_ROWS = POLES * 8
 half_shape = (HALF_ROWS, LANES)
 ROW_DOC, ROW_K, ROW_V, ROW_Q, ROW_G, ROWS_IN = 128, 144, 208, 272, 336, 400
-OUT_RES, OUT_GAIN, OUT_Q, OUT_KV, ROWS_OUT = 16, 48, 64, 128, 256
-BACK_SUM, BACK_GAIN, ROWS_BACK = 16, 48, 64
+OUT_RES, OUT_GAIN, OUT_Q, OUT_KV, ROWS_OUT = 16, 32, 48, 112, 240
+BACK_SUM, BACK_GAIN, ROWS_BACK = 16, 32, 48
 
 ROWS_TILE = 256
 KEYS_TILE = 512
@@ -138,10 +138,6 @@
 def pair_rows(row):
     high, low = split(jnp.broadcast_to(row, (8, LANES)))
     return jnp.concatenate([high.astype(F32), low.astype(F32)], axis=0).astype(BF16)
-
-
-def joined(ref, index, row):
-    return ref[index, row : row + 16, :].astype(F32) + ref[index, row + 16 : row + 32, :].astype(F32)
 
 
 def first_kernel(
@@ -357,9 +353,7 @@
             totals[n * 16 + 8 * g : n * 16 + 8 * g + 8, :] = carry[POLES + n]
     for p in range(GROUP):
         send[p, 0:16, :] = starts[every(chunk_of(p), POLES), :].astype(BF16)
-        high, low = split(totals[every(chunk_of(p), POLES), :])
-        send[p, BACK_SUM : BACK_SUM + 16, :] = high
-        send[p, BACK_SUM + 16 : BACK_GAIN, :] = low
+        send[p, BACK_SUM:BACK_GAIN, :] = totals[every(chunk_of(p), POLES), :].astype(BF16)
 
 
 def half_adjoint_kernel(docs_mine, ends, back, rate, docs_other, out):
@@ -377,7 +371,7 @@
     unit = met
     for b in reversed(range(GROUP)):
         end = decay * ends[b]
-        total = total + joined(back, block_at(b), BACK_SUM) + end * carry
+        total = total + back[block_at(b), BACK_SUM:BACK_GAIN, :].astype(F32) + end * carry
         reach = reach + end * unit
         pair = back[block_at(b), BACK_GAIN:ROWS_BACK, :].astype(F32)
         gains = gains + pair[0:8] + pair[8:16]
@@ -404,14 +398,13 @@
     late_start = mine[0:16, :] * (1.0 - early) + theirs[0:16, :] * early
     early_reach = mine[32:48, :] * early + theirs[32:48, :] * (1.0 - early)
     residue = mine[16:32, :] + theirs[16:32, :] + late_start * early_reach
-    res_high, res_low = split(scaling_of(rates) * residue)
+    residue = (scaling_of(rates) * residue).astype(BF16)
     pair = pair_rows((mine[48:56, :] + theirs[48:56, :])[0:1])
     carry = theirs[0:16, :] * met
     for b in reversed(range(GROUP)):
         at = block_at(b)
         send[at, 0:OUT_RES, :] = carry.astype(BF16)
-        send[at, OUT_RES : OUT_RES + 16, :] = res_high
-        send[at, OUT_RES + 16 : OUT_GAIN, :] = res_low
+        send[at, OUT_RES:OUT_GAIN, :] = residue
         send[at, OUT_GAIN:OUT_Q, :] = pair
         send[at, OUT_Q:OUT_KV, :] = dq[at]
         kv = own[at].astype(F32) + own_got[at].astype(F32) + prev_got[at].astype(F32) * early
@@ -426,7 +419,7 @@
     for p in range(GROUP):
         j = chunk_of(p)
         entry[16 * j : 16 * j + 16, :] = got[p, 0:OUT_RES, :].astype(F32)
-        gres[:, lanes(j)] = joined(got, p, OUT_RES)
+        gres[:, lanes(j)] = got[p, OUT_RES:OUT_GAIN, :].astype(F32)
         pair = got[p, OUT_GAIN:OUT_Q, :].astype(F32)
         ggain[:, lanes(j)] = pair[0:1] + pair[8:9]
         rows = slice(64 * (p % 2), 64 * (p % 2) + 64)

time: 119 us -> 118 us (level)
  blocking collectives: 58.6 us -> 57.1 us
    all_to_all x3, blocking collectives: 58.6 us -> 57.1 us  [exchange(): lax.all_to_all(x, 'ctx', 0, 0, tiled=True, axis_index_groups=[early, late])]
where the time goes in v5:
time: 118 us; the launch traced here: 117 us
  blocking collectives  57.1 us (48%)
  Pallas kernels  29.4 us (25%)
  starting transfers between devices  21 us (18%)
  waiting for transfers between devices  8.71 us (7%)
    all_to_all x3, blocking collectives, exchange(): lax.all_to_all(x, 'ctx', 0, 0, tiled=True, axis_index_groups=[early, late])  57.1 us
    pallas_call x14, Pallas kernels, call(): pl.pallas_call(kernel, out_shape=shapes, grid=grid, in_specs=ins, out_spe...  29.4 us
    ppermute x3, starting transfers between devices, body(): lax.ppermute(sums, 'chan', [(i, (i + k) % 4) for i in range(4)])  4.53 us
    ppermute x1, starting transfers between devices, body(): kv_half = lax.ppermute(kv_later, 'ctx', up_half)  3.84 us
    ppermute x1, starting transfers between devices, body(): half_other = lax.ppermute(half_mine, 'ctx', swap_half)  3.68 us
    ppermute x1, waiting for transfers between devices, body(): other = lax.ppermute(mine, 'ctx', swap_half)  2.47 us
    ppermute x1, waiting for transfers between devices, body(): half_other = lax.ppermute(half_mine, 'ctx', swap_half)  2.4 us
  transfers between devices with their start and end apart: 12, of which 5 were waited for; matrix products, arithmetic and copies ran while one was open for 0% of the time, Pallas kernels for 8%

profile of v5, /device:TPU:1, one launch (start us, length us, event | category | flops | bytes accessed | tf_op | source)
XLA Modules:
  0.0 117.3 jit_solution(7668737695254494166)
XLA Ops:
  0.6 5.3 %shard_map.179 = (bf16[16,400,128]{2,1,0:T(8,128)(2,1)}, f32[2048,128]{1,0:T(8,128)}, f32[256,128]{1,0:T(8,128)}, f32[256,128]{1,0:T(8,128)}, f32[128,128]{1,0:T(8,128)}, /*index=5*/f32[16,128]{1,0:T(8,128)}) custom-call(s32[128]{0:T(128)} %docs.7, s32[1,128]{1,0:T(1,128)} %bitcast.5, f32[16,2048]{1,0:T(8,128)} %rate_hbm.1, f32[16,2048]{1,0:T(8,128)} %res_hbm.1, ...), custom_call_target="tpu_custom_call" | custom-call | flops 40000000 | bytes 6000000 | tf_op jit(solution)/shard_map/pallas_call | solution.py:53
  6.0 29.5 %all_to_all.15.got = bf16[16,400,128]{2,1,0:T(8,128)(2,1)S(1)} all-to-all(bf16[16,400,128]{2,1,0:T(8,128)(2,1)} %get-tuple-element.46), channel_id=1, replica_groups={{0,4,8,12,16,20,24,28,32,36,40,44,48,52,56,60},{96,100,104,108,112,116,..., dimensions={0} | all-to-all | bytes 3276800 | tf_op jit(solution)/shard_map/all_to_all | solution.py:635
  35.4 0.6 shard_map.180
  36.0 0.0 copy-start.5
  36.0 0.0 copy-start.6
  36.1 2.0 %collective-permute-start = (f32[144,128]{1,0:T(8,128)S(1)}, f32[144,128]{1,0:T(8,128)S(1)}, u32[]{:S(2)}, u32[]{:S(2)}) collective-permute-start(f32[144,128]{1,0:T(8,128)S(1)} %get-tuple-element.49.mine.ids_mine.docs_mine), channel_id=1, source_target_pairs={{0,96},{4,100},{8,104},{12,108},{16,112},{20,116},{24,120},{28,124... | collective-permute-start | bytes 221192 | tf_op jit(solution)/shard_map/ppermute | solution.py:660
  38.1 2.5 %collective-permute-done.other.after.ids_other.docs_other = f32[144,128]{1,0:T(8,128)S(1)} collective-permute-done((f32[144,128]{1,0:T(8,128)S(1)}, f32[144,128]{1,0:T(8,128)S(1)}, u32[]{:S(2)}, u32[]{:S(2)}) %collective-permute-start) | collective-permute-done | bytes 73760 | tf_op jit(solution)/shard_map/ppermute | solution.py:660
  40.6 3.8 %collective-permute-start.6 = (bf16[16,128,128]{2,1,0:T(8,128)(2,1)S(1)}, bf16[16,128,128]{2,1,0:T(8,128)(2,1)S(1)}, u32[]{:S(2)}, u32[]{:S(2)}) collective-permute-start(bf16[16,128,128]{2,1,0:T(8,128)(2,1)S(1)} %shard_map.186), channel_id=1, source_target_pairs={{0,96},{4,100},{8,104},{12,108},{16,112},{20,116},{24,120},{28,124... | collective-permute-start | bytes 1572872 | tf_op jit(solution)/shard_map/ppermute | solution.py:667
  44.5 0.2 shard_map.181
  44.7 1.9 %collective-permute-start.1 = (f32[128,128]{1,0:T(8,128)S(1)}, f32[128,128]{1,0:T(8,128)S(1)}, u32[]{:S(2)}, u32[]{:S(2)}) collective-permute-start(f32[128,128]{1,0:T(8,128)S(1)} %get-tuple-element.51), channel_id=1, source_target_pairs={{0,4},{4,0},{8,12},{12,8},{16,20},{20,16},{24,28},{28,24},{32,36},... | collective-permute-start | bytes 196616 | tf_op jit(solution)/shard_map/ppermute | solution.py:680
  46.6 0.9 collective-permute-done.1.got
  47.5 3.3 %shard_map.182 = (f32[2048,128]{1,0:T(8,128)S(1)}, f32[8,128]{1,0:T(8,128)S(1)}) custom-call(s32[128]{0:T(128)S(1)} %copy-done.10, f32[128,128]{1,0:T(8,128)S(1)} %get-tuple-element.50.keep, f32[128,128]{1,0:T(8,128)S(1)} %collective-permute-done.1.got, f32[2048,128]{1,0:T(8,128)S(1)} %copy-done, f32[256,128]{1,0:T(8,128)S(1)} %copy-done.5, ...), custom_call_target="tpu_custom_call" | custom-call | flops 40000000 | bytes 6000000 | tf_op jit(solution)/shard_map/pallas_call | solution.py:53
  50.8 3.8 %collective-permute-start.4 = (f32[8,128]{1,0:T(8,128)S(1)}, f32[8,128]{1,0:T(8,128)S(1)}, u32[]{:S(2)}, u32[]{:S(2)}) collective-permute-start(f32[8,128]{1,0:T(8,128)S(1)} %get-tuple-element.55.s0), channel_id=1, source_target_pairs={{0,3},{1,0},{2,1},{3,2},{4,7},{5,4},{6,5},{7,6},{8,11},{9,8},{10,9... | collective-permute-start | bytes 12296 | tf_op jit(solution)/shard_map/ppermute | solution.py:687
  54.6 0.7 collective-permute-start.2
  55.3 1.2 %collective-permute-start.5 = (bf16[16,128,128]{2,1,0:T(8,128)(2,1)S(1)}, bf16[16,128,128]{2,1,0:T(8,128)(2,1)S(1)}, u32[]{:S(2)}, u32[]{:S(2)}) collective-permute-start(bf16[16,128,128]{2,1,0:T(8,128)(2,1)S(1)} %shard_map.184.kv), channel_id=1, source_target_pairs={{0,4},{4,0},{8,12},{12,8},{16,20},{20,16},{24,28},{28,24},{32,36},... | collective-permute-start | bytes 1572872 | tf_op jit(solution)/shard_map/ppermute | solution.py:663
  56.5 2.1 %collective-permute-done.3.s2 = f32[8,128]{1,0:T(8,128)S(1)} collective-permute-done((f32[8,128]{1,0:T(8,128)S(1)}, f32[8,128]{1,0:T(8,128)S(1)}, u32[]{:S(2)}, u32[]{:S(2)}) %collective-permute-start.3) | collective-permute-done | bytes 4128 | tf_op jit(solution)/shard_map/ppermute | solution.py:687
  58.6 1.9 %collective-permute-start.7 = (bf16[16,128,128]{2,1,0:T(8,128)(2,1)S(1)}, bf16[16,128,128]{2,1,0:T(8,128)(2,1)S(1)}, u32[]{:S(2)}, u32[]{:S(2)}) collective-permute-start(bf16[16,128,128]{2,1,0:T(8,128)(2,1)S(1)} %shard_map.187.kv_half), channel_id=1, source_target_pairs={{0,4},{4,0},{8,12},{12,8},{16,20},{20,16},{24,28},{28,24},{32,36},... | collective-permute-start | bytes 1572872 | tf_op jit(solution)/shard_map/ppermute | solution.py:695
  60.5 0.7 shard_map.185
  61.2 0.9 collective-permute-done.7.kv_half_core
  62.0 8.7 %shard_map.188 = (bf16[16,64,128]{2,1,0:T(8,128)(2,1)S(1)}, bf16[16,128,128]{2,1,0:T(8,128)(2,1)S(1)}, bf16[16,128,128]{2,1,0:T(8,128)(2,1)S(1)}, bf16[16,128,12...) custom-call(bf16[4,256,128]{2,1,0:T(8,128)(2,1)S(1)} %get-tuple-element.56.all_q, ...), custom_call_target="tpu_custom_call" | custom-call | flops 10000000000 | bytes 6000000 | tf_op jit(solution)/shard_map/pallas_call | solution.py:53
  70.7 0.5 collective-permute-start.8
  71.1 0.3 collective-permute-start.10
  71.4 5.2 %shard_map.189 = (bf16[128,2048]{1,0:T(8,128)(2,1)}, f32[2048,128]{1,0:T(8,128)S(1)}, bf16[16,48,128]{2,1,0:T(8,128)(2,1)S(1)}) custom-call(s32[128]{0:T(128)S(1)} %copy-done.10, f32[8,128]{1,0:T(8,128)S(1)} %shard_map.183.after.sums, f32[8,128]{1,0:T(8,128)S(1)} %get-tuple-element.63.after, f32[2048,128]{1,0:T(8,128)S(1)} %get-tuple-element.64.f, ...), custom_call_target="tpu_custom_call" | custom-call | flops 40000000 | bytes 6000000 | tf_op jit(solution)/shard_map/pallas_call | solution.py:53
  76.6 0.1 add_convert_fusion
  76.8 1.3 %collective-permute-start.11 = (bf16[16,128,128]{2,1,0:T(8,128)(2,1)S(1)}, bf16[16,128,128]{2,1,0:T(8,128)(2,1)S(1)}, u32[]{:S(2)}, u32[]{:S(2)}) collective-permute-start(bf16[16,128,128]{2,1,0:T(8,128)(2,1)S(1)} %add_convert_fusion), channel_id=1, source_target_pairs={{96,0},{100,4},{104,8},{108,12},{112,16},{116,20},{120,24},{124,28... | collective-permute-start | bytes 1572872 | tf_op jit(solution)/shard_map/ppermute | solution.py:723
  78.1 9.4 %all_to_all.16.back = bf16[16,48,128]{2,1,0:T(8,128)(2,1)S(1)} all-to-all(bf16[16,48,128]{2,1,0:T(8,128)(2,1)S(1)} %get-tuple-element.68), channel_id=1, replica_groups={{0,4,8,12,16,20,24,28,32,36,40,44,48,52,56,60},{96,100,104,108,112,116,..., dimensions={0} | all-to-all | bytes 393216 | tf_op jit(solution)/shard_map/all_to_all | solution.py:635
  87.5 0.2 shard_map.190.mine
  87.7 3.7 %collective-permute-start.9 = (f32[56,128]{1,0:T(8,128)S(1)}, f32[56,128]{1,0:T(8,128)S(1)}, u32[]{:S(2)}, u32[]{:S(2)}) collective-permute-start(f32[56,128]{1,0:T(8,128)S(1)} %shard_map.190.mine), channel_id=1, source_target_pairs={{0,96},{4,100},{8,104},{12,108},{16,112},{20,116},{24,120},{28,124... | collective-permute-start | bytes 86024 | tf_op jit(solution)/shard_map/ppermute | solution.py:729
  91.4 2.4 %collective-permute-done.9.theirs = f32[56,128]{1,0:T(8,128)S(1)} collective-permute-done((f32[56,128]{1,0:T(8,128)S(1)}, f32[56,128]{1,0:T(8,128)S(1)}, u32[]{:S(2)}, u32[]{:S(2)}) %collective-permute-start.9) | collective-permute-done | bytes 28704 | tf_op jit(solution)/shard_map/ppermute | solution.py:729
  93.8 0.4 shard_map.191
  94.2 18.3 %all_to_all.17.got = bf16[16,240,128]{2,1,0:T(8,128)(2,1)S(1)} all-to-all(bf16[16,240,128]{2,1,0:T(8,128)(2,1)S(1)} %shard_map.191), channel_id=1, replica_groups={{0,4,8,12,16,20,24,28,32,36,40,44,48,52,56,60},{96,100,104,108,112,116,..., dimensions={0} | all-to-all | bytes 1966080 | tf_op jit(solution)/shard_map/all_to_all | solution.py:635
  112.5 4.8 %shard_map.192 = (bf16[128,2048]{1,0:T(8,128)(2,1)}, bf16[128,2048]{1,0:T(8,128)(2,1)}, f32[16,2048]{1,0:T(8,128)}, f32[1,2048]{1,0:T(1,128)}, bf16[128,1024]{1,...) custom-call(s32[128]{0:T(128)S(1)} %copy-done.10, bf16[16,240,128]{2,1,0:T(8,128)(2,1)S(1)} %all_to_all.17.got, ...), custom_call_target="tpu_custom_call" | custom-call | flops 40000000 | bytes 6000000 | tf_op jit(solution)/shard_map/pallas_call | solution.py:53
  (32 shorter events, 0.2 us)
Async XLA Ops:
  6.0 29.5 %copy-start.7 = (f32[128,128]{1,0:T(8,128)S(1)}, f32[128,128]{1,0:T(8,128)}, u32[]{:S(2)}) copy-start(f32[128,128]{1,0:T(8,128)} %get-tuple-element.47.through) | copy-start | bytes 196612
  36.0 11.5 %copy-start = (f32[2048,128]{1,0:T(8,128)S(1)}, f32[2048,128]{1,0:T(8,128)}, u32[]{:S(2)}) copy-start(f32[2048,128]{1,0:T(8,128)} %get-tuple-element.52.m) | copy-start | bytes 3145732
  36.0 11.5 %copy-start.1 = (bf16[128,2048]{1,0:T(8,128)(2,1)S(1)}, bf16[128,2048]{1,0:T(8,128)(2,1)}, u32[]{:S(2)}) copy-start(bf16[128,2048]{1,0:T(8,128)(2,1)} %hq.3) | copy-start | bytes 1572868
  36.0 11.5 %copy-start.2 = (bf16[128,2048]{1,0:T(8,128)(2,1)S(1)}, bf16[128,2048]{1,0:T(8,128)(2,1)}, u32[]{:S(2)}) copy-start(bf16[128,2048]{1,0:T(8,128)(2,1)} %hg.3) | copy-start | bytes 1572868
  36.0 11.4 %copy-start.5 = (f32[256,128]{1,0:T(8,128)S(1)}, f32[256,128]{1,0:T(8,128)}, u32[]{:S(2)}) copy-start(f32[256,128]{1,0:T(8,128)} %get-tuple-element.53.dec) | copy-start | bytes 393220
  36.0 11.4 %copy-start.6 = (f32[256,128]{1,0:T(8,128)S(1)}, f32[256,128]{1,0:T(8,128)}, u32[]{:S(2)}) copy-start(f32[256,128]{1,0:T(8,128)} %get-tuple-element.54.wgt) | copy-start | bytes 393220
  36.1 11.4 %copy-start.8 = (f32[2048]{0:T(1024)S(1)}, f32[2048]{0:T(1024)}, u32[]{:S(2)}) copy-start(f32[2048]{0:T(1024)} %param.18) | copy-start | bytes 24580
  36.1 11.4 %copy-start.10 = (s32[128]{0:T(128)S(1)}, s32[128]{0:T(128)}, u32[]{:S(2)}) copy-start(s32[128]{0:T(128)} %docs.7) | copy-start | bytes 1540
  36.1 4.5 %collective-permute-start = (f32[144,128]{1,0:T(8,128)S(1)}, f32[144,128]{1,0:T(8,128)S(1)}, u32[]{:S(2)}, u32[]{:S(2)}) collective-permute-start(f32[144,128]{1,0:T(8,128)S(1)} %get-tuple-element.49.mine.ids_mine.docs_mine), channel_id=1, source_target_pairs={{0,96},{4,100},{8,104},{12,108},{16,112},{20,116},{24,120},{28,124... | collective-permute-start | bytes 221192 | tf_op jit(solution)/shard_map/ppermute | solution.py:660
  40.6 18.0 %collective-permute-start.6 = (bf16[16,128,128]{2,1,0:T(8,128)(2,1)S(1)}, bf16[16,128,128]{2,1,0:T(8,128)(2,1)S(1)}, u32[]{:S(2)}, u32[]{:S(2)}) collective-permute-start(bf16[16,128,128]{2,1,0:T(8,128)(2,1)S(1)} %shard_map.186), channel_id=1, source_target_pairs={{0,96},{4,100},{8,104},{12,108},{16,112},{20,116},{24,120},{28,124... | collective-permute-start | bytes 1572872 | tf_op jit(solution)/shard_map/ppermute | solution.py:667
  44.7 2.8 %collective-permute-start.1 = (f32[128,128]{1,0:T(8,128)S(1)}, f32[128,128]{1,0:T(8,128)S(1)}, u32[]{:S(2)}, u32[]{:S(2)}) collective-permute-start(f32[128,128]{1,0:T(8,128)S(1)} %get-tuple-element.51), channel_id=1, source_target_pairs={{0,4},{4,0},{8,12},{12,8},{16,20},{20,16},{24,28},{28,24},{32,36},... | collective-permute-start | bytes 196616 | tf_op jit(solution)/shard_map/ppermute | solution.py:680
  50.8 5.7 %collective-permute-start.4 = (f32[8,128]{1,0:T(8,128)S(1)}, f32[8,128]{1,0:T(8,128)S(1)}, u32[]{:S(2)}, u32[]{:S(2)}) collective-permute-start(f32[8,128]{1,0:T(8,128)S(1)} %get-tuple-element.55.s0), channel_id=1, source_target_pairs={{0,3},{1,0},{2,1},{3,2},{4,7},{5,4},{6,5},{7,6},{8,11},{9,8},{10,9... | collective-permute-start | bytes 12296 | tf_op jit(solution)/shard_map/ppermute | solution.py:687
  54.6 4.0 %collective-permute-start.3 = (f32[8,128]{1,0:T(8,128)S(1)}, f32[8,128]{1,0:T(8,128)S(1)}, u32[]{:S(2)}, u32[]{:S(2)}) collective-permute-start(f32[8,128]{1,0:T(8,128)S(1)} %get-tuple-element.55.s0), channel_id=1, source_target_pairs={{0,2},{1,3},{2,0},{3,1},{4,6},{5,7},{6,4},{7,5},{8,10},{9,11},{10,... | collective-permute-start | bytes 12296 | tf_op jit(solution)/shard_map/ppermute | solution.py:687
  54.6 4.0 %collective-permute-start.2 = (f32[8,128]{1,0:T(8,128)S(1)}, f32[8,128]{1,0:T(8,128)S(1)}, u32[]{:S(2)}, u32[]{:S(2)}) collective-permute-start(f32[8,128]{1,0:T(8,128)S(1)} %get-tuple-element.55.s0), channel_id=1, source_target_pairs={{0,1},{1,2},{2,3},{3,0},{4,5},{5,6},{6,7},{7,4},{8,9},{9,10},{10,1... | collective-permute-start | bytes 12296 | tf_op jit(solution)/shard_map/ppermute | solution.py:687
  55.3 5.2 %collective-permute-start.5 = (bf16[16,128,128]{2,1,0:T(8,128)(2,1)S(1)}, bf16[16,128,128]{2,1,0:T(8,128)(2,1)S(1)}, u32[]{:S(2)}, u32[]{:S(2)}) collective-permute-start(bf16[16,128,128]{2,1,0:T(8,128)(2,1)S(1)} %shard_map.184.kv), channel_id=1, source_target_pairs={{0,4},{4,0},{8,12},{12,8},{16,20},{20,16},{24,28},{28,24},{32,36},... | collective-permute-start | bytes 1572872 | tf_op jit(solution)/shard_map/ppermute | solution.py:663
  58.6 3.4 %collective-permute-start.7 = (bf16[16,128,128]{2,1,0:T(8,128)(2,1)S(1)}, bf16[16,128,128]{2,1,0:T(8,128)(2,1)S(1)}, u32[]{:S(2)}, u32[]{:S(2)}) collective-permute-start(bf16[16,128,128]{2,1,0:T(8,128)(2,1)S(1)} %shard_map.187.kv_half), channel_id=1, source_target_pairs={{0,4},{4,0},{8,12},{12,8},{16,20},{20,16},{24,28},{28,24},{32,36},... | collective-permute-start | bytes 1572872 | tf_op jit(solution)/shard_map/ppermute | solution.py:695
  70.7 5.9 %collective-permute-start.8 = (bf16[16,128,128]{2,1,0:T(8,128)(2,1)S(1)}, bf16[16,128,128]{2,1,0:T(8,128)(2,1)S(1)}, u32[]{:S(2)}, u32[]{:S(2)}) collective-permute-start(bf16[16,128,128]{2,1,0:T(8,128)(2,1)S(1)} %get-tuple-element.67), channel_id=1, source_target_pairs={{0,4},{4,0},{8,12},{12,8},{16,20},{20,16},{24,28},{28,24},{32,36},... | collective-permute-start | bytes 1572872 | tf_op jit(solution)/shard_map/ppermute | solution.py:719
  71.1 20.2 %collective-permute-start.10 = (bf16[16,128,128]{2,1,0:T(8,128)(2,1)S(1)}, bf16[16,128,128]{2,1,0:T(8,128)(2,1)S(1)}, u32[]{:S(2)}, u32[]{:S(2)}) collective-permute-start(bf16[16,128,128]{2,1,0:T(8,128)(2,1)S(1)} %get-tuple-element.73), channel_id=1, source_target_pairs={{0,4},{4,0},{8,12},{12,8},{16,20},{20,16},{24,28},{28,24},{32,36},... | collective-permute-start | bytes 1572872 | tf_op jit(solution)/shard_map/ppermute | solution.py:720
  76.6 10.8 %copy-start.9 = (f32[16,128]{1,0:T(8,128)S(1)}, f32[16,128]{1,0:T(8,128)}, u32[]{:S(2)}) copy-start(f32[16,128]{1,0:T(8,128)} %get-tuple-element.69.rate) | copy-start | bytes 24580
  76.8 17.0 %collective-permute-start.11 = (bf16[16,128,128]{2,1,0:T(8,128)(2,1)S(1)}, bf16[16,128,128]{2,1,0:T(8,128)(2,1)S(1)}, u32[]{:S(2)}, u32[]{:S(2)}) collective-permute-start(bf16[16,128,128]{2,1,0:T(8,128)(2,1)S(1)} %add_convert_fusion), channel_id=1, source_target_pairs={{96,0},{100,4},{104,8},{108,12},{112,16},{116,20},{120,24},{124,28... | collective-permute-start | bytes 1572872 | tf_op jit(solution)/shard_map/ppermute | solution.py:723
  87.7 6.1 %collective-permute-start.9 = (f32[56,128]{1,0:T(8,128)S(1)}, f32[56,128]{1,0:T(8,128)S(1)}, u32[]{:S(2)}, u32[]{:S(2)}) collective-permute-start(f32[56,128]{1,0:T(8,128)S(1)} %shard_map.190.mine), channel_id=1, source_target_pairs={{0,96},{4,100},{8,104},{12,108},{16,112},{20,116},{24,120},{28,124... | collective-permute-start | bytes 86024 | tf_op jit(solution)/shard_map/ppermute | solution.py:729
  94.2 18.3 %copy-start.3 = (bf16[128,2048]{1,0:T(8,128)(2,1)S(1)}, bf16[128,2048]{1,0:T(8,128)(2,1)}, u32[]{:S(2)}) copy-start(bf16[128,2048]{1,0:T(8,128)(2,1)} %hk.1) | copy-start | bytes 1572868
  94.2 18.3 %copy-start.4 = (bf16[128,2048]{1,0:T(8,128)(2,1)S(1)}, bf16[128,2048]{1,0:T(8,128)(2,1)}, u32[]{:S(2)}) copy-start(bf16[128,2048]{1,0:T(8,128)(2,1)} %hv.1) | copy-start | bytes 1572868

commit v6 on v5

--- a/solution.py
+++ b/solution.py
@@ -143,7 +143,7 @@
 def first_kernel(
     docs, doc_row, rate_hbm, res_hbm, hk_hbm, hv_hbm, ak_hbm, av_hbm, aq_hbm, ag_hbm,
     send, m_out, dec, wgt, through, rate_part,
-    thr_all, rate, res, hk, hv, ak, av, aq, ag, m, sems,
+    thr_all, rate, res, hk, hv, ak, av, aq, ag, m, states, heads, sems,
 ):
     pairs = (
         (rate_hbm, rate), (res_hbm, res), (hk_hbm, hk), (hv_hbm, hv),
@@ -157,7 +157,7 @@
         copy.start()
     ids = jnp.broadcast_to(doc_row[...].astype(F32), (16, LANES)).astype(BF16)
     for p in range(GROUP):
-        send[p, ROW_DOC:ROW_K, :] = ids
+        heads[p, 0 : ROW_K - ROW_DOC, :] = ids
     core = core_of()
     copies[0].wait()
     copies[1].wait()
@@ -178,8 +178,16 @@
     copies[3].wait()
     for j in range(CHUNKS):
         m[every(j, TOK), :] = hk[:, lanes(j)].astype(F32) * hv[:, lanes(j)].astype(F32)
-    leaving = pltpu.make_async_copy(m, m_out, sems.at[8])
-    leaving.start()
+    leaving = [pltpu.make_async_copy(m, m_out, sems.at[8])]
+    leaving[0].start()
+    for copy, row, ref in zip(copies[4:], (ROW_K, ROW_V, ROW_Q, ROW_G), (ak, av, aq, ag)):
+        copy.wait()
+        at = row - ROW_DOC
+        for p in range(GROUP):
+            part = slice(64 * (p % 2), 64 * (p % 2) + 64)
+            heads[p, at : at + 64, :] = ref[part, lanes(p // 2)]
+    leaving.append(pltpu.make_async_copy(heads, send.at[:, ROW_DOC:ROWS_IN, :], sems.at[9]))
+    leaving[1].start()
     for g in range(2):
         kept = [dec[n * 16 + 8 * g : n * 16 + 8 * g + 8, :] for n in range(POLES)]
 
@@ -191,13 +199,11 @@
         pairs = [jnp.concatenate(state[n : n + 2], axis=0).astype(BF16) for n in range(0, POLES, 2)]
         for p in range(g, GROUP, 2):
             for i, pair in enumerate(pairs):
-                send[p, 16 * i : 16 * i + 16, :] = pair
-    for copy, row, ref in zip(copies[4:], (ROW_K, ROW_V, ROW_Q, ROW_G), (ak, av, aq, ag)):
+                states[p, 16 * i : 16 * i + 16, :] = pair
+    leaving.append(pltpu.make_async_copy(states, send.at[:, 0:ROW_DOC, :], sems.at[10]))
+    leaving[2].start()
+    for copy in leaving:
         copy.wait()
-        for p in range(GROUP):
-            part = slice(64 * (p % 2), 64 * (p % 2) + 64)
-            send[p, row : row + 64, :] = ref[part, lanes(p // 2)]
-    leaving.wait()
 
 
 def is_late():
@@ -613,11 +619,6 @@
     def _():
         leave(0, prev, prev_send, lambda b: b)
 
-    @pl.when(jnp.logical_not(late))
-    def _():
-        prev[...] = jnp.zeros(prev.shape, BF16)
-        prev_send[...] = jnp.zeros(prev_send.shape, BF16)
-
 
 def body(
     hyena_q, hyena_k, hyena_v, hyena_grad, pole_rate, residue, norm_gain, doc_ids,
@@ -645,9 +646,10 @@
         + [(half_shape, F32), ((POLES, LANES), F32)],
         doc_ids, doc_ids.reshape(1, TOK), pole_rate, residue, hyena_k, hyena_v,
         attn_k, attn_v, attn_q, attn_grad,
-        smem=(0,), specs={i: hbm for i in range(2, 10)}, far=(1,),
+        smem=(0,), specs={i: hbm for i in range(2, 10)}, far=(0, 1),
         scratch=[vmem(params, F32)] + [vmem((POLES, CH), F32)] * 2 + [vmem((TOK, CH), BF16)] * 2
-        + [vmem((TOK, 1024), BF16)] * 4 + [vmem(sweep, F32), pltpu.SemaphoreType.DMA((9,))],
+        + [vmem((TOK, 1024), BF16)] * 4 + [vmem(sweep, F32), vmem((GROUP, HALF_ROWS, LANES), BF16)]
+        + [vmem((GROUP, ROWS_IN - ROW_DOC, LANES), BF16), pltpu.SemaphoreType.DMA((11,))],
         flops=40_000_000, nbytes=6_000_000, vmem=60 << 20,
     )
     got = exchange(send)

time: 118 us -> 118 us (level)
  starting transfers between devices: 21 us -> 24.1 us
  Pallas kernels: 29.4 us -> 26.5 us
    pallas_call x14, Pallas kernels: 29.4 us -> 26.5 us  [call(): pl.pallas_call(kernel, out_shape=shapes, grid=grid, in_specs=ins, out_spe...]
    ppermute x1, starting transfers between devices: 0.46 us -> 1.98 us  [body(): prev_got = lax.ppermute(prev_send, 'ctx', swap_core)]
    ppermute x1, starting transfers between devices: 3.68 us -> 5.2 us  [body(): half_other = lax.ppermute(half_mine, 'ctx', swap_half)]
where the time goes in v6:
time: 118 us; the launch traced here: 117 us
  blocking collectives  57.1 us (48%)
  Pallas kernels  26.5 us (22%)
  starting transfers between devices  24.1 us (20%)
  waiting for transfers between devices  8.7 us (7%)
    all_to_all x3, blocking collectives, exchange(): lax.all_to_all(x, 'ctx', 0, 0, tiled=True, axis_index_groups=[early, late])  57.1 us
    pallas_call x14, Pallas kernels, call(): pl.pallas_call(kernel, out_shape=shapes, grid=grid, in_specs=ins, out_spe...  26.5 us
    ppermute x1, starting transfers between devices, body(): half_other = lax.ppermute(half_mine, 'ctx', swap_half)  5.2 us
    ppermute x3, starting transfers between devices, body(): lax.ppermute(sums, 'chan', [(i, (i + k) % 4) for i in range(4)])  4.53 us
    ppermute x1, starting transfers between devices, body(): kv_half = lax.ppermute(kv_later, 'ctx', up_half)  3.84 us
    ppermute x1, waiting for transfers between devices, body(): other = lax.ppermute(mine, 'ctx', swap_half)  2.47 us
    ppermute x1, waiting for transfers between devices, body(): half_other = lax.ppermute(half_mine, 'ctx', swap_half)  2.4 us
  transfers between devices with their start and end apart: 12, of which 5 were waited for; matrix products, arithmetic and copies ran while one was open for 0% of the time, Pallas kernels for 8%

profile of v6, /device:TPU:1, one launch (start us, length us, event | category | flops | bytes accessed | tf_op | source)
XLA Modules:
  0.0 117.5 jit_solution(12211928304084530978)
XLA Ops:
  0.6 5.6 %shard_map.179 = (bf16[16,400,128]{2,1,0:T(8,128)(2,1)}, f32[2048,128]{1,0:T(8,128)}, f32[256,128]{1,0:T(8,128)}, f32[256,128]{1,0:T(8,128)}, f32[128,128]{1,0:T(8,128)}, /*index=5*/f32[16,128]{1,0:T(8,128)}) custom-call(s32[128]{0:T(128)} %docs.7, s32[1,128]{1,0:T(1,128)} %bitcast.5, f32[16,2048]{1,0:T(8,128)} %rate_hbm.1, f32[16,2048]{1,0:T(8,128)} %res_hbm.1, ...), custom_call_target="tpu_custom_call" | custom-call | flops 40000000 | bytes 6000000 | tf_op jit(solution)/shard_map/pallas_call | solution.py:53
  6.2 29.5 %all_to_all.15.got = bf16[16,400,128]{2,1,0:T(8,128)(2,1)S(1)} all-to-all(bf16[16,400,128]{2,1,0:T(8,128)(2,1)} %get-tuple-element.46), channel_id=1, replica_groups={{0,4,8,12,16,20,24,28,32,36,40,44,48,52,56,60},{96,100,104,108,112,116,..., dimensions={0} | all-to-all | bytes 3276800 | tf_op jit(solution)/shard_map/all_to_all | solution.py:636
  35.7 0.6 shard_map.180
  36.3 0.0 copy-start.5
  36.3 0.0 copy-start.6
  36.3 2.0 %collective-permute-start = (f32[144,128]{1,0:T(8,128)S(1)}, f32[144,128]{1,0:T(8,128)S(1)}, u32[]{:S(2)}, u32[]{:S(2)}) collective-permute-start(f32[144,128]{1,0:T(8,128)S(1)} %get-tuple-element.49.mine.ids_mine.docs_mine), channel_id=1, source_target_pairs={{0,96},{4,100},{8,104},{12,108},{16,112},{20,116},{24,120},{28,124... | collective-permute-start | bytes 221192 | tf_op jit(solution)/shard_map/ppermute | solution.py:662
  38.4 2.5 %collective-permute-done.other.after.ids_other.docs_other = f32[144,128]{1,0:T(8,128)S(1)} collective-permute-done((f32[144,128]{1,0:T(8,128)S(1)}, f32[144,128]{1,0:T(8,128)S(1)}, u32[]{:S(2)}, u32[]{:S(2)}) %collective-permute-start) | collective-permute-done | bytes 73760 | tf_op jit(solution)/shard_map/ppermute | solution.py:662
  40.9 3.8 %collective-permute-start.6 = (bf16[16,128,128]{2,1,0:T(8,128)(2,1)S(1)}, bf16[16,128,128]{2,1,0:T(8,128)(2,1)S(1)}, u32[]{:S(2)}, u32[]{:S(2)}) collective-permute-start(bf16[16,128,128]{2,1,0:T(8,128)(2,1)S(1)} %shard_map.186), channel_id=1, source_target_pairs={{0,96},{4,100},{8,104},{12,108},{16,112},{20,116},{24,120},{28,124... | collective-permute-start | bytes 1572872 | tf_op jit(solution)/shard_map/ppermute | solution.py:669
  44.7 0.2 shard_map.181
  44.9 1.9 %collective-permute-start.1 = (f32[128,128]{1,0:T(8,128)S(1)}, f32[128,128]{1,0:T(8,128)S(1)}, u32[]{:S(2)}, u32[]{:S(2)}) collective-permute-start(f32[128,128]{1,0:T(8,128)S(1)} %get-tuple-element.51), channel_id=1, source_target_pairs={{0,4},{4,0},{8,12},{12,8},{16,20},{20,16},{24,28},{28,24},{32,36},... | collective-permute-start | bytes 196616 | tf_op jit(solution)/shard_map/ppermute | solution.py:682
  46.8 0.9 collective-permute-done.1.got
  47.8 3.3 %shard_map.182 = (f32[2048,128]{1,0:T(8,128)S(1)}, f32[8,128]{1,0:T(8,128)S(1)}) custom-call(s32[128]{0:T(128)S(1)} %copy-done.10, f32[128,128]{1,0:T(8,128)S(1)} %get-tuple-element.50.keep, f32[128,128]{1,0:T(8,128)S(1)} %collective-permute-done.1.got, f32[2048,128]{1,0:T(8,128)S(1)} %copy-done, f32[256,128]{1,0:T(8,128)S(1)} %copy-done.5, ...), custom_call_target="tpu_custom_call" | custom-call | flops 40000000 | bytes 6000000 | tf_op jit(solution)/shard_map/pallas_call | solution.py:53
  51.0 3.8 %collective-permute-start.4 = (f32[8,128]{1,0:T(8,128)S(1)}, f32[8,128]{1,0:T(8,128)S(1)}, u32[]{:S(2)}, u32[]{:S(2)}) collective-permute-start(f32[8,128]{1,0:T(8,128)S(1)} %get-tuple-element.55.s0), channel_id=1, source_target_pairs={{0,3},{1,0},{2,1},{3,2},{4,7},{5,4},{6,5},{7,6},{8,11},{9,8},{10,9... | collective-permute-start | bytes 12296 | tf_op jit(solution)/shard_map/ppermute | solution.py:689
  54.9 0.7 collective-permute-start.2
  55.6 1.2 %collective-permute-start.5 = (bf16[16,128,128]{2,1,0:T(8,128)(2,1)S(1)}, bf16[16,128,128]{2,1,0:T(8,128)(2,1)S(1)}, u32[]{:S(2)}, u32[]{:S(2)}) collective-permute-start(bf16[16,128,128]{2,1,0:T(8,128)(2,1)S(1)} %shard_map.184.kv), channel_id=1, source_target_pairs={{0,4},{4,0},{8,12},{12,8},{16,20},{20,16},{24,28},{28,24},{32,36},... | collective-permute-start | bytes 1572872 | tf_op jit(solution)/shard_map/ppermute | solution.py:665
  56.8 2.1 %collective-permute-done.3.s2 = f32[8,128]{1,0:T(8,128)S(1)} collective-permute-done((f32[8,128]{1,0:T(8,128)S(1)}, f32[8,128]{1,0:T(8,128)S(1)}, u32[]{:S(2)}, u32[]{:S(2)}) %collective-permute-start.3) | collective-permute-done | bytes 4128 | tf_op jit(solution)/shard_map/ppermute | solution.py:689
  58.9 1.9 %collective-permute-start.7 = (bf16[16,128,128]{2,1,0:T(8,128)(2,1)S(1)}, bf16[16,128,128]{2,1,0:T(8,128)(2,1)S(1)}, u32[]{:S(2)}, u32[]{:S(2)}) collective-permute-start(bf16[16,128,128]{2,1,0:T(8,128)(2,1)S(1)} %shard_map.187.kv_half), channel_id=1, source_target_pairs={{0,4},{4,0},{8,12},{12,8},{16,20},{20,16},{24,28},{28,24},{32,36},... | collective-permute-start | bytes 1572872 | tf_op jit(solution)/shard_map/ppermute | solution.py:697
  60.8 0.7 shard_map.185
  61.4 0.9 collective-permute-done.7.kv_half_core
  62.3 5.5 %shard_map.188 = (bf16[16,64,128]{2,1,0:T(8,128)(2,1)S(1)}, bf16[16,128,128]{2,1,0:T(8,128)(2,1)S(1)}, bf16[16,128,128]{2,1,0:T(8,128)(2,1)S(1)}, bf16[16,128,12...) custom-call(bf16[4,256,128]{2,1,0:T(8,128)(2,1)S(1)} %get-tuple-element.56.all_q, ...), custom_call_target="tpu_custom_call" | custom-call | flops 10000000000 | bytes 6000000 | tf_op jit(solution)/shard_map/pallas_call | solution.py:53
  67.8 2.0 %collective-permute-start.8 = (bf16[16,128,128]{2,1,0:T(8,128)(2,1)S(1)}, bf16[16,128,128]{2,1,0:T(8,128)(2,1)S(1)}, u32[]{:S(2)}, u32[]{:S(2)}) collective-permute-start(bf16[16,128,128]{2,1,0:T(8,128)(2,1)S(1)} %get-tuple-element.67), channel_id=1, source_target_pairs={{0,4},{4,0},{8,12},{12,8},{16,20},{20,16},{24,28},{28,24},{32,36},... | collective-permute-start | bytes 1572872 | tf_op jit(solution)/shard_map/ppermute | solution.py:721
  69.8 0.3 collective-permute-start.10
  70.0 5.2 %shard_map.189 = (bf16[128,2048]{1,0:T(8,128)(2,1)}, f32[2048,128]{1,0:T(8,128)S(1)}, bf16[16,48,128]{2,1,0:T(8,128)(2,1)S(1)}) custom-call(s32[128]{0:T(128)S(1)} %copy-done.10, f32[8,128]{1,0:T(8,128)S(1)} %shard_map.183.after.sums, f32[8,128]{1,0:T(8,128)S(1)} %get-tuple-element.63.after, f32[2048,128]{1,0:T(8,128)S(1)} %get-tuple-element.64.f, ...), custom_call_target="tpu_custom_call" | custom-call | flops 40000000 | bytes 6000000 | tf_op jit(solution)/shard_map/pallas_call | solution.py:53
  75.3 0.1 add_convert_fusion
  75.4 1.3 %collective-permute-start.11 = (bf16[16,128,128]{2,1,0:T(8,128)(2,1)S(1)}, bf16[16,128,128]{2,1,0:T(8,128)(2,1)S(1)}, u32[]{:S(2)}, u32[]{:S(2)}) collective-permute-start(bf16[16,128,128]{2,1,0:T(8,128)(2,1)S(1)} %add_convert_fusion), channel_id=1, source_target_pairs={{96,0},{100,4},{104,8},{108,12},{112,16},{116,20},{120,24},{124,28... | collective-permute-start | bytes 1572872 | tf_op jit(solution)/shard_map/ppermute | solution.py:725
  76.7 9.4 %all_to_all.16.back = bf16[16,48,128]{2,1,0:T(8,128)(2,1)S(1)} all-to-all(bf16[16,48,128]{2,1,0:T(8,128)(2,1)S(1)} %get-tuple-element.68), channel_id=1, replica_groups={{0,4,8,12,16,20,24,28,32,36,40,44,48,52,56,60},{96,100,104,108,112,116,..., dimensions={0} | all-to-all | bytes 393216 | tf_op jit(solution)/shard_map/all_to_all | solution.py:636
  86.1 0.2 shard_map.190.mine
  86.3 5.2 %collective-permute-start.9 = (f32[56,128]{1,0:T(8,128)S(1)}, f32[56,128]{1,0:T(8,128)S(1)}, u32[]{:S(2)}, u32[]{:S(2)}) collective-permute-start(f32[56,128]{1,0:T(8,128)S(1)} %shard_map.190.mine), channel_id=1, source_target_pairs={{0,96},{4,100},{8,104},{12,108},{16,112},{20,116},{24,120},{28,124... | collective-permute-start | bytes 86024 | tf_op jit(solution)/shard_map/ppermute | solution.py:731
  91.5 2.4 %collective-permute-done.9.theirs = f32[56,128]{1,0:T(8,128)S(1)} collective-permute-done((f32[56,128]{1,0:T(8,128)S(1)}, f32[56,128]{1,0:T(8,128)S(1)}, u32[]{:S(2)}, u32[]{:S(2)}) %collective-permute-start.9) | collective-permute-done | bytes 28704 | tf_op jit(solution)/shard_map/ppermute | solution.py:731
  93.9 0.4 shard_map.191
  94.3 18.3 %all_to_all.17.got = bf16[16,240,128]{2,1,0:T(8,128)(2,1)S(1)} all-to-all(bf16[16,240,128]{2,1,0:T(8,128)(2,1)S(1)} %shard_map.191), channel_id=1, replica_groups={{0,4,8,12,16,20,24,28,32,36,40,44,48,52,56,60},{96,100,104,108,112,116,..., dimensions={0} | all-to-all | bytes 1966080 | tf_op jit(solution)/shard_map/all_to_all | solution.py:636
  112.6 4.8 %shard_map.192 = (bf16[128,2048]{1,0:T(8,128)(2,1)}, bf16[128,2048]{1,0:T(8,128)(2,1)}, f32[16,2048]{1,0:T(8,128)}, f32[1,2048]{1,0:T(1,128)}, bf16[128,1024]{1,...) custom-call(s32[128]{0:T(128)S(1)} %copy-done.10, bf16[16,240,128]{2,1,0:T(8,128)(2,1)S(1)} %all_to_all.17.got, ...), custom_call_target="tpu_custom_call" | custom-call | flops 40000000 | bytes 6000000 | tf_op jit(solution)/shard_map/pallas_call | solution.py:53
  (32 shorter events, 0.2 us)
Async XLA Ops:
  6.2 29.5 %copy-start.7 = (f32[128,128]{1,0:T(8,128)S(1)}, f32[128,128]{1,0:T(8,128)}, u32[]{:S(2)}) copy-start(f32[128,128]{1,0:T(8,128)} %get-tuple-element.47.through) | copy-start | bytes 196612
  36.3 11.5 %copy-start = (f32[2048,128]{1,0:T(8,128)S(1)}, f32[2048,128]{1,0:T(8,128)}, u32[]{:S(2)}) copy-start(f32[2048,128]{1,0:T(8,128)} %get-tuple-element.52.m) | copy-start | bytes 3145732
  36.3 11.5 %copy-start.1 = (bf16[128,2048]{1,0:T(8,128)(2,1)S(1)}, bf16[128,2048]{1,0:T(8,128)(2,1)}, u32[]{:S(2)}) copy-start(bf16[128,2048]{1,0:T(8,128)(2,1)} %hq.3) | copy-start | bytes 1572868
  36.3 11.5 %copy-start.2 = (bf16[128,2048]{1,0:T(8,128)(2,1)S(1)}, bf16[128,2048]{1,0:T(8,128)(2,1)}, u32[]{:S(2)}) copy-start(bf16[128,2048]{1,0:T(8,128)(2,1)} %hg.3) | copy-start | bytes 1572868
  36.3 11.4 %copy-start.5 = (f32[256,128]{1,0:T(8,128)S(1)}, f32[256,128]{1,0:T(8,128)}, u32[]{:S(2)}) copy-start(f32[256,128]{1,0:T(8,128)} %get-tuple-element.53.dec) | copy-start | bytes 393220
  36.3 11.4 %copy-start.6 = (f32[256,128]{1,0:T(8,128)S(1)}, f32[256,128]{1,0:T(8,128)}, u32[]{:S(2)}) copy-start(f32[256,128]{1,0:T(8,128)} %get-tuple-element.54.wgt) | copy-start | bytes 393220
  36.3 11.4 %copy-start.8 = (f32[2048]{0:T(1024)S(1)}, f32[2048]{0:T(1024)}, u32[]{:S(2)}) copy-start(f32[2048]{0:T(1024)} %param.18) | copy-start | bytes 24580
  36.3 11.4 %copy-start.10 = (s32[128]{0:T(128)S(1)}, s32[128]{0:T(128)}, u32[]{:S(2)}) copy-start(s32[128]{0:T(128)} %docs.7) | copy-start | bytes 1540
  36.3 4.5 %collective-permute-start = (f32[144,128]{1,0:T(8,128)S(1)}, f32[144,128]{1,0:T(8,128)S(1)}, u32[]{:S(2)}, u32[]{:S(2)}) collective-permute-start(f32[144,128]{1,0:T(8,128)S(1)} %get-tuple-element.49.mine.ids_mine.docs_mine), channel_id=1, source_target_pairs={{0,96},{4,100},{8,104},{12,108},{16,112},{20,116},{24,120},{28,124... | collective-permute-start | bytes 221192 | tf_op jit(solution)/shard_map/ppermute | solution.py:662
  40.9 18.0 %collective-permute-start.6 = (bf16[16,128,128]{2,1,0:T(8,128)(2,1)S(1)}, bf16[16,128,128]{2,1,0:T(8,128)(2,1)S(1)}, u32[]{:S(2)}, u32[]{:S(2)}) collective-permute-start(bf16[16,128,128]{2,1,0:T(8,128)(2,1)S(1)} %shard_map.186), channel_id=1, source_target_pairs={{0,96},{4,100},{8,104},{12,108},{16,112},{20,116},{24,120},{28,124... | collective-permute-start | bytes 1572872 | tf_op jit(solution)/shard_map/ppermute | solution.py:669
  44.9 2.8 %collective-permute-start.1 = (f32[128,128]{1,0:T(8,128)S(1)}, f32[128,128]{1,0:T(8,128)S(1)}, u32[]{:S(2)}, u32[]{:S(2)}) collective-permute-start(f32[128,128]{1,0:T(8,128)S(1)} %get-tuple-element.51), channel_id=1, source_target_pairs={{0,4},{4,0},{8,12},{12,8},{16,20},{20,16},{24,28},{28,24},{32,36},... | collective-permute-start | bytes 196616 | tf_op jit(solution)/shard_map/ppermute | solution.py:682
  51.0 5.7 %collective-permute-start.4 = (f32[8,128]{1,0:T(8,128)S(1)}, f32[8,128]{1,0:T(8,128)S(1)}, u32[]{:S(2)}, u32[]{:S(2)}) collective-permute-start(f32[8,128]{1,0:T(8,128)S(1)} %get-tuple-element.55.s0), channel_id=1, source_target_pairs={{0,3},{1,0},{2,1},{3,2},{4,7},{5,4},{6,5},{7,6},{8,11},{9,8},{10,9... | collective-permute-start | bytes 12296 | tf_op jit(solution)/shard_map/ppermute | solution.py:689
  54.9 4.0 %collective-permute-start.3 = (f32[8,128]{1,0:T(8,128)S(1)}, f32[8,128]{1,0:T(8,128)S(1)}, u32[]{:S(2)}, u32[]{:S(2)}) collective-permute-start(f32[8,128]{1,0:T(8,128)S(1)} %get-tuple-element.55.s0), channel_id=1, source_target_pairs={{0,2},{1,3},{2,0},{3,1},{4,6},{5,7},{6,4},{7,5},{8,10},{9,11},{10,... | collective-permute-start | bytes 12296 | tf_op jit(solution)/shard_map/ppermute | solution.py:689
  54.9 4.0 %collective-permute-start.2 = (f32[8,128]{1,0:T(8,128)S(1)}, f32[8,128]{1,0:T(8,128)S(1)}, u32[]{:S(2)}, u32[]{:S(2)}) collective-permute-start(f32[8,128]{1,0:T(8,128)S(1)} %get-tuple-element.55.s0), channel_id=1, source_target_pairs={{0,1},{1,2},{2,3},{3,0},{4,5},{5,6},{6,7},{7,4},{8,9},{9,10},{10,1... | collective-permute-start | bytes 12296 | tf_op jit(solution)/shard_map/ppermute | solution.py:689
  55.6 5.2 %collective-permute-start.5 = (bf16[16,128,128]{2,1,0:T(8,128)(2,1)S(1)}, bf16[16,128,128]{2,1,0:T(8,128)(2,1)S(1)}, u32[]{:S(2)}, u32[]{:S(2)}) collective-permute-start(bf16[16,128,128]{2,1,0:T(8,128)(2,1)S(1)} %shard_map.184.kv), channel_id=1, source_target_pairs={{0,4},{4,0},{8,12},{12,8},{16,20},{20,16},{24,28},{28,24},{32,36},... | collective-permute-start | bytes 1572872 | tf_op jit(solution)/shard_map/ppermute | solution.py:665
  58.9 3.4 %collective-permute-start.7 = (bf16[16,128,128]{2,1,0:T(8,128)(2,1)S(1)}, bf16[16,128,128]{2,1,0:T(8,128)(2,1)S(1)}, u32[]{:S(2)}, u32[]{:S(2)}) collective-permute-start(bf16[16,128,128]{2,1,0:T(8,128)(2,1)S(1)} %shard_map.187.kv_half), channel_id=1, source_target_pairs={{0,4},{4,0},{8,12},{12,8},{16,20},{20,16},{24,28},{28,24},{32,36},... | collective-permute-start | bytes 1572872 | tf_op jit(solution)/shard_map/ppermute | solution.py:697
  67.8 7.5 %collective-permute-start.8 = (bf16[16,128,128]{2,1,0:T(8,128)(2,1)S(1)}, bf16[16,128,128]{2,1,0:T(8,128)(2,1)S(1)}, u32[]{:S(2)}, u32[]{:S(2)}) collective-permute-start(bf16[16,128,128]{2,1,0:T(8,128)(2,1)S(1)} %get-tuple-element.67), channel_id=1, source_target_pairs={{0,4},{4,0},{8,12},{12,8},{16,20},{20,16},{24,28},{28,24},{32,36},... | collective-permute-start | bytes 1572872 | tf_op jit(solution)/shard_map/ppermute | solution.py:721
  69.8 21.8 %collective-permute-start.10 = (bf16[16,128,128]{2,1,0:T(8,128)(2,1)S(1)}, bf16[16,128,128]{2,1,0:T(8,128)(2,1)S(1)}, u32[]{:S(2)}, u32[]{:S(2)}) collective-permute-start(bf16[16,128,128]{2,1,0:T(8,128)(2,1)S(1)} %get-tuple-element.73), channel_id=1, source_target_pairs={{0,4},{4,0},{8,12},{12,8},{16,20},{20,16},{24,28},{28,24},{32,36},... | collective-permute-start | bytes 1572872 | tf_op jit(solution)/shard_map/ppermute | solution.py:722
  75.3 10.8 %copy-start.9 = (f32[16,128]{1,0:T(8,128)S(1)}, f32[16,128]{1,0:T(8,128)}, u32[]{:S(2)}) copy-start(f32[16,128]{1,0:T(8,128)} %get-tuple-element.69.rate) | copy-start | bytes 24580
  75.4 18.5 %collective-permute-start.11 = (bf16[16,128,128]{2,1,0:T(8,128)(2,1)S(1)}, bf16[16,128,128]{2,1,0:T(8,128)(2,1)S(1)}, u32[]{:S(2)}, u32[]{:S(2)}) collective-permute-start(bf16[16,128,128]{2,1,0:T(8,128)(2,1)S(1)} %add_convert_fusion), channel_id=1, source_target_pairs={{96,0},{100,4},{104,8},{108,12},{112,16},{116,20},{120,24},{124,28... | collective-permute-start | bytes 1572872 | tf_op jit(solution)/shard_map/ppermute | solution.py:725
  86.3 7.6 %collective-permute-start.9 = (f32[56,128]{1,0:T(8,128)S(1)}, f32[56,128]{1,0:T(8,128)S(1)}, u32[]{:S(2)}, u32[]{:S(2)}) collective-permute-start(f32[56,128]{1,0:T(8,128)S(1)} %shard_map.190.mine), channel_id=1, source_target_pairs={{0,96},{4,100},{8,104},{12,108},{16,112},{20,116},{24,120},{28,124... | collective-permute-start | bytes 86024 | tf_op jit(solution)/shard_map/ppermute | solution.py:731
  94.3 18.3 %copy-start.3 = (bf16[128,2048]{1,0:T(8,128)(2,1)S(1)}, bf16[128,2048]{1,0:T(8,128)(2,1)}, u32[]{:S(2)}) copy-start(bf16[128,2048]{1,0:T(8,128)(2,1)} %hk.1) | copy-start | bytes 1572868
  94.3 18.3 %copy-start.4 = (bf16[128,2048]{1,0:T(8,128)(2,1)S(1)}, bf16[128,2048]{1,0:T(8,128)(2,1)}, u32[]{:S(2)}) copy-start(bf16[128,2048]{1,0:T(8,128)(2,1)} %hv.1) | copy-start | bytes 1572868
